TPU v7x, 128 devices: a whole 4x4x4 slice. The times are simulated.
128 devices in a mesh: ctx: 8 (over z_lo, x), exp: 16 (over z_hi, y, core).
Axes of the slice: x: 4, y: 4, z: 4 (z_hi: 2, z_lo: 2; z = z_hi * 2 + z_lo), core: 2. Of those that a mesh axis runs over, the one named last changes fastest.
Arguments:
- tokens: bfloat16 [16, 1024, 1024], P('exp', 'ctx'), may hold values from -6 to 6
- cotangent: bfloat16 [16, 1024, 1024], P('exp', 'ctx'), may hold values from -6 to 6
- span_order: int32 [16], replicated, may hold values from 0 to 15, each once
- expert_choice: int32 [16, 1024, 8], P('exp', 'ctx'), may hold values from 0 to 31, all different within a row; in each aligned block of 128 rows (0 to 127, 128 to 255, ..., all dimensions but the last counted through in order) at most 48 rows name the same one
- norm_attn: bfloat16 [1024], P('exp'), may hold values from 0.5 to 1.5
- w_query: bfloat16 [1024, 1024], P('exp'), may hold values from -0.1875 to 0.1875
- key_matrix: bfloat16 [1024, 512], P('exp'), may hold values from -0.1875 to 0.1875
- value_matrix: bfloat16 [1024, 512], P('exp'), may hold values from -0.1875 to 0.1875
- w_out: bfloat16 [1024, 1024], P('exp'), may hold values from -1.5 to 1.5
- norm_moe: bfloat16 [1024], P('exp'), may hold values from 0.5 to 1.5
- w_router: bfloat16 [1024, 32], P('exp'), may hold values from -0.09375 to 0.09375
- w_gate: bfloat16 [32, 1024, 512], P('exp', 'ctx'), may hold values from -0.1875 to 0.1875
- w_up: bfloat16 [32, 1024, 512], P('exp', 'ctx'), may hold values from -0.1875 to 0.1875
- w_down: bfloat16 [32, 512, 1024], P('exp', 'ctx'), may hold values from -1 to 1
Outputs:
- out: bfloat16 [16, 1024, 1024], P('exp', 'ctx')
- grad_tokens: float32 [16, 1024, 1024], P('exp', 'ctx')
- grad_norm_attn: float32 [1024], P('exp')
- grad_w_query: float32 [1024, 1024], P('exp')
- grad_w_key: float32 [1024, 512], P('exp')
- grad_w_value: float32 [1024, 512], P('exp')
- grad_w_out: float32 [1024, 1024], P('exp')
- grad_norm_moe: float32 [1024], P('exp')
- grad_w_router: float32 [1024, 32], P('exp')
- grad_w_gate: float32 [32, 1024, 512], P('exp', 'ctx')
- grad_w_up: float32 [32, 1024, 512], P('exp', 'ctx')
- grad_w_down: float32 [32, 512, 1024], P('exp', 'ctx')
Inputs may be any that keep to these rules, and one draw needn't show every extreme that they name: Index i of ctx holds spans span_order[2 i] and span_order[2 i + 1] of each sequence, in this order; each span number appears once. `expert_choice`: A token's 8 experts differ. Among the choices of the 128 tokens of one device no expert appears more than 48 times, and in every draw some expert appears exactly 48 times among the tokens of some device.
All inputs are finite; a program needn't handle non-finite values.
Results may differ from a plain program's by a relative error of at most 0.025.
Values may be sent and summed in bfloat16 or wider, within the bound.
A program may use at most 128 MiB of HBM per device.

v0:
```python
import jax
import jax.numpy as jnp
from jax import lax
from jax.sharding import PartitionSpec as P

QUERY_HEADS = 16
KEY_VALUE_HEADS = 8
HEAD_SIZE = 64
TOP = 8


eps_norm = 1e-06
rope_base = 10000.0
neg_big = -1e30


def normalize(values, gain):
    factor = lax.rsqrt(jnp.mean(values * values, axis=-1, keepdims=True) + eps_norm)
    return (values * factor * gain, factor)


def normalize_back(values, factor, gain, upstream):
    scaled = upstream * gain
    gain_grad = jnp.sum(upstream * values * factor, axis=0)
    inner = jnp.mean(scaled * values, axis=-1, keepdims=True)
    return (factor * scaled - values * factor * factor * factor * inner, gain_grad)


def softmax_rows(values):
    largest = jnp.max(values, axis=-1, keepdims=True)
    shifted = jnp.exp(values - largest)
    totals = jnp.sum(shifted, axis=-1, keepdims=True)
    return (shifted / totals, largest + jnp.log(totals))


def apply_rotary(values, cosine_table, sine_table, heads, direction):
    count_of_rows = values.shape[0]
    by_head = values.reshape(count_of_rows, heads, HEAD_SIZE)
    leading = by_head[:, :, : HEAD_SIZE // 2]
    trailing = by_head[:, :, HEAD_SIZE // 2 :]
    turned = jnp.concatenate(
        [
            leading * cosine_table - direction * trailing * sine_table,
            trailing * cosine_table + direction * leading * sine_table,
        ],
        axis=2,
    )
    return turned.reshape(count_of_rows, heads * HEAD_SIZE)


def score_block(rotated_queries, every_key, query_places, key_places):
    query_rows = rotated_queries.reshape(
        rotated_queries.shape[0], KEY_VALUE_HEADS, QUERY_HEADS // KEY_VALUE_HEADS, HEAD_SIZE
    )
    heads_of_keys = every_key.reshape(every_key.shape[0], KEY_VALUE_HEADS, HEAD_SIZE)
    raw_scores = jnp.einsum(
        "bkgh,jkh->kgbj", query_rows, heads_of_keys, preferred_element_type=jnp.float32
    )
    visible = key_places[None, :] <= query_places[:, None]
    return jnp.where(visible, raw_scores * HEAD_SIZE ** (-0.5), neg_big)


def body(
    tokens,
    cotangent,
    span_order,
    expert_choice,
    norm_attn,
    w_query,
    key_matrix,
    value_matrix,
    w_out,
    norm_moe,
    w_router,
    w_gate,
    w_up,
    w_down,
):
    inputs = tokens[0].astype(jnp.float32)
    upstream = cotangent[0].astype(jnp.float32)
    choice_rows = expert_choice[0]
    count_of_rows = inputs.shape[0]
    cycle_size = lax.axis_size("ctx")
    cycle_place = lax.axis_index("ctx")
    groups = lax.axis_size("exp")
    wq, wk, wv, wo, wr, gain_attn, gain_moe = (
        lax.all_gather(w_query, "exp", axis=0, tiled=True),
        lax.all_gather(key_matrix, "exp", axis=0, tiled=True),
        lax.all_gather(value_matrix, "exp", axis=0, tiled=True),
        lax.all_gather(w_out, "exp", axis=0, tiled=True),
        lax.all_gather(w_router, "exp", axis=0, tiled=True),
        lax.all_gather(norm_attn, "exp", axis=0, tiled=True),
        lax.all_gather(norm_moe, "exp", axis=0, tiled=True),
    )
    wg, wu, wd = (
        lax.all_gather(w_gate, "ctx", axis=1, tiled=True),
        lax.all_gather(w_up, "ctx", axis=1, tiled=True),
        lax.all_gather(w_down, "ctx", axis=1, tiled=True),
    )
    gain_a = gain_attn.astype(jnp.float32)
    gain_m = gain_moe.astype(jnp.float32)
    span_len = count_of_rows // 2
    local_ids = jnp.arange(count_of_rows, dtype=jnp.int32)
    own_spans = lax.dynamic_slice_in_dim(span_order, cycle_place * 2, 2)
    query_places = (
        jnp.where(local_ids < span_len, own_spans[0], own_spans[1]) * span_len
        + local_ids % span_len
    )
    every_id = jnp.arange(count_of_rows * cycle_size, dtype=jnp.int32)
    table = every_id[:, None] // span_len == jnp.arange(2 * cycle_size, dtype=jnp.int32)[None, :]
    key_places = (
        jnp.sum(jnp.where(table, span_order[None, :], 0), axis=1) * span_len + every_id % span_len
    )
    freqs = rope_base ** (-(jnp.arange(HEAD_SIZE // 2, dtype=jnp.float32) * 2.0 / HEAD_SIZE))
    turned = query_places.astype(jnp.float32)[:, None] * freqs[None, :]
    cosine_table = jnp.cos(turned)[:, None, :]
    sine_table = jnp.sin(turned)[:, None, :]
    h_one, factor_one = normalize(inputs, gain_a)
    act_low = h_one.astype(jnp.bfloat16)
    query = jnp.dot(act_low, wq, preferred_element_type=jnp.float32)
    key_unrotated = jnp.dot(act_low, wk, preferred_element_type=jnp.float32)
    value_pre = jnp.dot(act_low, wv, preferred_element_type=jnp.float32)
    rotated_queries = apply_rotary(query, cosine_table, sine_table, QUERY_HEADS, 1.0).astype(
        jnp.bfloat16
    )
    rotated_keys = apply_rotary(
        key_unrotated, cosine_table, sine_table, KEY_VALUE_HEADS, 1.0
    ).astype(jnp.bfloat16)
    value_reduced = value_pre.astype(jnp.bfloat16)
    every_key, every_value = (
        lax.all_gather(rotated_keys, "ctx", axis=0, tiled=True),
        lax.all_gather(value_reduced, "ctx", axis=0, tiled=True),
    )
    probs, log_totals = softmax_rows(
        score_block(rotated_queries, every_key, query_places, key_places)
    )
    probs_low = probs.astype(jnp.bfloat16)
    heads_of_values = every_value.reshape(every_value.shape[0], KEY_VALUE_HEADS, HEAD_SIZE)
    mixed = jnp.einsum(
        "kgbj,jkh->bkgh", probs_low, heads_of_values, preferred_element_type=jnp.float32
    )
    attn_low = mixed.reshape(count_of_rows, QUERY_HEADS * HEAD_SIZE).astype(jnp.bfloat16)
    x_mid = inputs + jnp.dot(attn_low, wo, preferred_element_type=jnp.float32)
    h_two, factor_two = normalize(x_mid, gain_m)
    routed_in = h_two.astype(jnp.bfloat16)
    logits = jnp.dot(routed_in, wr, preferred_element_type=jnp.float32)
    experts_total = wr.shape[1]
    expert_ids = jnp.arange(experts_total, dtype=jnp.int32)
    onehot = (choice_rows[:, :, None] == expert_ids[None, None, :]).astype(jnp.float32)
    chosen = jnp.sum(onehot * logits[:, None, :], axis=-1)
    gates, unused_lse = softmax_rows(chosen)
    capacity = 3 * count_of_rows * TOP // (2 * experts_total)
    flat_choice = choice_rows.reshape(-1)
    onehot_int = (flat_choice[:, None] == expert_ids[None, :]).astype(jnp.int32)
    earlier = jnp.cumsum(onehot_int, axis=0) - onehot_int
    slot_ids = jnp.sum(earlier * onehot_int, axis=1)
    targets = flat_choice * capacity + slot_ids
    source_token = jnp.arange(count_of_rows * TOP, dtype=jnp.int32) // TOP
    source_rows = jnp.zeros((experts_total * capacity,), jnp.int32).at[targets].set(source_token)
    filled = jnp.zeros((experts_total * capacity,), jnp.int32).at[targets].set(1)
    outgoing = jnp.where(filled[:, None] > 0, routed_in[source_rows], jnp.zeros((), jnp.bfloat16))
    local_experts = experts_total // groups
    outgoing = outgoing.reshape(groups, local_experts, capacity, routed_in.shape[1])
    received = lax.all_to_all(outgoing, "exp", split_axis=0, concat_axis=0, tiled=True)
    gate_h = jnp.einsum("sxcd,xdf->sxcf", received, wg, preferred_element_type=jnp.float32)
    up_h = jnp.einsum("sxcd,xdf->sxcf", received, wu, preferred_element_type=jnp.float32)
    sigmoid_g = jax.nn.sigmoid(gate_h)
    silu_g = gate_h * sigmoid_g
    hidden = (silu_g * up_h).astype(jnp.bfloat16)
    expert_out = jnp.einsum(
        "sxcf,xfd->sxcd", hidden, wd, preferred_element_type=jnp.float32
    ).astype(jnp.bfloat16)
    returned = lax.all_to_all(expert_out, "exp", split_axis=0, concat_axis=0, tiled=True).reshape(
        experts_total * capacity, -1
    )
    gathered_out = returned[targets].reshape(count_of_rows, TOP, -1).astype(jnp.float32)
    x_out = x_mid + jnp.sum(gates[:, :, None] * gathered_out, axis=1)
    result = x_out.astype(jnp.bfloat16)
    grad_rows = (
        (gates[:, :, None] * upstream[:, None, :])
        .astype(jnp.bfloat16)
        .reshape(count_of_rows * TOP, -1)
    )
    grad_gates = jnp.sum(gathered_out * upstream[:, None, :], axis=-1)
    slot_grads = (
        jnp.zeros((experts_total * capacity, grad_rows.shape[1]), jnp.bfloat16)
        .at[targets]
        .set(grad_rows)
    )
    grad_exp = lax.all_to_all(
        slot_grads.reshape(groups, local_experts, capacity, -1),
        "exp",
        split_axis=0,
        concat_axis=0,
        tiled=True,
    )
    grad_wd = jnp.einsum("sxcf,sxcd->xfd", hidden, grad_exp, preferred_element_type=jnp.float32)
    grad_hidden = jnp.einsum("sxcd,xfd->sxcf", grad_exp, wd, preferred_element_type=jnp.float32)
    grad_gate = (grad_hidden * up_h * (sigmoid_g * (1.0 + gate_h * (1.0 - sigmoid_g)))).astype(
        jnp.bfloat16
    )
    grad_up = (grad_hidden * silu_g).astype(jnp.bfloat16)
    grad_wg = jnp.einsum("sxcd,sxcf->xdf", received, grad_gate, preferred_element_type=jnp.float32)
    grad_wu = jnp.einsum("sxcd,sxcf->xdf", received, grad_up, preferred_element_type=jnp.float32)
    grad_in = jnp.einsum("sxcf,xdf->sxcd", grad_gate, wg, preferred_element_type=jnp.float32)
    grad_in = (
        grad_in + jnp.einsum("sxcf,xdf->sxcd", grad_up, wu, preferred_element_type=jnp.float32)
    ).astype(jnp.bfloat16)
    grad_back = lax.all_to_all(grad_in, "exp", split_axis=0, concat_axis=0, tiled=True).reshape(
        experts_total * capacity, -1
    )
    grad_routed = jnp.sum(
        grad_back[targets].reshape(count_of_rows, TOP, -1).astype(jnp.float32), axis=1
    )
    centered = grad_gates - jnp.sum(gates * grad_gates, axis=-1, keepdims=True)
    grad_logits = jnp.sum(onehot * (gates * centered)[:, :, None], axis=1).astype(jnp.bfloat16)
    grad_wr = jnp.einsum("td,te->de", routed_in, grad_logits, preferred_element_type=jnp.float32)
    grad_routed = grad_routed + jnp.einsum(
        "te,de->td", grad_logits, wr, preferred_element_type=jnp.float32
    )
    grad_mid_norm, grad_gain_moe = normalize_back(x_mid, factor_two, gain_m, grad_routed)
    grad_mid = upstream + grad_mid_norm
    grad_branch = grad_mid.astype(jnp.bfloat16)
    grad_wo = jnp.einsum("ti,td->id", attn_low, grad_branch, preferred_element_type=jnp.float32)
    attention_gradient = jnp.einsum(
        "td,id->ti", grad_branch, wo, preferred_element_type=jnp.float32
    ).astype(jnp.bfloat16)
    keys_for_backward, values_for_backward = (every_key, every_value)
    probs_back = jnp.exp(
        score_block(rotated_queries, keys_for_backward, query_places, key_places) - log_totals
    )
    probs_back_low = probs_back.astype(jnp.bfloat16)
    heads_of_keys = keys_for_backward.reshape(
        keys_for_backward.shape[0], KEY_VALUE_HEADS, HEAD_SIZE
    )
    value_for_backward = values_for_backward.reshape(
        values_for_backward.shape[0], KEY_VALUE_HEADS, HEAD_SIZE
    )
    head_gradient = attention_gradient.reshape(
        count_of_rows, KEY_VALUE_HEADS, QUERY_HEADS // KEY_VALUE_HEADS, HEAD_SIZE
    )
    heads_of_queries = rotated_queries.reshape(
        count_of_rows, KEY_VALUE_HEADS, QUERY_HEADS // KEY_VALUE_HEADS, HEAD_SIZE
    )
    grad_probs = jnp.einsum(
        "bkgh,jkh->kgbj", head_gradient, value_for_backward, preferred_element_type=jnp.float32
    )
    weighted = jnp.sum(probs_back * grad_probs, axis=-1, keepdims=True)
    grad_scores = (probs_back * (grad_probs - weighted)).astype(jnp.bfloat16)
    score_scale = HEAD_SIZE ** (-0.5)
    grad_qrot = (
        jnp.einsum(
            "kgbj,jkh->bkgh", grad_scores, heads_of_keys, preferred_element_type=jnp.float32
        ).reshape(count_of_rows, QUERY_HEADS * HEAD_SIZE)
        * score_scale
    )
    grad_kall = (
        jnp.einsum(
            "kgbj,bkgh->jkh", grad_scores, heads_of_queries, preferred_element_type=jnp.float32
        ).reshape(-1, KEY_VALUE_HEADS * HEAD_SIZE)
        * score_scale
    )
    grad_vall = jnp.einsum(
        "kgbj,bkgh->jkh", probs_back_low, head_gradient, preferred_element_type=jnp.float32
    ).reshape(-1, KEY_VALUE_HEADS * HEAD_SIZE)
    rotated_key_gradient, grad_vlow = (
        lax.psum_scatter(
            grad_kall.astype(jnp.bfloat16), "ctx", scatter_dimension=0, tiled=True
        ).astype(jnp.float32),
        lax.psum_scatter(
            grad_vall.astype(jnp.bfloat16), "ctx", scatter_dimension=0, tiled=True
        ).astype(jnp.float32),
    )
    grad_query = apply_rotary(grad_qrot, cosine_table, sine_table, QUERY_HEADS, -1.0).astype(
        jnp.bfloat16
    )
    key_gradient = apply_rotary(
        rotated_key_gradient, cosine_table, sine_table, KEY_VALUE_HEADS, -1.0
    ).astype(jnp.bfloat16)
    grad_value = grad_vlow.astype(jnp.bfloat16)
    grad_wq = jnp.einsum("td,ti->di", act_low, grad_query, preferred_element_type=jnp.float32)
    grad_wk = jnp.einsum("td,ti->di", act_low, key_gradient, preferred_element_type=jnp.float32)
    grad_wv = jnp.einsum("td,ti->di", act_low, grad_value, preferred_element_type=jnp.float32)
    grad_h_one = jnp.einsum("ti,di->td", grad_query, wq, preferred_element_type=jnp.float32)
    grad_h_one = grad_h_one + jnp.einsum(
        "ti,di->td", key_gradient, wk, preferred_element_type=jnp.float32
    )
    grad_h_one = grad_h_one + jnp.einsum(
        "ti,di->td", grad_value, wv, preferred_element_type=jnp.float32
    )
    grad_in_norm, grad_gain_attn = normalize_back(inputs, factor_one, gain_a, grad_h_one)
    grad_tokens = grad_mid + grad_in_norm
    shares = (
        lax.psum_scatter(
            grad_wq.astype(jnp.bfloat16), "exp", scatter_dimension=0, tiled=True
        ).astype(jnp.float32),
        lax.psum_scatter(
            grad_wk.astype(jnp.bfloat16), "exp", scatter_dimension=0, tiled=True
        ).astype(jnp.float32),
        lax.psum_scatter(
            grad_wv.astype(jnp.bfloat16), "exp", scatter_dimension=0, tiled=True
        ).astype(jnp.float32),
        lax.psum_scatter(
            grad_wo.astype(jnp.bfloat16), "exp", scatter_dimension=0, tiled=True
        ).astype(jnp.float32),
        lax.psum_scatter(
            grad_wr.astype(jnp.bfloat16), "exp", scatter_dimension=0, tiled=True
        ).astype(jnp.float32),
        lax.psum_scatter(
            grad_gain_attn.astype(jnp.bfloat16), "exp", scatter_dimension=0, tiled=True
        ).astype(jnp.float32),
        lax.psum_scatter(
            grad_gain_moe.astype(jnp.bfloat16), "exp", scatter_dimension=0, tiled=True
        ).astype(jnp.float32),
    )
    owned = (
        lax.psum(shares[0].astype(jnp.bfloat16), "ctx").astype(jnp.float32),
        lax.psum(shares[1].astype(jnp.bfloat16), "ctx").astype(jnp.float32),
        lax.psum(shares[2].astype(jnp.bfloat16), "ctx").astype(jnp.float32),
        lax.psum(shares[3].astype(jnp.bfloat16), "ctx").astype(jnp.float32),
        lax.psum(shares[4].astype(jnp.bfloat16), "ctx").astype(jnp.float32),
        lax.psum(shares[5].astype(jnp.bfloat16), "ctx").astype(jnp.float32),
        lax.psum(shares[6].astype(jnp.bfloat16), "ctx").astype(jnp.float32),
    )
    expert_owned = (
        lax.psum_scatter(
            grad_wg.astype(jnp.bfloat16), "ctx", scatter_dimension=1, tiled=True
        ).astype(jnp.float32),
        lax.psum_scatter(
            grad_wu.astype(jnp.bfloat16), "ctx", scatter_dimension=1, tiled=True
        ).astype(jnp.float32),
        lax.psum_scatter(
            grad_wd.astype(jnp.bfloat16), "ctx", scatter_dimension=1, tiled=True
        ).astype(jnp.float32),
    )
    return (
        result[None],
        grad_tokens[None],
        owned[5],
        owned[0],
        owned[1],
        owned[2],
        owned[3],
        owned[6],
        owned[4],
        expert_owned[0],
        expert_owned[1],
        expert_owned[2],
    )


def solution(mesh):
    return jax.shard_map(
        body,
        mesh=mesh,
        in_specs=(
            P("exp", "ctx", None),
            P("exp", "ctx", None),
            P(),
            P("exp", "ctx", None),
            P("exp"),
            P("exp", None),
            P("exp", None),
            P("exp", None),
            P("exp", None),
            P("exp"),
            P("exp", None),
            P("exp", "ctx", None),
            P("exp", "ctx", None),
            P("exp", "ctx", None),
        ),
        out_specs=(
            P("exp", "ctx", None),
            P("exp", "ctx", None),
            P("exp"),
            P("exp", None),
            P("exp", None),
            P("exp", None),
            P("exp", None),
            P("exp"),
            P("exp", None),
            P("exp", "ctx", None),
            P("exp", "ctx", None),
            P("exp", "ctx", None),
        ),
        check_vma=False,
    )
```

profile of v0, /device:TPU:2, one launch (start us, length us, event | category | flops | bytes accessed | tf_op | source)
XLA Modules:
  0.0 1222.1 jit_solution(11140493342865274893)
XLA Ops:
  12.4 39.1 %all-reduce.5 = (bf16[1024]{0:T(1024)(128)(2,1)S(1)}, bf16[1024]{0:T(1024)(128)(2,1)S(1)}) all-reduce(bf16[1024]{0:T(1024)(128)(2,1)S(1)} %dynamic-update-slice, bf16[1024]{0:T(1024)(128)(2,1)S(1)} %dynamic-update-slice.1), channel_id=1, replica_groups=mesh['ctx'=8,'exp'=16] {'exp'}, use_global_device_ids=true, to_apply=%add | all-reduce | flops 2048 | bytes 8192
  64.4 40.0 %all-gather.15.cloned.1.call-done = bf16[1024,512]{1,0:T(8,128)(2,1)} async-done(((bf16[64,512]{1,0:T(8,128)(2,1)}), bf16[1024,512]{1,0:T(8,128)(2,1)}) %all-gather.15.cloned.1.call-update) | async-done | bytes 1048592 | tf_op jit(solution)/shard_map/all_gather | solution.py:88
  110.5 9.0 reduce-window.6
  130.7 11.2 all-gather.13.cloned.1.call-done
  143.4 50.6 %all-gather.19.cloned.1.call-done = bf16[1024,1024]{1,0:T(8,128)(2,1)} async-done(((bf16[64,1024]{1,0:T(8,128)(2,1)}), bf16[1024,1024]{1,0:T(8,128)(2,1)}) %all-gather.19.cloned.1.call-update) | async-done | bytes 2097168 | tf_op jit(solution)/shard_map/all_gather | solution.py:87
  199.2 32.0 %all-gather.17.cloned.1.call-done = bf16[1024,512]{0,1:T(8,128)(2,1)} async-done(((bf16[128,512]{0,1:T(8,128)(2,1)}), bf16[1024,512]{0,1:T(8,128)(2,1)}) %all-gather.17.cloned.1.call-update) | async-done | bytes 1048592 | tf_op jit(solution)/shard_map/all_gather | solution.py:131
  238.8 45.6 %all-gather.21.cloned.1.call-done = bf16[1024,1024]{1,0:T(8,128)(2,1)} async-done(((bf16[64,1024]{1,0:T(8,128)(2,1)}), bf16[1024,1024]{1,0:T(8,128)(2,1)}) %all-gather.21.cloned.1.call-update) | async-done | bytes 2097168 | tf_op jit(solution)/shard_map/all_gather | solution.py:90
  299.9 55.3 %all-gather = bf16[16,64,32]{1,2,0:T(8,128)(2,1)S(1)} all-gather(bf16[1,64,32]{1,2,0:T(8,128)(2,1)S(1)} %bitcast.312), channel_id=1, replica_groups=mesh['ctx'=8,'exp'=16] {'exp'}, dimensions={0}, use_global_device_ids=true | all-gather | bytes 69632 | tf_op jit(solution)/shard_map/all_gather | solution.py:91
  357.1 8.2 scatter_custom_fusion.2
  369.8 6.0 fusion.26
  377.4 6.1 fusion.28
  383.5 49.6 %all-gather.27.cloned.1.call-done = bf16[2,512,1024]{2,1,0:T(8,128)(2,1)} async-done(((bf16[2,64,1024]{2,1,0:T(8,128)(2,1)}), bf16[2,512,1024]{2,1,0:T(8,128)(2,1)}) %all-gather.27.cloned.1.call-update) | async-done | bytes 2097168 | tf_op jit(solution)/shard_map/all_gather | solution.py:98
  433.1 9.3 fusion.15
  446.3 6.6 all-to-all-start.1
  460.9 34.4 %all-to-all-done.1 = bf16[16,2,48,1024]{3,2,1,0:T(8,128)(2,1)S(1)} async-done(((bf16[16,2,48,1024]{3,2,1,0:T(8,128)(2,1)}), bf16[16,2,48,1024]{3,2,1,0:T(8,128)(2,1)S(1)}, u32[]{:S(2)}, u32[]{:S(2)}) %all-to-all-start.1) | async-done | bytes 3145760 | tf_op jit(solution)/shard_map/all_to_all | solution.py:173
  497.0 5.8 all-to-all-start.3
  505.6 8.5 gather_fusion.1
  521.3 23.9 %all-to-all-done.3 = bf16[16,2,48,1024]{3,2,1,0:T(8,128)(2,1)S(1)} async-done(((bf16[16,2,48,1024]{3,2,1,0:T(8,128)(2,1)}), bf16[16,2,48,1024]{3,2,1,0:T(8,128)(2,1)S(1)}, u32[]{:S(2)}, u32[]{:S(2)}) %all-to-all-start.3) | async-done | bytes 3145760 | tf_op jit(solution)/shard_map/all_to_all | solution.py:209
  545.2 5.8 gather_fusion.2
  585.3 5.7 bitcast_convert_fusion.1
  606.6 37.1 %reduce-scatter.31.cloned.1.call-done = bf16[128,512]{1,0:T(8,128)(2,1)} async-done(((bf16[1024,512]{1,0:T(8,128)(2,1)}), bf16[128,512]{1,0:T(8,128)(2,1)}) %reduce-scatter.31.cloned.1.call-update) | async-done | bytes 131088
  648.7 65.7 %reduce-scatter.35.cloned.1.call-done = bf16[64,32]{1,0:T(8,128)(2,1)} async-done(((bf16[1024,32]{1,0:T(8,128)(2,1)}), bf16[64,32]{1,0:T(8,128)(2,1)}) %reduce-scatter.35.cloned.1.call-update) | async-done | bytes 4112
  715.2 40.3 %reduce-scatter.29.cloned.1.call-done = bf16[2,64,1024]{2,1,0:T(8,128)(2,1)} async-done(((bf16[2,512,1024]{2,1,0:T(8,128)(2,1)}), bf16[2,64,1024]{2,1,0:T(8,128)(2,1)}) %reduce-scatter.29.cloned.1.call-update) | async-done | bytes 262160 | tf_op jit(solution)/shard_map/reduce_scatter | solution.py:332
  757.3 42.2 %reduce-scatter.27.cloned.1.call-done = bf16[2,128,512]{2,1,0:T(8,128)(2,1)} async-done(((bf16[2,1024,512]{2,1,0:T(8,128)(2,1)}), bf16[2,128,512]{2,1,0:T(8,128)(2,1)}) %reduce-scatter.27.cloned.1.call-update) | async-done | bytes 262160 | tf_op jit(solution)/shard_map/reduce_scatter | solution.py:329
  801.3 41.6 %reduce-scatter.25.cloned.1.call-done = bf16[2,128,512]{2,1,0:T(8,128)(2,1)} async-done(((bf16[2,1024,512]{2,1,0:T(8,128)(2,1)}), bf16[2,128,512]{2,1,0:T(8,128)(2,1)}) %reduce-scatter.25.cloned.1.call-update) | async-done | bytes 262160 | tf_op jit(solution)/shard_map/reduce_scatter | solution.py:326
  847.1 34.6 %all-reduce.4 = (bf16[1024]{0:T(1024)(128)(2,1)S(1)}, bf16[1024]{0:T(1024)(128)(2,1)S(1)}) all-reduce(bf16[1024]{0:T(1024)(128)(2,1)S(1)} %get-tuple-element.16, bf16[1024]{0:T(1024)(128)(2,1)S(1)} %get-tuple-element.14), channel_id=4, replica_groups=mesh['ctx'=8,'exp'=16] {'exp'}, use_global_device_ids=true, to_apply=%region_25.26.clone | all-reduce | flops 2048 | bytes 8192
  881.9 18.7 %all-reduce.6 = (bf16[64]{0:T(256)(128)(2,1)S(1)}, bf16[64]{0:T(256)(128)(2,1)S(1)}, bf16[64,32]{0,1:T(8,128)(2,1)S(1)}) all-reduce(bf16[64]{0:T(256)(128)(2,1)S(1)} %dynamic-slice.3, bf16[64]{0:T(256)(128)(2,1)S(1)} %dynamic-slice.5, bf16[64,32]{0,1:T(8,128)(2,1)S(1)} %copy.150), channel_id=1, replica_groups=mesh['ctx'=8,'exp'=16] {'ctx'}, use_global_device_ids=true, to_apply=%region_26.27 | all-reduce | flops 2176 | bytes 8704 | tf_op jit(solution)/shard_map/psum | solution.py:322
  902.2 18.1 %reduce-scatter.23.cloned.1.call-done = bf16[64,1024]{1,0:T(8,128)(2,1)} async-done(((bf16[1024,1024]{1,0:T(8,128)(2,1)}), bf16[64,1024]{1,0:T(8,128)(2,1)}) %reduce-scatter.23.cloned.1.call-update) | async-done | bytes 131088 | tf_op jit(solution)/shard_map/reduce_scatter | solution.py:303
  920.3 74.2 %reduce-scatter.17.cloned.1.call-done = bf16[64,1024]{1,0:T(8,128)(2,1)} async-done(((bf16[1024,1024]{1,0:T(8,128)(2,1)}), bf16[64,1024]{1,0:T(8,128)(2,1)}) %reduce-scatter.17.cloned.1.call-update) | async-done | bytes 131088 | tf_op jit(solution)/shard_map/reduce_scatter | solution.py:294
  994.5 70.0 %reduce-scatter.21.cloned.1.call-done = bf16[64,512]{1,0:T(8,128)(2,1)} async-done(((bf16[1024,512]{1,0:T(8,128)(2,1)}), bf16[64,512]{1,0:T(8,128)(2,1)}) %reduce-scatter.21.cloned.1.call-update) | async-done | bytes 65552 | tf_op jit(solution)/shard_map/reduce_scatter | solution.py:300
  1064.6 69.7 %reduce-scatter.19.cloned.1.call-done = bf16[64,512]{1,0:T(8,128)(2,1)} async-done(((bf16[1024,512]{1,0:T(8,128)(2,1)}), bf16[64,512]{1,0:T(8,128)(2,1)}) %reduce-scatter.19.cloned.1.call-update) | async-done | bytes 65552 | tf_op jit(solution)/shard_map/reduce_scatter | solution.py:297
  1135.3 73.3 %all-reduce.10.cloned.1.call-done = (bf16[64,1024]{1,0:T(8,128)(2,1)}, bf16[64,512]{1,0:T(8,128)(2,1)}, bf16[64,512]{1,0:T(8,128)(2,1)}, bf16[64,1024]{1,0:T(8,128)(2,1)}) async-done(((bf16[64,1024]{1,0:T(8,128)(2,1)}, bf16[64,512]{1,0:T(8,128)(2,1)}, bf16[64,512]{1,0:T(8,128)(2,1)}, bf16[64,1024]{1,0:T(8,128)(2,1)}), (bf16[64,1024]{1,0:T(8,128)(2,1)}, bf16[64,512]{1,0:T(8,128)(2,1)}, ...) | async-done | bytes 393232 | tf_op jit(solution)/shard_map/psum | solution.py:317
  (274 shorter events, 166.9 us)
Async XLA Ops:
  7.2 98.7 %copy-start.3 = (bf16[1,128,1024]{2,1,0:T(8,128)(2,1)S(1)}, bf16[1,128,1024]{2,1,0:T(8,128)(2,1)}, u32[]{:S(2)}) copy-start(bf16[1,128,1024]{2,1,0:T(8,128)(2,1)} %param.14) | copy-start | bytes 786436
  7.2 50.8 %all-gather.11.cloned.1.call-start = ((), (), s32[]{:S(2)}) async-start(), calls=%async_computation.14 | async-start | bytes 1114112 | tf_op jit(solution)/shard_map/all_gather | solution.py:89
  7.9 96.4 %all-gather.15.cloned.1.call-start = ((), (), s32[]{:S(2)}) async-start(), calls=%async_computation.16 | async-start | bytes 1114112 | tf_op jit(solution)/shard_map/all_gather | solution.py:88
  8.7 133.2 %all-gather.13.cloned.1.call-start = ((), (), s32[]{:S(2)}) async-start(), calls=%async_computation.15 | async-start | bytes 1179648 | tf_op jit(solution)/shard_map/all_gather | solution.py:132
  52.7 56.6 %copy-start.34 = (s32[1,128,8]{1,2,0:T(8,128)S(1)}, s32[1,128,8]{1,2,0:T(8,128)}, u32[]{:S(2)}) copy-start(s32[1,128,8]{1,2,0:T(8,128)} %param.17) | copy-start | bytes 12292
  60.4 133.6 %all-gather.19.cloned.1.call-start = ((), (), s32[]{:S(2)}) async-start(), calls=%async_computation.18 | async-start | bytes 2228224 | tf_op jit(solution)/shard_map/all_gather | solution.py:87
  61.0 170.2 %all-gather.17.cloned.1.call-start = ((), (), s32[]{:S(2)}) async-start(), calls=%async_computation.17 | async-start | bytes 1179648 | tf_op jit(solution)/shard_map/all_gather | solution.py:131
  107.1 177.3 %all-gather.21.cloned.1.call-start = ((), (), s32[]{:S(2)}) async-start(), calls=%async_computation.19 | async-start | bytes 2228224 | tf_op jit(solution)/shard_map/all_gather | solution.py:90
  107.7 262.1 %all-gather.25.cloned.1.call-start = ((), (), s32[]{:S(2)}) async-start(), calls=%async_computation.21 | async-start | bytes 2359296 | tf_op jit(solution)/shard_map/all_gather | solution.py:97
  108.5 268.9 %all-gather.23.cloned.1.call-start = ((), (), s32[]{:S(2)}) async-start(), calls=%async_computation.20 | async-start | bytes 2359296 | tf_op jit(solution)/shard_map/all_gather | solution.py:96
  120.0 74.0 %copy-start.41 = (s32[1024,1]{0,1:T(1,128)}, s32[1024,1]{0,1:T(1,128)S(1)}, u32[]{:S(2)}) copy-start(s32[1024,1]{0,1:T(1,128)S(1)} %compare_select_fusion) | copy-start | bytes 12292
  143.4 91.7 %copy-start.11 = (bf16[1024,512]{0,1:T(8,128)(2,1)}, bf16[1024,512]{0,1:T(8,128)(2,1)S(1)}, u32[]{:S(2)}) copy-start(bf16[1024,512]{0,1:T(8,128)(2,1)S(1)} %copy.107) | copy-start | bytes 3145732
  294.5 61.2 %copy-start.35 = (s32[1,128,8]{1,2,0:T(8,128)S(1)}, s32[1,128,8]{1,2,0:T(8,128)}, u32[]{:S(2)}) copy-start(s32[1,128,8]{1,2,0:T(8,128)} %param.17) | copy-start | bytes 12292
  294.5 70.8 %all-to-all-start = ((bf16[16,2,48,1024]{3,2,1,0:T(8,128)(2,1)}), bf16[16,2,48,1024]{3,2,1,0:T(8,128)(2,1)}, u32[]{:S(2)}, u32[]{:S(2)}) async-start(bf16[16,2,48,1024]{3,2,1,0:T(8,128)(2,1)} %broadcast_select_fusion), calls=%async_computation | async-start | bytes 6291456 | tf_op jit(solution)/shard_map/all_to_all | solution.py:164
  299.1 134.0 %all-gather.27.cloned.1.call-start = ((), (), s32[]{:S(2)}) async-start(), calls=%async_computation.22 | async-start | bytes 2359296 | tf_op jit(solution)/shard_map/all_gather | solution.py:98
  299.9 65.4 %copy-start.10 = (f32[128,1024]{1,0:T(8,128)}, f32[128,1024]{1,0:T(8,128)S(1)}, u32[]{:S(2)}) copy-start(f32[128,1024]{1,0:T(8,128)S(1)} %bitcast_convert_fusion.4) | copy-start | bytes 1572868
  365.3 67.8 %all-to-all-start.2 = ((bf16[16,2,48,1024]{3,2,1,0:T(8,128)(2,1)}), bf16[16,2,48,1024]{3,2,1,0:T(8,128)(2,1)}, u32[]{:S(2)}, u32[]{:S(2)}) async-start(bf16[16,2,48,1024]{3,2,1,0:T(8,128)(2,1)} %bitcast.43), calls=%async_computation.2 | async-start | bytes 6291456 | tf_op jit(solution)/shard_map/all_to_all | solution.py:190
  446.3 49.0 %all-to-all-start.1 = ((bf16[16,2,48,1024]{3,2,1,0:T(8,128)(2,1)}), bf16[16,2,48,1024]{3,2,1,0:T(8,128)(2,1)S(1)}, u32[]{:S(2)}, u32[]{:S(2)}) async-start(bf16[16,2,48,1024]{3,2,1,0:T(8,128)(2,1)} %copy.120), calls=%async_computation.1 | async-start | bytes 6291456 | tf_op jit(solution)/shard_map/all_to_all | solution.py:173
  497.0 48.2 %all-to-all-start.3 = ((bf16[16,2,48,1024]{3,2,1,0:T(8,128)(2,1)}), bf16[16,2,48,1024]{3,2,1,0:T(8,128)(2,1)S(1)}, u32[]{:S(2)}, u32[]{:S(2)}) async-start(bf16[16,2,48,1024]{3,2,1,0:T(8,128)(2,1)} %copy.123), calls=%async_computation.3 | async-start | bytes 6291456 | tf_op jit(solution)/shard_map/all_to_all | solution.py:209
  502.8 101.2 %reduce-scatter.33.cloned.1.call-start = ((), (), s32[]{:S(2)}) async-start(), calls=%async_computation.31 | async-start | bytes 1179648
  563.7 79.9 %reduce-scatter.31.cloned.1.call-start = ((), (), s32[]{:S(2)}) async-start(), calls=%async_computation.30 | async-start | bytes 1179648
  578.2 136.2 %reduce-scatter.35.cloned.1.call-start = ((), (), s32[]{:S(2)}) async-start(), calls=%async_computation.32 | async-start | bytes 278528
  579.3 176.1 %reduce-scatter.29.cloned.1.call-start = ((), (), s32[]{:S(2)}) async-start(), calls=%async_computation.29 | async-start | bytes 2359296 | tf_op jit(solution)/shard_map/reduce_scatter | solution.py:332
  585.3 214.3 %reduce-scatter.27.cloned.1.call-start = ((), (), s32[]{:S(2)}) async-start(), calls=%async_computation.28 | async-start | bytes 2359296 | tf_op jit(solution)/shard_map/reduce_scatter | solution.py:329
  591.0 251.8 %reduce-scatter.25.cloned.1.call-start = ((), (), s32[]{:S(2)}) async-start(), calls=%async_computation.27 | async-start | bytes 2359296 | tf_op jit(solution)/shard_map/reduce_scatter | solution.py:326
  596.3 324.0 %reduce-scatter.23.cloned.1.call-start = ((), (), s32[]{:S(2)}) async-start(), calls=%async_computation.26 | async-start | bytes 2228224 | tf_op jit(solution)/shard_map/reduce_scatter | solution.py:303
  598.4 396.1 %reduce-scatter.17.cloned.1.call-start = ((), (), s32[]{:S(2)}) async-start(), calls=%async_computation.23 | async-start | bytes 2228224 | tf_op jit(solution)/shard_map/reduce_scatter | solution.py:294
  603.9 460.7 %reduce-scatter.21.cloned.1.call-start = ((), (), s32[]{:S(2)}) async-start(), calls=%async_computation.25 | async-start | bytes 1114112 | tf_op jit(solution)/shard_map/reduce_scatter | solution.py:300
  606.5 527.7 %reduce-scatter.19.cloned.1.call-start = ((), (), s32[]{:S(2)}) async-start(), calls=%async_computation.24 | async-start | bytes 1114112 | tf_op jit(solution)/shard_map/reduce_scatter | solution.py:297
  646.4 562.2 %all-reduce.10.cloned.1.call-start = ((), (), s32[]{:S(2)}) async-start(), calls=%async_computation.33 | async-start | bytes 786432 | tf_op jit(solution)/shard_map/psum | solution.py:317
  647.1 199.5 %copy-start.24 = (bf16[128,512]{1,0:T(8,128)(2,1)S(1)}, bf16[128,512]{1,0:T(8,128)(2,1)}, u32[]{:S(2)}) copy-start(bf16[128,512]{1,0:T(8,128)(2,1)} %reduce-scatter.33.cloned.1.call-done) | copy-start | bytes 393220
  648.7 197.8 %copy-start.13 = (bf16[1024,512]{1,0:T(8,128)(2,1)S(1)}, bf16[1024,512]{1,0:T(8,128)(2,1)}, u32[]{:S(2)}) copy-start(bf16[1024,512]{1,0:T(8,128)(2,1)} %all-gather.11.cloned.1.call-done) | copy-start | bytes 3145732
  (42 other events, 569.3 us)
Sparse Core Ops, SparseCore 0:
  10.5 47.5 all-gather.10
  60.5 43.8 all-gather.14
  106.6 35.2 all-gather.12
  144.2 49.7 all-gather.18
  196.0 35.1 all-gather.16
  233.5 50.8 all-gather.20
  286.1 49.4 all-gather.24
  337.2 40.1 all-gather.22
  379.1 53.9 all-gather.26
  563.9 39.4 reduce-scatter.32
  605.8 37.8 reduce-scatter.30
  647.8 66.5 reduce-scatter.34
  717.0 38.4 reduce-scatter.28
  757.9 41.6 reduce-scatter.26
  801.9 40.9 reduce-scatter.24
  847.2 73.0 reduce-scatter.22
  924.6 69.8 reduce-scatter.16
  998.7 65.7 reduce-scatter.20
  1068.4 65.7 reduce-scatter.18
  1137.0 71.5 all-reduce.9
where the time goes:
time: 1230 us; the launch traced here: 1220 us
  waiting for transfers between devices  831 us (68%)
  blocking collectives  148 us (12%)
  matrix products  85.5 us (7%)
  local copies, waits for them, and re-layouts  59.1 us (5%)
  other arithmetic  58.6 us (5%)
  starting transfers between devices  22.8 us (2%)
  between operations  17.1 us (1%)
    unnamed x23, waiting for transfers between devices  108 us
    reduce_scatter x1, waiting for transfers between devices, body(): lax.psum_scatter(grad_wq.astype(jnp.bfloat16), 'exp', scatter_dimension=0...  74.2 us
    unnamed x2, blocking collectives  73.7 us
    psum x1, waiting for transfers between devices, body(): lax.psum(shares[0].astype(jnp.bfloat16), 'ctx').astype(jnp.float32)  73.3 us
    reduce_scatter x1, waiting for transfers between devices, body(): lax.psum_scatter(grad_wv.astype(jnp.bfloat16), 'exp', scatter_dimension=0...  70 us
    reduce_scatter x1, waiting for transfers between devices, body(): lax.psum_scatter(grad_wk.astype(jnp.bfloat16), 'exp', scatter_dimension=0...  69.7 us
    all_gather x1, blocking collectives, body(): lax.all_gather(w_router, 'exp', axis=0, tiled=True)  55.3 us
    all_gather x1, waiting for transfers between devices, body(): lax.all_gather(w_query, 'exp', axis=0, tiled=True)  50.6 us
  transfers between devices with their start and end apart: 24, of which 20 were waited for; matrix products, arithmetic and copies ran while one was open for 13% of the time, Pallas kernels for 0%

commit v1 on v0

v1 whole, which is shorter than its diff:
```python
import jax
import jax.numpy as jnp
from jax import lax
from jax.experimental import pallas as pl
from jax.experimental.pallas import tpu as pltpu
from jax.sharding import PartitionSpec as P

HEAD_SIZE = 64
HALF = 32
N_CTX = 8
N_EXP = 16
eps_norm = 1e-06
rope_base = 10000.0
neg_big = -1e30
f32, bf16 = jnp.float32, jnp.bfloat16

MESH = pl.DeviceIdType.MESH
ANY = pl.BlockSpec(memory_space=pl.ANY)
VMEM = pl.BlockSpec(memory_space=pltpu.VMEM)
DMA = pltpu.SemaphoreType.DMA
NEAR_LAST = (6, 2, 4, 5, 3, 1, 7)
NEAR_FIRST = (1, 7, 3, 5, 4, 2, 6)
CTX_ORDER = (2, 6, 4, 1, 3, 5, 7)


def remote(src, dst, send, recv, where):
    return pltpu.make_async_remote_copy(
        src_ref=src, dst_ref=dst, send_sem=send, recv_sem=recv, device_id=where, device_id_type=MESH
    )


def greet(places, amount=None):
    barrier = pltpu.get_barrier_semaphore()
    for where in places:
        pl.semaphore_signal(barrier, inc=1, device_id=where, device_id_type=MESH)
    pl.semaphore_wait(barrier, len(places) if amount is None else amount)


class Here:
    def __init__(self):
        self.c = lax.axis_index("ctx")
        self.e = lax.axis_index("exp")
        self.core = lax.rem(self.e, 2)
        self.chip = self.e // 2
        self.partner = {"exp": self.e + 1 - 2 * self.core}

    def ctx(self, k):
        return lax.rem(self.c + k, N_CTX)

    def chip_at(self, k):
        return lax.rem(self.chip + k, 8)

    def ctx_peers(self):
        return [{"ctx": self.ctx(k)} for k in range(1, N_CTX)]

    def same_core(self, k):
        return {"exp": 2 * self.chip_at(k) + self.core}

    def exp_peers(self):
        return [self.partner] + [self.same_core(k) for k in range(1, 8)]

    def other_core_peers(self):
        return [{"exp": 2 * self.chip_at(k) + 1 - self.core} for k in range(1, 8)]


class Gather:
    sems = (8, 8)

    def __init__(self, here, x, out, send, recv):
        self.copies = [pltpu.make_async_copy(x, out.at[here.c], send.at[0])]
        for k in CTX_ORDER:
            self.copies.append(remote(x, out.at[here.c], send.at[k], recv.at[k], {"ctx": here.ctx(k)}))

    def start(self):
        for c in self.copies:
            c.start()

    def wait(self):
        for c in self.copies:
            c.wait()


class Turn:
    sems = (8, 8)

    def __init__(self, here, x, out, send, recv):
        rows, cols = out.shape[0], x.shape[1]
        into = out.at[:, pl.ds(pl.multiple_of(here.c * cols, cols), cols)]

        def part(j):
            return x.at[pl.ds(pl.multiple_of(j * rows, rows), rows)]

        self.copies = [pltpu.make_async_copy(part(here.c), into, send.at[0])]
        for k in CTX_ORDER:
            j = here.ctx(k)
            self.copies.append(remote(part(j), into, send.at[k], recv.at[k], {"ctx": j}))

    start = Gather.start
    wait = Gather.wait


class PairGather:
    sems = (8, 8, 8, 8)

    def __init__(self, here, x, out, send, recv, fsend, frecv):
        e = here.e
        self.own = pltpu.make_async_copy(x, out.at[e], fsend.at[0])
        self.first = remote(x, out.at[e], send.at[0], recv.at[0], here.partner)
        self.far, self.forward = {}, {}
        for k in NEAR_LAST:
            self.far[k] = remote(x, out.at[e], send.at[k], recv.at[k], here.same_core(k))
            slot = 2 * here.chip_at(8 - k) + here.core
            self.forward[k] = remote(out.at[slot], out.at[slot], fsend.at[k], frecv.at[k], here.partner)

    def start(self):
        for k in NEAR_LAST:
            self.far[k].start()
        self.first.start()
        self.own.start()

    def pass_on(self):
        for k in NEAR_FIRST:
            self.far[k].wait_recv()
            self.forward[k].start()

    def wait(self):
        self.own.wait()
        self.first.wait()
        for k in NEAR_FIRST:
            self.far[k].wait_send()
            self.forward[k].wait()


class PairScatter:
    sems = (8, 8, 8, 8, 8)

    @staticmethod
    def scratch(x):
        return [pltpu.VMEM((8,) + x.shape[1:], x.dtype)] * 4

    def __init__(self, here, x, total, mine, near, summed, far, load, nsend, nrecv, fsend, frecv):
        self.total, self.mine, self.near, self.summed, self.far = total, mine, near, summed, far
        self.loads, self.nears, self.fars = {}, {}, {}
        self.order = NEAR_LAST + (0,)
        for k in self.order:
            there = here.chip_at(k)
            self.nears[k] = remote(x.at[2 * there + 1 - here.core], near.at[k], nsend.at[k], nrecv.at[k], here.partner)
            self.loads[k] = pltpu.make_async_copy(x.at[2 * there + here.core], mine.at[k], load.at[k])
            if k:
                self.fars[k] = remote(summed.at[k], far.at[k], fsend.at[k], frecv.at[k], here.same_core(k))

    def start(self):
        for k in self.order:
            self.nears[k].start()
            self.loads[k].start()

    def pass_on(self):
        for k in self.order:
            self.loads[k].wait()
            self.nears[k].wait_recv()
            both = self.mine[k].astype(f32) + self.near[k].astype(f32)
            if k:
                self.summed[k] = both.astype(self.summed.dtype)
                self.fars[k].start()
            else:
                self.total[...] = both

    def wait(self):
        for k in NEAR_FIRST:
            self.fars[k].wait_recv()
            self.total[...] += self.far[k].astype(f32)
        for k in self.order:
            self.nears[k].wait_send()
            if k:
                self.fars[k].wait_send()


class Spread:
    sems = (16, 16)

    def __init__(self, here, x, out, send, recv):
        self.copies = [pltpu.make_async_copy(x.at[here.e], out.at[here.e], send.at[0])]
        for k in range(1, N_EXP):
            j = lax.rem(here.e + k, N_EXP)
            self.copies.append(remote(x.at[j], out.at[here.e], send.at[k], recv.at[k], {"exp": j}))

    start = Gather.start
    wait = Gather.wait


def sem_shapes(*kinds):
    return [DMA((n,)) for kind in kinds for n in kind.sems]


def params(cid):
    return pltpu.CompilerParams(collective_id=cid, has_side_effects=True, vmem_limit_bytes=40 * 2**20)


def call(kernel, outs, scratch, cid, *args, out_specs=None):
    return pl.pallas_call(
        kernel,
        out_shape=outs,
        in_specs=[ANY] * len(args),
        out_specs=out_specs or [ANY] * len(outs),
        scratch_shapes=scratch,
        compiler_params=params(cid),
    )(*args)


def shape(s, t):
    return jax.ShapeDtypeStruct(s, t)


def start_exchange(tokens, pack, wo, cot):
    def kernel(x, p, w, u, xs, ps, ws, us, *sems):
        here = Here()
        greet(here.ctx_peers() + here.exp_peers())
        a = Gather(here, x, xs, *sems[0:2])
        g = [PairGather(here, i, o, *sems[2 + 4 * n : 6 + 4 * n]) for n, (i, o) in enumerate(((p, ps), (w, ws), (u, us)))]
        a.start()
        for i in g:
            i.start()
        for i in g:
            i.pass_on()
        a.wait()
        for i in g:
            i.wait()

    return call(
        kernel,
        [shape((8,) + tokens.shape, bf16)] + [shape((16,) + a.shape, bf16) for a in (pack, wo, cot)],
        sem_shapes(Gather, PairGather, PairGather, PairGather),
        1,
        tokens,
        pack,
        wo,
        cot,
    )


def turn_exchange(attn):
    def kernel(x, out, *sems):
        here = Here()
        greet(here.ctx_peers())
        t = Turn(here, x, out, *sems)
        t.start()
        t.wait()

    return call(kernel, [shape((attn.shape[0] // 8, attn.shape[1] * 8), attn.dtype)], sem_shapes(Turn), 2, attn)[0]


def routed_exchange(routed, gates):
    def kernel(x, g, xs, gs, *sems):
        here = Here()
        greet(here.exp_peers())
        items = [PairGather(here, g, gs, *sems[4:8]), PairGather(here, x, xs, *sems[0:4])]
        for i in items:
            i.start()
        for i in items:
            i.pass_on()
        for i in items:
            i.wait()

    return call(
        kernel,
        [shape((16,) + a.shape, a.dtype) for a in (routed, gates)],
        sem_shapes(PairGather, PairGather),
        3,
        routed,
        gates,
    )


def grad_exchange(parts, gate_parts):
    def kernel(x, g, total, gs, *rest):
        here = Here()
        greet(here.exp_peers() + here.other_core_peers())
        sems = rest[4:]
        small = Spread(here, g, gs, *sems[5:7])
        s = PairScatter(here, x, total, *rest[:4], *sems[0:5])
        s.start()
        small.start()
        s.pass_on()
        s.wait()
        small.wait()

    return call(
        kernel,
        [shape(parts.shape[1:], f32), shape(gate_parts.shape, f32)],
        PairScatter.scratch(parts) + sem_shapes(PairScatter, Spread),
        4,
        parts,
        gate_parts,
        out_specs=[VMEM, ANY],
    )


def branch_exchange(branch, out_parts):
    def kernel(b, x, bs, total, *rest):
        here = Here()
        greet(here.ctx_peers() + here.exp_peers())
        sems = rest[4:]
        a = Gather(here, b, bs, *sems[5:7])
        s = PairScatter(here, x, total, *rest[:4], *sems[0:5])
        a.start()
        s.start()
        s.pass_on()
        s.wait()
        a.wait()

    return call(
        kernel,
        [shape((8,) + branch.shape, bf16), shape(out_parts.shape[1:], f32)],
        PairScatter.scratch(out_parts) + sem_shapes(PairScatter, Gather),
        5,
        branch,
        out_parts,
        out_specs=[ANY, VMEM],
    )


def last_exchange(grads, shares):
    def kernel(g, x, back, alls, wos, total, low, *rest):
        here = Here()
        greet(here.ctx_peers() + here.exp_peers())
        sems = rest[4:]
        turn = Turn(here, g, back, *sems[5:7])
        s = PairScatter(here, x, total, *rest[:4], *sems[0:5])
        spread = Gather(here, low, alls, *sems[7:9])
        wsend, wrecv = sems[9:11]
        chunk = pl.ds(256, 128)
        moves = [pltpu.make_async_copy(alls.at[here.chip, :, chunk], wos.at[here.chip], wsend.at[0])]
        for k in NEAR_LAST:
            moves.append(
                remote(alls.at[here.chip_at(k), :, chunk], wos.at[here.chip], wsend.at[k], wrecv.at[k], here.same_core(k))
            )
        s.start()
        turn.start()
        s.pass_on()
        s.wait()
        low[...] = total[...].astype(bf16)
        spread.start()
        spread.wait()
        for m in moves:
            m.start()
        for m in moves:
            m.wait()
        turn.wait()

    rows, cols = shares.shape[1:]
    return call(
        kernel,
        [
            shape((grads.shape[0] // 8, grads.shape[1] * 8), bf16),
            shape((8, rows, cols), bf16),
            shape((8, rows, 128), bf16),
        ],
        [pltpu.VMEM((rows, cols), f32), pltpu.VMEM((rows, cols), bf16)]
        + PairScatter.scratch(shares)
        + sem_shapes(PairScatter, Turn, Gather, Gather),
        6,
        grads,
        shares,
    )


def dot(a, b, dims=((1,), (0,))):
    return lax.dot_general(a, b, (dims, ((), ())), preferred_element_type=f32)


NT = ((1,), (1,))
TN = ((0,), (0,))


def swap_halves(x):
    parts = []
    for i in range(0, x.shape[1], HEAD_SIZE):
        parts += [-x[:, i + HALF : i + HEAD_SIZE], x[:, i : i + HALF]]
    return jnp.concatenate(parts, axis=1)


def unswap_halves(x):
    return -swap_halves(x)


def factor_of(values):
    return lax.rsqrt(jnp.mean(values * values, axis=-1, keepdims=True) + eps_norm)


def normalize_back(values, factor, gain, upstream):
    scaled = upstream * gain
    inner = jnp.mean(scaled * values, axis=-1, keepdims=True)
    return factor * scaled - values * factor * factor * factor * inner


def body(
    tokens, cotangent, span_order, expert_choice, norm_attn, w_query, key_matrix, value_matrix,
    w_out, norm_moe, w_router, w_gate, w_up, w_down,
):
    c = lax.axis_index("ctx")
    tokens, cotangent, choice = tokens[0], cotangent[0], expert_choice[0]
    rows, width = tokens.shape
    own_rows = w_query.shape[0]
    wgu_own = jnp.concatenate([w_gate[0], w_gate[1], w_up[0], w_up[1]], axis=1)
    wgu = lax.all_gather(wgu_own, "ctx", axis=0, tiled=True)
    wd_own = jnp.concatenate([w_down[0], w_down[1]], axis=1)
    wd_wide = lax.all_gather(wd_own, "ctx", axis=0, tiled=True)
    wd = jnp.concatenate([wd_wide[:, :width], wd_wide[:, width:]], axis=0)
    wqkv_own = jnp.concatenate(
        [
            w_query.reshape(own_rows, N_CTX, 128),
            key_matrix.reshape(own_rows, N_CTX, 64),
            value_matrix.reshape(own_rows, N_CTX, 64),
        ],
        axis=2,
    ).reshape(own_rows, N_CTX * 256)
    wqkv = lax.all_gather(wqkv_own, "exp", axis=0, tiled=True)
    own_cols = lax.dynamic_slice_in_dim(wqkv_own, c * 256, 256, axis=1)
    pack = jnp.concatenate(
        [
            own_cols,
            swap_halves(own_cols[:, :192]),
            w_router,
            norm_attn[:, None],
            norm_moe[:, None],
            jnp.zeros((own_rows, 512 - 448 - 34), bf16),
        ],
        axis=1,
    )
    x_all, pack_all, wo, up_all = start_exchange(tokens, pack, w_out, cotangent)
    pack_all = pack_all.reshape(width, 512)
    wo = wo.reshape(width, width)
    up_all = up_all.reshape(N_EXP * rows, width)
    gain_a = pack_all[:, 480].astype(f32)[None, :]
    gain_m = pack_all[:, 481].astype(f32)[None, :]
    wr = pack_all[:, 448:480]
    count = N_CTX * rows
    span_len = rows // 2
    ids = jnp.arange(count, dtype=jnp.int32)
    table = ids[:, None] // span_len == jnp.arange(2 * N_CTX, dtype=jnp.int32)[None, :]
    places = jnp.sum(jnp.where(table, span_order[None, :], 0), axis=1) * span_len + ids % span_len
    freqs = rope_base ** (-(jnp.arange(HALF, dtype=f32) * 2.0 / HEAD_SIZE))
    turned = places.astype(f32)[:, None] * freqs[None, :]
    cosine = jnp.tile(jnp.cos(turned), (1, 6))
    sine = jnp.tile(jnp.sin(turned), (1, 6))
    x_seq = x_all.reshape(count, width).astype(f32)
    h_all = (x_seq * factor_of(x_seq) * gain_a).astype(bf16)
    projected = dot(h_all, pack_all[:, :448])
    qk = (projected[:, :192] * cosine + projected[:, 256:448] * sine).astype(bf16)
    v = projected[:, 192:256].astype(bf16)
    q = qk[:, :128].reshape(count, 2, HEAD_SIZE)
    k = qk[:, 128:]
    visible = places[None, :] <= places[:, None]
    scores = jnp.einsum("qhd,kd->hqk", q, k, preferred_element_type=f32) * HEAD_SIZE ** (-0.5)
    scores = jnp.where(visible[None], scores, neg_big)
    largest = jnp.max(scores, axis=-1, keepdims=True)
    shifted = jnp.exp(scores - largest)
    probs = shifted / jnp.sum(shifted, axis=-1, keepdims=True)
    probs_low = probs.astype(bf16)
    attn = jnp.einsum("hqk,kd->qhd", probs_low, v, preferred_element_type=f32)
    attn = attn.reshape(count, 128).astype(bf16)
    attn_low = turn_exchange(attn)
    inputs = tokens.astype(f32)
    upstream = cotangent.astype(f32)
    x_mid = inputs + dot(attn_low, wo)
    factor_two = factor_of(x_mid)
    routed_in = (x_mid * factor_two * gain_m).astype(bf16)
    logits = dot(routed_in, wr)
    expert_ids = jnp.arange(32, dtype=jnp.int32)
    chosen = jnp.any(choice[:, :, None] == expert_ids[None, None, :], axis=1)
    masked = jnp.where(chosen, logits, neg_big)
    lifted = jnp.where(chosen, jnp.exp(masked - jnp.max(masked, axis=-1, keepdims=True)), 0.0)
    gates = lifted / jnp.sum(lifted, axis=-1, keepdims=True)
    routed_all, gates_all = routed_exchange(routed_in, gates.T)
    e = lax.axis_index("exp")
    routed_all = routed_all.reshape(N_EXP * rows, width)
    own_gates = lax.dynamic_slice_in_dim(gates_all, e * 2, 2, axis=1)
    own_gates = own_gates.transpose(0, 2, 1).reshape(N_EXP * rows, 2)
    f = wd.shape[0] // 2
    gate_col = jnp.concatenate(
        [jnp.broadcast_to(own_gates[:, i : i + 1], (N_EXP * rows, f)) for i in range(2)], axis=1
    )
    lifted_h = dot(routed_all, wgu)
    gate_h, up_h = lifted_h[:, : 2 * f], lifted_h[:, 2 * f :]
    sig = jax.nn.sigmoid(gate_h)
    silu = gate_h * sig
    hidden = silu * up_h
    hidden_gated = (hidden * gate_col).astype(bf16)
    out_part = dot(hidden_gated, wd).astype(bf16)
    back = dot(up_all, wd, NT)
    gate_parts = jnp.sum((hidden * back).reshape(N_EXP * rows, 2, f), axis=2)
    grad_hidden = back * gate_col
    grad_lifted = jnp.concatenate(
        [
            (grad_hidden * up_h * (sig * (1.0 + gate_h * (1.0 - sig)))).astype(bf16),
            (grad_hidden * silu).astype(bf16),
        ],
        axis=1,
    )
    in_part = dot(grad_lifted, wgu, NT).astype(bf16)
    grad_wgu = dot(routed_all, grad_lifted, TN).astype(bf16)
    grad_wd = jnp.concatenate(
        [dot(hidden_gated[:, i * f : (i + 1) * f], up_all, TN) for i in range(2)], axis=1
    ).astype(bf16)
    gate_parts = jnp.pad(gate_parts.reshape(N_EXP, rows, 2).transpose(0, 2, 1), ((0, 0), (0, 6), (0, 0)))
    grad_routed, gate_back = grad_exchange(in_part.reshape(N_EXP, rows, width), gate_parts)
    wgu_share = lax.psum_scatter(grad_wgu, "ctx", scatter_dimension=0, tiled=True).astype(f32)
    wd_share = lax.psum_scatter(grad_wd, "ctx", scatter_dimension=0, tiled=True).astype(f32)
    grad_gates = gate_back[:, :2].reshape(32, rows).T
    weighted = gates * grad_gates
    grad_logits = (weighted - gates * jnp.sum(weighted, axis=-1, keepdims=True)).astype(bf16)
    grad_wr = dot(routed_in, grad_logits, TN)
    grad_routed = grad_routed + dot(grad_logits, wr, NT)
    grad_gain_m = jnp.sum(grad_routed * x_mid * factor_two, axis=0)
    grad_mid = upstream + normalize_back(x_mid, factor_two, gain_m, grad_routed)
    branch_all, moe_out = branch_exchange(grad_mid.astype(bf16), out_part.reshape(N_EXP, rows, width))
    result = (x_mid + moe_out).astype(bf16)
    branch_all = branch_all.reshape(count, width)
    wo_rows = lax.dynamic_slice_in_dim(wo, c * 128, 128, axis=0)
    grad_attn = dot(branch_all, wo_rows, NT).astype(bf16)
    grad_wo = dot(attn, branch_all, TN)
    heads_grad = grad_attn.reshape(count, 2, HEAD_SIZE)
    grad_probs = jnp.einsum("qhd,kd->hqk", heads_grad, v, preferred_element_type=f32)
    grad_scores = probs * (grad_probs - jnp.sum(probs * grad_probs, axis=-1, keepdims=True))
    grad_scores = grad_scores.astype(bf16)
    scale = HEAD_SIZE ** (-0.5)
    grad_q = jnp.einsum("hqk,kd->qhd", grad_scores, k, preferred_element_type=f32).reshape(count, 128) * scale
    grad_k = jnp.einsum("hqk,qhd->kd", grad_scores, q, preferred_element_type=f32) * scale
    grad_v = jnp.einsum("hqk,qhd->kd", probs_low, heads_grad, preferred_element_type=f32)
    grad_qk = jnp.concatenate([grad_q, grad_k], axis=1)
    grad_qk = grad_qk * cosine + unswap_halves(grad_qk * sine)
    grad_qkv = jnp.concatenate([grad_qk, grad_v], axis=1).astype(bf16)
    grad_w = dot(h_all, grad_qkv, TN).astype(bf16).reshape(N_EXP, own_rows, 256)
    wo_chunks = grad_wo.astype(bf16).reshape(2, 8, 8, width).transpose(1, 0, 2, 3).reshape(N_EXP, own_rows, 128)
    small = jnp.concatenate(
        [grad_wr, grad_gain_m[:, None], jnp.zeros((width, 128 - 33), f32)], axis=1
    ).astype(bf16)
    shares = jnp.concatenate([grad_w, wo_chunks, small.reshape(N_EXP, own_rows, 128)], axis=2)
    grad_tokens_qkv, owned, wo_owned = last_exchange(grad_qkv, shares)
    grad_h_one = dot(grad_tokens_qkv, wqkv, NT)
    grad_tokens = grad_mid + normalize_back(inputs, factor_of(inputs), gain_a, grad_h_one)
    owned = owned.astype(f32)
    by_head = owned.transpose(1, 0, 2)
    out_wq = by_head[:, :, :128].reshape(own_rows, width)
    out_wk = by_head[:, :, 128:192].reshape(own_rows, width // 2)
    out_wv = by_head[:, :, 192:256].reshape(own_rows, width // 2)
    out_wo = wo_owned.astype(f32).reshape(own_rows, width)
    tail = jnp.sum(owned[:, :, 384:], axis=0)
    out_gain_a = (
        jnp.sum(w_query.astype(f32) * out_wq, axis=1)
        + jnp.sum(key_matrix.astype(f32) * out_wk, axis=1)
        + jnp.sum(value_matrix.astype(f32) * out_wv, axis=1)
    ) / norm_attn.astype(f32)
    f_own = wgu_share.shape[1] // 4
    return (
        result[None],
        grad_tokens[None],
        out_gain_a,
        out_wq,
        out_wk,
        out_wv,
        out_wo,
        tail[:, 32],
        tail[:, :32],
        jnp.stack([wgu_share[:, :f_own], wgu_share[:, f_own : 2 * f_own]]),
        jnp.stack([wgu_share[:, 2 * f_own : 3 * f_own], wgu_share[:, 3 * f_own :]]),
        jnp.stack([wd_share[:, :width], wd_share[:, width:]]),
    )


def solution(mesh):
    return jax.shard_map(
        body,
        mesh=mesh,
        in_specs=(
            P("exp", "ctx", None),
            P("exp", "ctx", None),
            P(),
            P("exp", "ctx", None),
            P("exp"),
            P("exp", None),
            P("exp", None),
            P("exp", None),
            P("exp", None),
            P("exp"),
            P("exp", None),
            P("exp", "ctx", None),
            P("exp", "ctx", None),
            P("exp", "ctx", None),
        ),
        out_specs=(
            P("exp", "ctx", None),
            P("exp", "ctx", None),
            P("exp"),
            P("exp", None),
            P("exp", None),
            P("exp", None),
            P("exp", None),
            P("exp"),
            P("exp", None),
            P("exp", "ctx", None),
            P("exp", "ctx", None),
            P("exp", "ctx", None),
        ),
        check_vma=False,
    )
```

time: 1230 us -> 509 us (0.41)
  waiting for transfers between devices: 831 us -> 0.12 us
  Pallas kernels: 0 us -> 292 us
  blocking collectives: 148 us -> 0 us
  matrix products: 85.5 us -> 114 us
  starting transfers between devices: 22.8 us -> 0.42 us
  other arithmetic: 58.6 us -> 38.5 us
  local copies, waits for them, and re-layouts: 59.1 us -> 40.3 us
    reduce_scatter x7 -> x2, waiting for transfers between devices: 356 us -> 0.01 us  [the longest x1 0.01 us: body(): lax.psum_scatter(grad_wd, 'ctx', scatter_dimension=0, tiled=True)]
    pallas_call x0 -> x6, Pallas kernels: none -> 292 us  [call(): pl.pallas_call(kernel, out_shape=outs, in_specs=[ANY] * len(args), out_sp...]
    all_gather x9 -> x3, waiting for transfers between devices: 236 us -> 0.02 us  [the longest x1 0.02 us: body(): wgu = lax.all_gather(wgu_own, 'ctx', axis=0, tiled=True)]
    unnamed x23 -> x5, waiting for transfers between devices: 108 us -> 0.08 us
    unnamed x2 -> x0, blocking collectives: 73.7 us -> none
    psum x1 -> x0, waiting for transfers between devices: 73.3 us -> none  [body(): lax.psum(shares[0].astype(jnp.bfloat16), 'ctx').astype(jnp.float32)]
    all_to_all x4 -> x0, waiting for transfers between devices: 58.2 us -> none  [the longest x1 34.4 us: body(): lax.all_to_all(expert_out, 'exp', split_axis=0, concat_axis=0, tiled=True)]
    all_gather x1 -> x0, blocking collectives: 55.3 us -> none  [body(): lax.all_gather(w_router, 'exp', axis=0, tiled=True)]
  transfers between devices with their start and end apart: 24 -> 5, of which waited for: 20 -> 0; matrix products, arithmetic and copies ran while one was open for 13% -> 35% of each run, Pallas kernels for 0% -> 58%
where the time goes in v1:
time: 509 us; the launch traced here: 501 us
  Pallas kernels  292 us (57%)
  matrix products  114 us (22%)
  local copies, waits for them, and re-layouts  40.3 us (8%)
  other arithmetic  38.5 us (8%)
  between operations  15.3 us (3%)
    pallas_call x6, Pallas kernels, call(): pl.pallas_call(kernel, out_shape=outs, in_specs=[ANY] * len(args), out_sp...  292 us
    dot_general x16, matrix products, dot(): return lax.dot_general(a, b, (dims, ((), ())), preferred_element_type=f32)  88.7 us
    unnamed x106, local copies, waits for them, and re-layouts  15.8 us
  transfers between devices with their start and end apart: 5, of which 0 were waited for; matrix products, arithmetic and copies ran while one was open for 35% of the time, Pallas kernels for 58%

profile of v1, /device:TPU:2, one launch (start us, length us, event | category | flops | bytes accessed | tf_op | source)
XLA Modules:
  0.0 500.7 jit_solution(175556115783093225)
XLA Ops:
  15.8 72.4 %shard_map.229 = (bf16[8,128,1024]{2,1,0:T(8,128)(2,1)S(1)}, bf16[16,64,512]{2,1,0:T(8,128)(2,1)S(1)}, bf16[16,64,1024]{2,1,0:T(8,128)(2,1)S(1)}, bf16[16,128,1024]{2,1,0:T(8,128)(2,1)S(1)}) custom-call(bf16[128,1024]{1,0:T(8,128)(2,1)S(1)} %bitcast.196, bf16[64,512]{1,0:T(8,128)(2,1)S(1)} %concatenate.47.p, bf16[64,1024]{1,0:T(8,128)(2,1)S(1)} %copy-done.7, ...), custom_call_target="tpu_custom_call" | custom-call | tf_op jit(solution)/shard_map/pallas_call | solution.py:200
  89.6 2.0 copy-done.8
  98.1 5.5 %fusion.101 = (f32[2,1024]{1,0:T(2,128)S(1)}, f32[2,1024,1024]{1,2,0:T(8,128)}) fusion(pred[1024,1024]{0,1:T(8,128)(4,1)S(1)} %broadcast_compare_fusion, bf16[1024,2,64]{0,2,1:T(8,128)(2,1)S(1)} %bitcast.230, bf16[1024,192]{0,1:T(8,128)(2,1)S(1)} %fusion.50), kind=kOutput, calls=%fused_computation.191 | convolution fusion | flops 276825088 | bytes 9838592 | tf_op jit(solution)/shard_map/sub | solution.py:457
  103.6 4.6 fusion.35
  108.5 30.6 %shard_map.230 = bf16[128,1024]{1,0:T(8,128)(2,1)S(1)} custom-call(bf16[1024,128]{1,0:T(8,128)(2,1)S(1)} %copy.145.x), custom_call_target="tpu_custom_call" | custom-call | tf_op jit(solution)/shard_map/pallas_call | solution.py:200
  142.6 35.0 %shard_map.231 = (bf16[16,128,1024]{2,1,0:T(8,128)(2,1)S(1)}, f32[16,32,128]{2,1,0:T(8,128)S(1)}) custom-call(bf16[128,1024]{1,0:T(8,128)(2,1)S(1)} %multiply_convert_fusion.2.x, f32[32,128]{1,0:T(8,128)S(1)} %fusion.73.g), custom_call_target="tpu_custom_call" | custom-call | tf_op jit(solution)/shard_map/pallas_call | solution.py:200
  177.7 2.0 copy-done.10
  184.4 15.7 %fusion.102 = f32[2048,2048]{0,1:T(8,128)} fusion(bf16[2048,1024]{1,0:T(8,128)(2,1)} %bitcast.207, bf16[1024,2048]{1,0:T(8,128)(2,1)} %all-gather.6.cloned.1.call-done), kind=kOutput, calls=%fused_computation.192 | convolution fusion | flops 8589934592 | bytes 25165824 | tf_op jit(solution)/shard_map/dot_general | solution.py:368
  200.0 2.5 broadcast_in_dim.102
  202.5 2.5 broadcast_in_dim.104
  205.0 22.7 %multiply_convert_fusion.1 = (bf16[2048,1024]{0,1:T(8,128)(2,1)}, bf16[2048,1024]{0,1:T(8,128)(2,1)}, bf16[2048,1024]{0,1:T(8,128)(2,1)}, f32[2048,1024]{0,1:T(8,128)}) fusion(f32[2048,2048]{0,1:T(8,128)} %fusion.102, f32[2048,512]{0,1:T(8,128)} %broadcast_in_dim.104, f32[2048,512]{0,1:T(8,128)} %broadcast_in_dim.102, bf16[2048,1024]{1,0:T(8,128)(2,1)} %bitcast.204, ...), kind=kOutput, calls=%fused_computation.14 | convolution fusion | flops 4336910336 | bytes 52428800 | tf_op jit(solution)/shard_map/dot_general | solution.py:368
  227.7 9.6 %bitcast_reduce_fusion = f32[2048,2]{0,1:T(2,128)S(1)} fusion(f32[2048,1024]{0,1:T(8,128)} %get-tuple-element.141, f32[2048,2048]{0,1:T(8,128)} %fusion.102), kind=kLoop, calls=%fused_computation.11 | loop fusion | flops 14675968 | bytes 25182208 | tf_op jit(solution)/shard_map/reduce_sum | solution.py:491
  237.3 11.8 %fusion.16 = bf16[2048,1024]{1,0:T(8,128)(2,1)S(1)} fusion(bf16[1024,2048]{1,0:T(8,128)(2,1)S(1)} %copy-done.46, bf16[2048,1024]{0,1:T(8,128)(2,1)} %get-tuple-element.93, bf16[2048,1024]{0,1:T(8,128)(2,1)} %get-tuple-element.92), kind=kOutput, calls=%fused_computation.30 | convolution fusion | flops 8608808960 | bytes 16777216 | tf_op jit(solution)/shard_map/dot_general | solution.py:368
  249.1 36.1 %shard_map.232 = (f32[128,1024]{1,0:T(8,128)S(1)}, f32[16,8,128]{2,1,0:T(8,128)S(1)}) custom-call(bf16[16,128,1024]{2,1,0:T(8,128)(2,1)S(1)} %bitcast.195, f32[16,8,128]{2,1,0:T(8,128)S(1)} %pad.4.g), custom_call_target="tpu_custom_call" | custom-call | tf_op jit(solution)/shard_map/pallas_call | solution.py:200
  285.3 2.3 fusion.27
  287.6 2.3 fusion.30
  294.5 7.1 %convolution_convert_fusion = bf16[2048,1024]{1,0:T(8,128)(2,1)S(1)} fusion(bf16[2048,1024]{0,1:T(8,128)(2,1)} %get-tuple-element.94, bf16[512,1024]{1,0:T(8,128)(2,1)} %copy-done.29, bf16[512,1024]{1,0:T(8,128)(2,1)S(1)} %get-tuple-element.95), kind=kOutput, calls=%fused_computation.32 | convolution fusion | flops 4301258752 | bytes 10485760 | tf_op jit(solution)/shard_map/dot_general | solution.py:368
  301.6 59.5 %shard_map.233 = (bf16[8,128,1024]{2,1,0:T(8,128)(2,1)S(1)}, f32[128,1024]{1,0:T(8,128)S(1)}) custom-call(bf16[128,1024]{1,0:T(8,128)(2,1)S(1)} %fusion.95.b, bf16[16,128,1024]{2,1,0:T(8,128)(2,1)S(1)} %bitcast.194), custom_call_target="tpu_custom_call" | custom-call | tf_op jit(solution)/shard_map/pallas_call | solution.py:200
  362.5 1.8 convolution_convert_fusion.3
  364.2 14.6 %fusion.17 = bf16[1024,2048]{1,0:T(8,128)(2,1)} fusion(bf16[2048,1024]{1,0:T(8,128)(2,1)} %bitcast.208, bf16[2048,1024]{0,1:T(8,128)(2,1)} %get-tuple-element.93, bf16[2048,1024]{0,1:T(8,128)(2,1)} %get-tuple-element.92), kind=kOutput, calls=%fused_computation.31 | convolution fusion | flops 8608808960 | bytes 16777216 | tf_op jit(solution)/shard_map/dot_general | solution.py:368
  379.5 5.1 %fusion.4 = (f32[2,1024]{1,0:T(2,128)S(1)}, f32[1024,1024,2]{1,0,2:T(8,128)S(1)}) fusion(f32[2,1024,1024]{1,2,0:T(8,128)} %get-tuple-element.136, f32[2,1024]{1,0:T(2,128)S(1)} %copy-done.40, bf16[1024,2,64]{0,2,1:T(8,128)(2,1)S(1)} %bitcast.232, f32[1024,448]{0,1:T(8,128)} %copy-done.23), kind=kOutput, calls=%fused_computation.8 | convolution fusion | flops 274724864 | bytes 17186816 | tf_op jit(solution)/shard_map/qhd,kd->hqk/dot_general | solution.py:523
  384.9 2.7 fusion.6
  387.7 2.0 copy-done.11
  389.6 1.7 convolution_multiply_fusion.1
  391.6 4.8 fusion.41
  398.4 3.8 fusion.34
  403.2 2.3 fusion.98
  405.4 2.3 concatenate.54
  412.1 2.6 concatenate.58.x
  414.7 58.1 %shard_map.234 = (bf16[128,2048]{1,0:T(8,128)(2,1)S(1)}, bf16[8,64,512]{2,1,0:T(8,128)(2,1)S(1)}, bf16[8,64,128]{2,1,0:T(8,128)(2,1)S(1)}) custom-call(bf16[1024,256]{1,0:T(8,128)(2,1)S(1)} %pad_maximum_fusion.14.g, bf16[16,64,512]{2,1,0:T(8,128)(2,1)S(1)} %concatenate.58.x), custom_call_target="tpu_custom_call" | custom-call | tf_op jit(solution)/shard_map/pallas_call | solution.py:200
  481.0 1.8 multiply_reduce_fusion.4
  483.9 3.8 fusion.51
  (202 shorter events, 53.9 us)
Async XLA Ops:
  7.2 7.0 %copy-start.41 = (bf16[64,32]{0,1:T(8,128)(2,1)S(1)}, bf16[64,32]{0,1:T(8,128)(2,1)}, u32[]{:S(2)}) copy-start(bf16[64,32]{0,1:T(8,128)(2,1)} %param.24) | copy-start | bytes 12292
  7.2 7.1 %copy-start.43 = (bf16[64]{0:T(256)(128)(2,1)S(1)}, bf16[64]{0:T(256)(128)(2,1)}, u32[]{:S(2)}) copy-start(bf16[64]{0:T(256)(128)(2,1)} %param.18) | copy-start | bytes 388
  7.2 7.2 %copy-start.44 = (bf16[64]{0:T(256)(128)(2,1)S(1)}, bf16[64]{0:T(256)(128)(2,1)}, u32[]{:S(2)}) copy-start(bf16[64]{0:T(256)(128)(2,1)} %param.23) | copy-start | bytes 388
  7.2 8.5 %copy-start = (bf16[1,128,1024]{2,1,0:T(8,128)(2,1)S(1)}, bf16[1,128,1024]{2,1,0:T(8,128)(2,1)}, u32[]{:S(2)}) copy-start(bf16[1,128,1024]{2,1,0:T(8,128)(2,1)} %param.14) | copy-start | bytes 786436
  7.2 8.5 %copy-start.4 = (bf16[1,128,1024]{2,1,0:T(8,128)(2,1)S(1)}, bf16[1,128,1024]{2,1,0:T(8,128)(2,1)}, u32[]{:S(2)}) copy-start(bf16[1,128,1024]{2,1,0:T(8,128)(2,1)} %param.15) | copy-start | bytes 786436
  7.3 8.5 %copy-start.7 = (bf16[64,1024]{1,0:T(8,128)(2,1)S(1)}, bf16[64,1024]{1,0:T(8,128)(2,1)}, u32[]{:S(2)}) copy-start(bf16[64,1024]{1,0:T(8,128)(2,1)} %w.1) | copy-start | bytes 393220
  7.3 175.3 %all-gather.4.cloned.1.call-start = ((), (), s32[]{:S(2)}) async-start(), calls=%async_computation.2 | async-start | bytes 2359296 | tf_op jit(solution)/shard_map/all_gather | solution.py:407
  9.1 175.2 %all-gather.6.cloned.1.call-start = ((), (), s32[]{:S(2)}) async-start(), calls=%async_computation.3 | async-start | bytes 4718592 | tf_op jit(solution)/shard_map/all_gather | solution.py:405
  11.2 472.7 %all-gather.8.cloned.1.call-start = ((), (), s32[]{:S(2)}) async-start(), calls=%async_computation.4 | async-start | bytes 4456448 | tf_op jit(solution)/shard_map/all_gather | solution.py:417
  13.4 475.6 %reduce-scatter.5.cloned.1.call-start = ((), (), s32[]{:S(2)}) async-start(), calls=%async_computation.6 | async-start | bytes 2359296 | tf_op jit(solution)/shard_map/reduce_scatter | solution.py:508
  97.1 6.5 %copy-start.22 = (bf16[1024,192]{0,1:T(8,128)(2,1)}, bf16[1024,192]{0,1:T(8,128)(2,1)S(1)}, u32[]{:S(2)}) copy-start(bf16[1024,192]{0,1:T(8,128)(2,1)S(1)} %fusion.50) | copy-start | bytes 1179652
  97.4 6.1 %copy-start.35 = (bf16[1024,128]{0,1:T(8,128)(2,1)}, bf16[1024,128]{0,1:T(8,128)(2,1)S(1)}, u32[]{:S(2)}) copy-start(bf16[1024,128]{0,1:T(8,128)(2,1)S(1)} %slice.206) | copy-start | bytes 786436
  103.6 35.5 %copy-start.3 = (bf16[16,64,1024]{2,1,0:T(8,128)(2,1)S(1)}, bf16[16,64,1024]{2,1,0:T(8,128)(2,1)}, u32[]{:S(2)}) copy-start(bf16[16,64,1024]{2,1,0:T(8,128)(2,1)} %copy-done.2) | copy-start | bytes 6291460
  108.3 30.8 %copy-start.25 = (bf16[64,2,1024]{2,0,1:T(8,128)(2,1)}, bf16[64,2,1024]{2,0,1:T(8,128)(2,1)S(1)}, u32[]{:S(2)}) copy-start(bf16[64,2,1024]{2,0,1:T(8,128)(2,1)S(1)} %fusion.35) | copy-start | bytes 786436
  108.3 32.8 %copy-start.42 = (s32[1,128,8]{1,2,0:T(8,128)S(1)}, s32[1,128,8]{1,2,0:T(8,128)}, u32[]{:S(2)}) copy-start(s32[1,128,8]{1,2,0:T(8,128)} %param.17) | copy-start | bytes 12292
  139.7 154.6 %copy-start.12 = (f32[128,1024]{1,0:T(8,128)}, f32[128,1024]{1,0:T(8,128)S(1)}, u32[]{:S(2)}) copy-start(f32[128,1024]{1,0:T(8,128)S(1)} %get-tuple-element.138) | copy-start | bytes 1572868
  184.3 20.6 %copy-start.29 = (bf16[512,1024]{1,0:T(8,128)(2,1)}, bf16[512,1024]{1,0:T(8,128)(2,1)S(1)}, u32[]{:S(2)}) copy-start(bf16[512,1024]{1,0:T(8,128)(2,1)S(1)} %get-tuple-element.96) | copy-start | bytes 3145732
  227.7 9.6 %copy-start.46 = (bf16[1024,2048]{1,0:T(8,128)(2,1)S(1)}, bf16[1024,2048]{1,0:T(8,128)(2,1)}, u32[]{:S(2)}) copy-start(bf16[1024,2048]{1,0:T(8,128)(2,1)} %all-gather.6.cloned.1.call-done) | copy-start | bytes 12582916
  237.3 47.9 %copy-start.47 = (bf16[2048,1024]{0,1:T(8,128)(2,1)S(1)}, bf16[2048,1024]{0,1:T(8,128)(2,1)}, u32[]{:S(2)}) copy-start(bf16[2048,1024]{0,1:T(8,128)(2,1)} %get-tuple-element.94) | copy-start | bytes 12582916
  249.1 36.1 %copy-start.9 = (bf16[16,128,1024]{2,1,0:T(8,128)(2,1)S(1)}, bf16[16,128,1024]{2,1,0:T(8,128)(2,1)}, u32[]{:S(2)}) copy-start(bf16[16,128,1024]{2,1,0:T(8,128)(2,1)} %copy-done.8) | copy-start | bytes 12582916
  291.5 199.3 %reduce-scatter.3.cloned.1.call-start = ((), (), s32[]{:S(2)}) async-start(), calls=%async_computation.5 | async-start | bytes 4718592 | tf_op jit(solution)/shard_map/reduce_scatter | solution.py:507
  294.3 7.3 %copy-start.14 = (f32[128,1024]{1,0:T(8,128)}, f32[128,1024]{1,0:T(8,128)S(1)}, u32[]{:S(2)}) copy-start(f32[128,1024]{1,0:T(8,128)S(1)} %get-tuple-element.142) | copy-start | bytes 1572868
  301.6 59.6 %copy-start.26 = (bf16[64,2,1024]{2,0,1:T(8,128)(2,1)S(1)}, bf16[64,2,1024]{2,0,1:T(8,128)(2,1)}, u32[]{:S(2)}) copy-start(bf16[64,2,1024]{2,0,1:T(8,128)(2,1)} %copy-done.25) | copy-start | bytes 786436
  391.6 6.8 %copy-start.36 = (bf16[1024,128]{0,1:T(8,128)(2,1)S(1)}, bf16[1024,128]{0,1:T(8,128)(2,1)}, u32[]{:S(2)}) copy-start(bf16[1024,128]{0,1:T(8,128)(2,1)} %copy-done.35) | copy-start | bytes 786436
  396.4 6.6 %copy-start.17 = (f32[1024,192]{1,0:T(8,128)S(1)}, f32[1024,192]{1,0:T(8,128)}, u32[]{:S(2)}) copy-start(f32[1024,192]{1,0:T(8,128)} %copy.154) | copy-start | bytes 2359300
  414.7 66.3 %copy-start.32 = (bf16[64,1024]{1,0:T(8,128)(2,1)S(1)}, bf16[64,1024]{1,0:T(8,128)(2,1)}, u32[]{:S(2)}) copy-start(bf16[64,1024]{1,0:T(8,128)(2,1)} %param.19) | copy-start | bytes 393220
  414.7 69.2 %copy-start.1 = (bf16[1,128,1024]{2,1,0:T(8,128)(2,1)S(1)}, bf16[1,128,1024]{2,1,0:T(8,128)(2,1)}, u32[]{:S(2)}) copy-start(bf16[1,128,1024]{2,1,0:T(8,128)(2,1)} %param.14) | copy-start | bytes 786436
  414.7 69.2 %copy-start.38 = (f32[1024,1]{0,1:T(1,128)S(1)}, f32[1024,1]{0,1:T(1,128)}, u32[]{:S(2)}) copy-start(f32[1024,1]{0,1:T(1,128)} %copy-done.37) | copy-start | bytes 12292
  475.5 13.4 %copy-start.30 = (f32[64,512]{1,0:T(8,128)}, f32[64,512]{1,0:T(8,128)S(1)}, u32[]{:S(2)}) copy-start(f32[64,512]{1,0:T(8,128)S(1)} %reshape.360) | copy-start | bytes 393220
  475.5 12.2 %copy-start.13 = (f32[128,1024]{1,0:T(8,128)S(1)}, f32[128,1024]{1,0:T(8,128)}, u32[]{:S(2)}) copy-start(f32[128,1024]{1,0:T(8,128)} %copy-done.12) | copy-start | bytes 1572868
  475.5 12.2 %copy-start.15 = (f32[128,1024]{1,0:T(8,128)S(1)}, f32[128,1024]{1,0:T(8,128)}, u32[]{:S(2)}) copy-start(f32[128,1024]{1,0:T(8,128)} %copy-done.14) | copy-start | bytes 1572868
  475.8 13.1 %copy-start.31 = (f32[64,512]{1,0:T(8,128)}, f32[64,512]{1,0:T(8,128)S(1)}, u32[]{:S(2)}) copy-start(f32[64,512]{1,0:T(8,128)S(1)} %reshape.359) | copy-start | bytes 393220
  (23 other events, 61.5 us)
Sparse Core Ops, SparseCore 0:
  10.3 84.2 all-gather.3
  96.8 52.5 all-gather.5
  152.4 64.1 all-gather.7
  291.7 78.2 reduce-scatter.4
  379.0 70.8 reduce-scatter.2

commit v2 on v1

--- a/solution.py
+++ b/solution.py
@@ -18,8 +18,8 @@
 ANY = pl.BlockSpec(memory_space=pl.ANY)
 VMEM = pl.BlockSpec(memory_space=pltpu.VMEM)
 DMA = pltpu.SemaphoreType.DMA
-NEAR_LAST = (6, 2, 4, 5, 3, 1, 7)
-NEAR_FIRST = (1, 7, 3, 5, 4, 2, 6)
+NEAR_LAST = (6, 5, 7, 2, 4, 1, 3)
+NEAR_FIRST = (1, 3, 2, 4, 5, 7, 6)
 CTX_ORDER = (2, 6, 4, 1, 3, 5, 7)
 
 
@@ -48,7 +48,10 @@
         return lax.rem(self.c + k, N_CTX)
 
     def chip_at(self, k):
-        return lax.rem(self.chip + k, 8)
+        return 4 * lax.rem(self.chip // 4 + k // 4, 2) + lax.rem(lax.rem(self.chip, 4) + lax.rem(k, 4), 4)
+
+    def chip_from(self, k):
+        return 4 * lax.rem(self.chip // 4 + k // 4, 2) + lax.rem(lax.rem(self.chip, 4) + 4 - lax.rem(k, 4), 4)
 
     def ctx_peers(self):
         return [{"ctx": self.ctx(k)} for k in range(1, N_CTX)]
@@ -109,7 +112,7 @@
         self.far, self.forward = {}, {}
         for k in NEAR_LAST:
             self.far[k] = remote(x, out.at[e], send.at[k], recv.at[k], here.same_core(k))
-            slot = 2 * here.chip_at(8 - k) + here.core
+            slot = 2 * here.chip_from(k) + here.core
             self.forward[k] = remote(out.at[slot], out.at[slot], fsend.at[k], frecv.at[k], here.partner)
 
     def start(self):
@@ -249,50 +252,219 @@
     return call(kernel, [shape((attn.shape[0] // 8, attn.shape[1] * 8), attn.dtype)], sem_shapes(Turn), 2, attn)[0]
 
 
-def routed_exchange(routed, gates):
-    def kernel(x, g, xs, gs, *sems):
+def experts(routed, gates, up_all, wgu, wd):
+    rows, width = routed.shape
+    both = 2 * rows
+    hid = wd.shape[0]
+    f = hid // 2
+    chunk = 256
+
+    def kernel(
+        x, g, up, wgu, wd, out_part, total, gback, dwgu, dwd,
+        xs, gs, parts, near, summed, far, hg, dgu, gparts,
+        xsend, xrecv, xfsend, xfrecv, gsend, grecv, gfsend, gfrecv,
+        nsend, nrecv, rsend, rrecv, psend, precv,
+    ):
         here = Here()
-        greet(here.exp_peers())
-        items = [PairGather(here, g, gs, *sems[4:8]), PairGather(here, x, xs, *sems[0:4])]
-        for i in items:
-            i.start()
-        for i in items:
-            i.pass_on()
-        for i in items:
-            i.wait()
-
-    return call(
+        core, e = here.core, here.e
+        greet(here.exp_peers() + here.other_core_peers())
+        own = [pltpu.make_async_copy(g, gs.at[e], gfsend.at[0]), pltpu.make_async_copy(x, xs.at[e], xfsend.at[0])]
+        first = [
+            remote(g, gs.at[e], gsend.at[0], grecv.at[0], here.partner),
+            remote(x, xs.at[e], xsend.at[0], xrecv.at[0], here.partner),
+        ]
+        for copy in own + first:
+            copy.start()
+
+        def away(k):
+            return [
+                remote(g, gs.at[e], gsend.at[k], grecv.at[k], here.same_core(k)),
+                remote(x, xs.at[e], xsend.at[k], xrecv.at[k], here.same_core(k)),
+            ]
+
+        def pass_on(k):
+            slot = 2 * here.chip_from(k) + core
+            return [
+                remote(gs.at[slot], gs.at[slot], gfsend.at[k], gfrecv.at[k], here.partner),
+                remote(xs.at[slot], xs.at[slot], xfsend.at[k], xfrecv.at[k], here.partner),
+            ]
+
+        def to_partner(k):
+            return remote(parts.at[k, 1 - core], near.at[k], nsend.at[k], nrecv.at[k], here.partner)
+
+        def to_chip(k):
+            where = {"exp": 2 * here.chip_from(k) + core}
+            return remote(summed.at[k], far.at[k], rsend.at[k], rrecv.at[k], where)
+
+        def gate_part(j):
+            return remote(gparts.at[j], gback.at[e], psend.at[j], precv.at[e], {"exp": j})
+
+        for k in range(1, 8):
+            for copy in away(k):
+                copy.start()
+
+        picks = lax.broadcasted_iota(jnp.int32, (32, 2 * 128), 0) == 2 * e + (
+            lax.broadcasted_iota(jnp.int32, (32, 2 * 128), 1) // 128
+        )
+        picks = picks.astype(f32)
+
+        def finish(k):
+            to_partner(k).wait_recv()
+            both_cores = parts[k, core].astype(f32) + near[k].astype(f32)
+
+            @pl.when(k == 0)
+            def _():
+                total[...] = both_cores
+
+            @pl.when(k > 0)
+            def _():
+                summed[k] = both_cores.astype(bf16)
+                to_chip(k).start()
+
+        def step(k, carry):
+            @pl.when(k < 7)
+            def _():
+                for copy in away(k + 1):
+                    copy.wait_recv()
+                for copy in pass_on(k + 1):
+                    copy.start()
+
+            @pl.when(k == 0)
+            def _():
+                for copy in own:
+                    copy.wait()
+                for copy in first:
+                    copy.wait_recv()
+
+            @pl.when(k > 0)
+            def _():
+                for copy in pass_on(k):
+                    copy.wait_recv()
+
+            chip = here.chip_from(k)
+            at = pl.ds(pl.multiple_of(chip * both, both), both)
+            xb = xs[pl.ds(2 * chip, 2)].reshape(both, width)
+            ub = up[at]
+            gate_cols = jnp.concatenate(
+                [
+                    lax.dot_general(
+                        gs[2 * chip + i], picks, (TN, ((), ())), precision=lax.Precision.HIGHEST,
+                        preferred_element_type=f32,
+                    )
+                    for i in range(2)
+                ],
+                axis=0,
+            )
+            gate_sums = jnp.zeros((8, both), f32)
+            for i in range(2):
+                gate = jnp.concatenate([gate_cols[:, 128 * i : 128 * (i + 1)]] * (chunk // 128), axis=1)
+                to_row = (lax.broadcasted_iota(jnp.int32, (8, chunk), 0) == i).astype(bf16)
+                for j in range(i * f, (i + 1) * f, chunk):
+                    cols, up_cols = pl.ds(j, chunk), pl.ds(hid + j, chunk)
+                    gate_h = dot(xb, wgu[:, cols])
+                    up_h = dot(xb, wgu[:, up_cols])
+                    back = dot(ub, wd[cols], NT)
+                    sig = 1.0 / (1.0 + jnp.exp(-gate_h))
+                    silu = gate_h * sig
+                    hidden = silu * up_h
+                    hg[at, cols] = (hidden * gate).astype(bf16)
+                    gate_sums += dot(to_row, (hidden * back).astype(bf16), NT)
+                    grad_hidden = back * gate
+                    dgu[at, cols] = (grad_hidden * up_h * (sig * (1.0 + gate_h * (1.0 - sig)))).astype(bf16)
+                    dgu[at, up_cols] = (grad_hidden * silu).astype(bf16)
+            for i in range(2):
+                gparts[2 * chip + i] = gate_sums[:, rows * i : rows * (i + 1)]
+            parts[k] = dot(dgu[at], wgu[...], NT).astype(bf16).reshape(2, rows, width)
+            to_partner(k).start()
+            gate_part(2 * chip + 1 - core).start()
+
+            @pl.when(k > 0)
+            def _():
+                gate_part(2 * chip + core).start()
+
+            out_part[pl.ds(2 * chip, 2)] = dot(hg[at], wd[...]).astype(bf16).reshape(2, rows, width)
+
+            @pl.when(k > 0)
+            def _():
+                finish(k - 1)
+
+            return carry
+
+        lax.fori_loop(0, 8, step, 0)
+        mine = pltpu.make_async_copy(gparts.at[e], gback.at[e], psend.at[e])
+        mine.start()
+        finish(jnp.int32(7))
+
+        def weight_rows(i, carry):
+            at = pl.ds(pl.multiple_of(i * 256, 256), 256)
+            columns = xs[:, :, at].reshape(16 * rows, 256)
+            dwgu[at] = dot(columns, dgu[...], TN).astype(bf16)
+            return carry
+
+        lax.fori_loop(0, width // 256, weight_rows, 0)
+
+        def down_rows(i, carry):
+            at = pl.ds(pl.multiple_of(i * 256, 256), 256)
+            grads = dot(hg[:, at], up[...], TN).astype(bf16)
+            down = pl.ds(pl.multiple_of(lax.rem(i, 2) * 256, 256), 256)
+            dwd[down, pl.ds(pl.multiple_of((i // 2) * width, width), width)] = grads
+            return carry
+
+        lax.fori_loop(0, hid // 256, down_rows, 0)
+
+        def collect(k, carry):
+            to_chip(k).wait_recv()
+            total[...] += far[k].astype(f32)
+            return carry
+
+        lax.fori_loop(1, 8, collect, 0)
+        for copy in first:
+            copy.wait_send()
+        mine.wait()
+
+        def drain(k, carry):
+            for copy in away(k) + pass_on(k) + [to_partner(k), to_chip(k)]:
+                copy.wait_send()
+            return carry
+
+        lax.fori_loop(1, 8, drain, 0)
+        to_partner(0).wait_send()
+
+        def drain_gates(k, carry):
+            j = lax.rem(e + k, N_EXP)
+            gate_part(j).wait_send()
+            remote(gparts.at[j], gback.at[j], psend.at[j], precv.at[j], {"exp": j}).wait_recv()
+            return carry
+
+        lax.fori_loop(1, N_EXP, drain_gates, 0)
+
+    block = (8, rows, width)
+    return pl.pallas_call(
         kernel,
-        [shape((16,) + a.shape, a.dtype) for a in (routed, gates)],
-        sem_shapes(PairGather, PairGather),
-        3,
-        routed,
-        gates,
-    )
-
-
-def grad_exchange(parts, gate_parts):
-    def kernel(x, g, total, gs, *rest):
-        here = Here()
-        greet(here.exp_peers() + here.other_core_peers())
-        sems = rest[4:]
-        small = Spread(here, g, gs, *sems[5:7])
-        s = PairScatter(here, x, total, *rest[:4], *sems[0:5])
-        s.start()
-        small.start()
-        s.pass_on()
-        s.wait()
-        small.wait()
-
-    return call(
-        kernel,
-        [shape(parts.shape[1:], f32), shape(gate_parts.shape, f32)],
-        PairScatter.scratch(parts) + sem_shapes(PairScatter, Spread),
-        4,
-        parts,
-        gate_parts,
-        out_specs=[VMEM, ANY],
-    )
+        out_shape=[
+            shape((16, rows, width), bf16),
+            shape((rows, width), f32),
+            shape((16, 8, rows), f32),
+            shape(wgu.shape, bf16),
+            shape((f, 2 * width), bf16),
+        ],
+        in_specs=[ANY, ANY, VMEM, VMEM, VMEM],
+        out_specs=[VMEM, VMEM, ANY, VMEM, VMEM],
+        scratch_shapes=[
+            pltpu.VMEM((16, rows, width), bf16),
+            pltpu.VMEM((16, 32, rows), f32),
+            pltpu.VMEM((8, 2, rows, width), bf16),
+            pltpu.VMEM(block, bf16),
+            pltpu.VMEM(block, bf16),
+            pltpu.VMEM(block, bf16),
+            pltpu.VMEM((16 * rows, hid), bf16),
+            pltpu.VMEM((16 * rows, 2 * hid), bf16),
+            pltpu.VMEM((16, 8, rows), f32),
+        ]
+        + [DMA((8,))] * 12
+        + [DMA((16,))] * 2,
+        compiler_params=pltpu.CompilerParams(collective_id=3, has_side_effects=True, vmem_limit_bytes=60 * 2**20),
+    )(routed, gates, up_all, wgu, wd)
 
 
 def branch_exchange(branch, out_parts):
@@ -471,39 +643,7 @@
     masked = jnp.where(chosen, logits, neg_big)
     lifted = jnp.where(chosen, jnp.exp(masked - jnp.max(masked, axis=-1, keepdims=True)), 0.0)
     gates = lifted / jnp.sum(lifted, axis=-1, keepdims=True)
-    routed_all, gates_all = routed_exchange(routed_in, gates.T)
-    e = lax.axis_index("exp")
-    routed_all = routed_all.reshape(N_EXP * rows, width)
-    own_gates = lax.dynamic_slice_in_dim(gates_all, e * 2, 2, axis=1)
-    own_gates = own_gates.transpose(0, 2, 1).reshape(N_EXP * rows, 2)
-    f = wd.shape[0] // 2
-    gate_col = jnp.concatenate(
-        [jnp.broadcast_to(own_gates[:, i : i + 1], (N_EXP * rows, f)) for i in range(2)], axis=1
-    )
-    lifted_h = dot(routed_all, wgu)
-    gate_h, up_h = lifted_h[:, : 2 * f], lifted_h[:, 2 * f :]
-    sig = jax.nn.sigmoid(gate_h)
-    silu = gate_h * sig
-    hidden = silu * up_h
-    hidden_gated = (hidden * gate_col).astype(bf16)
-    out_part = dot(hidden_gated, wd).astype(bf16)
-    back = dot(up_all, wd, NT)
-    gate_parts = jnp.sum((hidden * back).reshape(N_EXP * rows, 2, f), axis=2)
-    grad_hidden = back * gate_col
-    grad_lifted = jnp.concatenate(
-        [
-            (grad_hidden * up_h * (sig * (1.0 + gate_h * (1.0 - sig)))).astype(bf16),
-            (grad_hidden * silu).astype(bf16),
-        ],
-        axis=1,
-    )
-    in_part = dot(grad_lifted, wgu, NT).astype(bf16)
-    grad_wgu = dot(routed_all, grad_lifted, TN).astype(bf16)
-    grad_wd = jnp.concatenate(
-        [dot(hidden_gated[:, i * f : (i + 1) * f], up_all, TN) for i in range(2)], axis=1
-    ).astype(bf16)
-    gate_parts = jnp.pad(gate_parts.reshape(N_EXP, rows, 2).transpose(0, 2, 1), ((0, 0), (0, 6), (0, 0)))
-    grad_routed, gate_back = grad_exchange(in_part.reshape(N_EXP, rows, width), gate_parts)
+    out_part, grad_routed, gate_back, grad_wgu, grad_wd = experts(routed_in, gates.T, up_all, wgu, wd)
     wgu_share = lax.psum_scatter(grad_wgu, "ctx", scatter_dimension=0, tiled=True).astype(f32)
     wd_share = lax.psum_scatter(grad_wd, "ctx", scatter_dimension=0, tiled=True).astype(f32)
     grad_gates = gate_back[:, :2].reshape(32, rows).T
@@ -513,7 +653,7 @@
     grad_routed = grad_routed + dot(grad_logits, wr, NT)
     grad_gain_m = jnp.sum(grad_routed * x_mid * factor_two, axis=0)
     grad_mid = upstream + normalize_back(x_mid, factor_two, gain_m, grad_routed)
-    branch_all, moe_out = branch_exchange(grad_mid.astype(bf16), out_part.reshape(N_EXP, rows, width))
+    branch_all, moe_out = branch_exchange(grad_mid.astype(bf16), out_part)
     result = (x_mid + moe_out).astype(bf16)
     branch_all = branch_all.reshape(count, width)
     wo_rows = lax.dynamic_slice_in_dim(wo, c * 128, 128, axis=0)

time: 509 us -> 434 us (0.85); the launches traced: 501 us -> 433 us
  matrix products: 114 us -> 38.2 us
  Pallas kernels: 292 us -> 310 us
  other arithmetic: 38.5 us -> 29.4 us
    pallas_call x0 -> x1, Pallas kernels: none -> 90.4 us  [experts(): pl.pallas_call(kernel, out_shape=[shape((16, rows, width), bf16), shape((...]
    dot_general x16 -> x9, matrix products: 88.7 us -> 13.1 us  [dot(): return lax.dot_general(a, b, (dims, ((), ())), preferred_element_type=f32)]
    pallas_call x6 -> x4, Pallas kernels: 292 us -> 219 us  [call(): pl.pallas_call(kernel, out_shape=outs, in_specs=[ANY] * len(args), out_sp...]
    reduce_sum x1 -> x0, other arithmetic: 9.58 us -> none  [body(): gate_parts = jnp.sum((hidden * back).reshape(N_EXP * rows, 2, f), axis=2)]
    unnamed x106 -> x98, local copies, waits for them, and re-layouts: 15.8 us -> 16 us
  transfers between devices with their start and end apart: 5 -> 5, of which waited for: 0 -> 1; matrix products, arithmetic and copies ran while one was open for 35% -> 21% of each run, Pallas kernels for 58% -> 71%
where the time goes in v2:
time: 434 us; the launch traced here: 433 us
  Pallas kernels  310 us (71%)
  local copies, waits for them, and re-layouts  39.5 us (9%)
  matrix products  38.2 us (9%)
  other arithmetic  29.4 us (7%)
  between operations  14.7 us (3%)
    pallas_call x4, Pallas kernels, call(): pl.pallas_call(kernel, out_shape=outs, in_specs=[ANY] * len(args), out_sp...  219 us
    pallas_call x1, Pallas kernels, experts(): pl.pallas_call(kernel, out_shape=[shape((16, rows, width), bf16), shape((...  90.4 us
    unnamed x98, local copies, waits for them, and re-layouts  16 us
    dot_general x9, matrix products, dot(): return lax.dot_general(a, b, (dims, ((), ())), preferred_element_type=f32)  13.1 us
  transfers between devices with their start and end apart: 5, of which 1 were waited for; matrix products, arithmetic and copies ran while one was open for 21% of the time, Pallas kernels for 71%

profile of v2, /device:TPU:2, one launch (start us, length us, event | category | flops | bytes accessed | tf_op | source)
XLA Modules:
  0.0 433.4 jit_solution(3283860568363646179)
XLA Ops:
  15.7 72.8 %shard_map.229 = (bf16[8,128,1024]{2,1,0:T(8,128)(2,1)S(1)}, bf16[16,64,512]{2,1,0:T(8,128)(2,1)S(1)}, bf16[16,64,1024]{2,1,0:T(8,128)(2,1)S(1)}, bf16[16,128,1024]{2,1,0:T(8,128)(2,1)S(1)}) custom-call(bf16[128,1024]{1,0:T(8,128)(2,1)S(1)} %bitcast.173, bf16[64,512]{1,0:T(8,128)(2,1)S(1)} %concatenate.37.p, bf16[64,1024]{1,0:T(8,128)(2,1)S(1)} %copy-done.8, ...), custom_call_target="tpu_custom_call" | custom-call | tf_op jit(solution)/shard_map/pallas_call | solution.py:203
  88.5 2.0 copy-done
  90.5 1.3 copy-done.3
  98.8 5.4 %fusion.76 = (f32[2,1024]{1,0:T(2,128)S(1)}, f32[2,1024,1024]{1,2,0:T(8,128)}) fusion(pred[1024,1024]{0,1:T(8,128)(4,1)S(1)} %broadcast_compare_fusion, bf16[1024,2,64]{0,2,1:T(8,128)(2,1)S(1)} %bitcast.202, bf16[1024,192]{0,1:T(8,128)(2,1)S(1)} %fusion.30), kind=kOutput, calls=%fused_computation.160 | convolution fusion | flops 276825088 | bytes 9838592 | tf_op jit(solution)/shard_map/sub | solution.py:629
  104.3 4.5 %fusion.15 = bf16[64,2,1024]{2,0,1:T(8,128)(2,1)S(1)} fusion(f32[1024,448]{0,1:T(8,128)} %copy-done.22, f32[2,1024,1024]{1,2,0:T(8,128)} %get-tuple-element.133, f32[2,1024]{1,0:T(2,128)S(1)} %get-tuple-element.132), kind=kOutput, calls=%fused_computation.30 | convolution fusion | flops 272760832 | bytes 8790016 | tf_op jit(solution)/shard_map/hqk,kd->qhd/dot_general | solution.py:632
  109.0 30.8 %shard_map.230 = bf16[128,1024]{1,0:T(8,128)(2,1)S(1)} custom-call(bf16[1024,128]{1,0:T(8,128)(2,1)S(1)} %copy.141.x), custom_call_target="tpu_custom_call" | custom-call | tf_op jit(solution)/shard_map/pallas_call | solution.py:203
  141.8 1.5 fusion.56
  143.9 1.7 fusion.72
  145.7 1.5 pad_maximum_fusion.wd
  147.2 1.6 all-gather.4.cloned.1.call-done.wgu
  148.8 90.4 %shard_map.231 = (bf16[16,128,1024]{2,1,0:T(8,128)(2,1)}, f32[128,1024]{1,0:T(8,128)}, f32[16,8,128]{2,1,0:T(8,128)}, bf16[1024,2048]{1,0:T(8,128)(2,1)}, bf16[512,2048]{1,0:T(8,128)(2,1)}) custom-call(bf16[128,1024]{1,0:T(8,128)(2,1)} %copy-done.16, f32[32,128]{1,0:T(8,128)} %fusion.53.g, bf16[2048,1024]{1,0:T(8,128)(2,1)} %bitcast.172, ...), custom_call_target="tpu_custom_call" | custom-call | tf_op jit(solution)/shard_map/pallas_call | solution.py:442
  239.4 1.3 copy.149
  240.8 1.3 copy.148
  243.4 1.5 multiply_reduce_fusion.1
  245.7 2.2 copy-done.1
  247.9 52.8 %shard_map.232 = (bf16[8,128,1024]{2,1,0:T(8,128)(2,1)S(1)}, f32[128,1024]{1,0:T(8,128)S(1)}) custom-call(bf16[128,1024]{1,0:T(8,128)(2,1)S(1)} %fusion.71.b, bf16[16,128,1024]{2,1,0:T(8,128)(2,1)S(1)} %copy-done.1), custom_call_target="tpu_custom_call" | custom-call | tf_op jit(solution)/shard_map/pallas_call | solution.py:203
  301.9 1.8 reshape.333
  303.6 2.5 convolution_convert_fusion.2
  307.1 5.3 %fusion.1 = (f32[2,1024]{1,0:T(2,128)S(1)}, f32[1024,1024,2]{1,0,2:T(8,128)S(1)}) fusion(f32[2,1024,1024]{1,2,0:T(8,128)} %get-tuple-element.133, f32[2,1024]{1,0:T(2,128)S(1)} %copy-done.38, bf16[1024,2,64]{0,2,1:T(8,128)(2,1)S(1)} %bitcast.204, f32[1024,448]{0,1:T(8,128)} %copy-done.22), kind=kOutput, calls=%fused_computation.3 | convolution fusion | flops 274724864 | bytes 17186816 | tf_op jit(solution)/shard_map/qhd,kd->hqk/dot_general | solution.py:663
  312.5 2.4 fusion.3
  315.0 1.9 copy-done.9
  316.9 1.7 convolution_multiply_fusion.1
  318.8 4.8 %fusion.21 = bf16[1024,64]{0,1:T(8,128)(2,1)S(1)} fusion(bf16[1024,2,64]{0,2,1:T(8,128)(2,1)S(1)} %bitcast.205, f32[2,1024,1024]{1,2,0:T(8,128)} %get-tuple-element.133, f32[2,1024]{1,0:T(2,128)S(1)} %copy-done.38), kind=kOutput, calls=%fused_computation.34 | convolution fusion | flops 272695296 | bytes 8790016 | tf_op jit(solution)/shard_map/hqk,qhd->kd/dot_general | solution.py:669
  325.6 3.4 fusion.14
  329.2 2.3 fusion.74
  331.5 3.4 concatenate.42
  334.8 1.6 add_convert_fusion
  337.6 1.6 convolution_convert_fusion
  339.9 3.1 concatenate.46.x
  343.1 62.8 %shard_map.233 = (bf16[128,2048]{1,0:T(8,128)(2,1)S(1)}, bf16[8,64,512]{2,1,0:T(8,128)(2,1)S(1)}, bf16[8,64,128]{2,1,0:T(8,128)(2,1)S(1)}) custom-call(bf16[1024,256]{1,0:T(8,128)(2,1)S(1)} %pad_maximum_fusion.3.g, bf16[16,64,512]{2,1,0:T(8,128)(2,1)S(1)} %concatenate.46.x), custom_call_target="tpu_custom_call" | custom-call | tf_op jit(solution)/shard_map/pallas_call | solution.py:203
  414.0 1.8 multiply_reduce_fusion.4
  417.0 3.8 fusion.31
  (180 shorter events, 41.9 us)
Async XLA Ops:
  7.2 5.1 %copy-start.33 = (bf16[64,512]{1,0:T(8,128)(2,1)S(1)}, bf16[64,512]{1,0:T(8,128)(2,1)}, u32[]{:S(2)}) copy-start(bf16[64,512]{1,0:T(8,128)(2,1)} %param.21) | copy-start | bytes 196612
  7.2 6.2 %copy-start.39 = (bf16[64,32]{0,1:T(8,128)(2,1)S(1)}, bf16[64,32]{0,1:T(8,128)(2,1)}, u32[]{:S(2)}) copy-start(bf16[64,32]{0,1:T(8,128)(2,1)} %param.24) | copy-start | bytes 12292
  7.2 6.3 %copy-start.41 = (bf16[64]{0:T(256)(128)(2,1)S(1)}, bf16[64]{0:T(256)(128)(2,1)}, u32[]{:S(2)}) copy-start(bf16[64]{0:T(256)(128)(2,1)} %param.18) | copy-start | bytes 388
  7.2 6.4 %copy-start.42 = (bf16[64]{0:T(256)(128)(2,1)S(1)}, bf16[64]{0:T(256)(128)(2,1)}, u32[]{:S(2)}) copy-start(bf16[64]{0:T(256)(128)(2,1)} %param.23) | copy-start | bytes 388
  7.2 8.5 %copy-start.2 = (bf16[1,128,1024]{2,1,0:T(8,128)(2,1)S(1)}, bf16[1,128,1024]{2,1,0:T(8,128)(2,1)}, u32[]{:S(2)}) copy-start(bf16[1,128,1024]{2,1,0:T(8,128)(2,1)} %param.14) | copy-start | bytes 786436
  7.2 8.5 %copy-start.5 = (bf16[1,128,1024]{2,1,0:T(8,128)(2,1)S(1)}, bf16[1,128,1024]{2,1,0:T(8,128)(2,1)}, u32[]{:S(2)}) copy-start(bf16[1,128,1024]{2,1,0:T(8,128)(2,1)} %param.15) | copy-start | bytes 786436
  7.3 8.5 %copy-start.8 = (bf16[64,1024]{1,0:T(8,128)(2,1)S(1)}, bf16[64,1024]{1,0:T(8,128)(2,1)}, u32[]{:S(2)}) copy-start(bf16[64,1024]{1,0:T(8,128)(2,1)} %w.1) | copy-start | bytes 393220
  7.3 136.7 %all-gather.6.cloned.1.call-start = ((), (), s32[]{:S(2)}) async-start(), calls=%async_computation.3 | async-start | bytes 2359296 | tf_op jit(solution)/shard_map/all_gather | solution.py:579
  9.1 84.9 %copy-start.43 = (s32[16]{0:T(128)S(1)}, s32[16]{0:T(128)}, u32[]{:S(2)}) copy-start(s32[16]{0:T(128)} %param.16) | copy-start | bytes 196
  9.1 139.6 %all-gather.4.cloned.1.call-start = ((), (), s32[]{:S(2)}) async-start(), calls=%async_computation.2 | async-start | bytes 4718592 | tf_op jit(solution)/shard_map/all_gather | solution.py:577
  11.2 405.8 %all-gather.8.cloned.1.call-start = ((), (), s32[]{:S(2)}) async-start(), calls=%async_computation.4 | async-start | bytes 4456448 | tf_op jit(solution)/shard_map/all_gather | solution.py:589
  13.4 408.7 %reduce-scatter.5.cloned.1.call-start = ((), (), s32[]{:S(2)}) async-start(), calls=%async_computation.6 | async-start | bytes 2359296 | tf_op jit(solution)/shard_map/reduce_scatter | solution.py:648
  97.2 7.1 %copy-start.21 = (bf16[1024,192]{0,1:T(8,128)(2,1)}, bf16[1024,192]{0,1:T(8,128)(2,1)S(1)}, u32[]{:S(2)}) copy-start(bf16[1024,192]{0,1:T(8,128)(2,1)S(1)} %fusion.30) | copy-start | bytes 1179652
  97.2 7.1 %copy-start.35 = (bf16[1024,128]{0,1:T(8,128)(2,1)}, bf16[1024,128]{0,1:T(8,128)(2,1)S(1)}, u32[]{:S(2)}) copy-start(bf16[1024,128]{0,1:T(8,128)(2,1)S(1)} %slice.182) | copy-start | bytes 786436
  104.3 36.8 %copy-start.40 = (s32[1,128,8]{1,2,0:T(8,128)S(1)}, s32[1,128,8]{1,2,0:T(8,128)}, u32[]{:S(2)}) copy-start(s32[1,128,8]{1,2,0:T(8,128)} %param.17) | copy-start | bytes 12292
  104.3 36.8 %copy-start.4 = (bf16[16,64,1024]{2,1,0:T(8,128)(2,1)S(1)}, bf16[16,64,1024]{2,1,0:T(8,128)(2,1)}, u32[]{:S(2)}) copy-start(bf16[16,64,1024]{2,1,0:T(8,128)(2,1)} %copy-done.3) | copy-start | bytes 6291460
  108.8 32.3 %copy-start.25 = (bf16[64,2,1024]{2,0,1:T(8,128)(2,1)}, bf16[64,2,1024]{2,0,1:T(8,128)(2,1)S(1)}, u32[]{:S(2)}) copy-start(bf16[64,2,1024]{2,0,1:T(8,128)(2,1)S(1)} %fusion.15) | copy-start | bytes 786436
  141.7 103.2 %copy-start.10 = (f32[128,1024]{1,0:T(8,128)}, f32[128,1024]{1,0:T(8,128)S(1)}, u32[]{:S(2)}) copy-start(f32[128,1024]{1,0:T(8,128)S(1)} %get-tuple-element.135) | copy-start | bytes 1572868
  141.8 5.4 %copy-start.16 = (bf16[128,1024]{1,0:T(8,128)(2,1)}, bf16[128,1024]{1,0:T(8,128)(2,1)S(1)}, u32[]{:S(2)}) copy-start(bf16[128,1024]{1,0:T(8,128)(2,1)S(1)} %multiply_convert_fusion.x) | copy-start | bytes 786436
  148.8 90.5 %copy-start.24 = (f32[1024,32]{0,1:T(8,128)S(1)}, f32[1024,32]{0,1:T(8,128)}, u32[]{:S(2)}) copy-start(f32[1024,32]{0,1:T(8,128)} %copy-done.23) | copy-start | bytes 393220
  239.2 184.7 %reduce-scatter.3.cloned.1.call-start = ((), (), s32[]{:S(2)}) async-start(), calls=%async_computation.5 | async-start | bytes 4718592 | tf_op jit(solution)/shard_map/reduce_scatter | solution.py:647
  243.3 57.3 %copy-start.26 = (bf16[64,2,1024]{2,0,1:T(8,128)(2,1)S(1)}, bf16[64,2,1024]{2,0,1:T(8,128)(2,1)}, u32[]{:S(2)}) copy-start(bf16[64,2,1024]{2,0,1:T(8,128)(2,1)} %copy-done.25) | copy-start | bytes 786436
  301.1 5.0 %copy-start.38 = (f32[2,1024]{1,0:T(2,128)S(1)}, f32[2,1024]{1,0:T(2,128)}, u32[]{:S(2)}) copy-start(f32[2,1024]{1,0:T(2,128)} %copy-done.37) | copy-start | bytes 24580
  306.2 6.2 %slice-start = ((s8[8388608]{0:T(1024)(128)(4,1)}), s8[4194304]{0:T(1024)(128)(4,1)S(1)}, s32[]{:S(2)}) async-start(s8[8388608]{0:T(1024)(128)(4,1)} %bitcast.181), calls=%async_computation.7 | async-start | bytes 8388608
  307.1 5.4 %slice-start.1 = ((s8[8388608]{0:T(1024)(128)(4,1)}), s8[4194304]{0:T(1024)(128)(4,1)S(1)}, s32[]{:S(2)}) async-start(s8[8388608]{0:T(1024)(128)(4,1)} %bitcast.181), calls=%async_computation.8 | async-start | bytes 8388608
  323.6 5.4 %copy-start.15 = (f32[1024,192]{1,0:T(8,128)S(1)}, f32[1024,192]{1,0:T(8,128)}, u32[]{:S(2)}) copy-start(f32[1024,192]{1,0:T(8,128)} %copy.149) | copy-start | bytes 2359300
  329.2 5.6 %copy-start.14 = (f32[1024,192]{1,0:T(8,128)S(1)}, f32[1024,192]{1,0:T(8,128)}, u32[]{:S(2)}) copy-start(f32[1024,192]{1,0:T(8,128)} %copy.148) | copy-start | bytes 2359300
  343.1 70.9 %copy-start.31 = (bf16[64,1024]{1,0:T(8,128)(2,1)S(1)}, bf16[64,1024]{1,0:T(8,128)(2,1)}, u32[]{:S(2)}) copy-start(bf16[64,1024]{1,0:T(8,128)(2,1)} %param.19) | copy-start | bytes 393220
  408.6 13.4 %copy-start.29 = (f32[64,512]{1,0:T(8,128)}, f32[64,512]{1,0:T(8,128)S(1)}, u32[]{:S(2)}) copy-start(f32[64,512]{1,0:T(8,128)S(1)} %reshape.336) | copy-start | bytes 393220
  408.6 12.2 %copy-start.11 = (f32[128,1024]{1,0:T(8,128)S(1)}, f32[128,1024]{1,0:T(8,128)}, u32[]{:S(2)}) copy-start(f32[128,1024]{1,0:T(8,128)} %copy-done.10) | copy-start | bytes 1572868
  408.6 12.2 %copy-start.13 = (f32[128,1024]{1,0:T(8,128)S(1)}, f32[128,1024]{1,0:T(8,128)}, u32[]{:S(2)}) copy-start(f32[128,1024]{1,0:T(8,128)} %copy-done.12) | copy-start | bytes 1572868
  408.9 13.1 %copy-start.30 = (f32[64,512]{1,0:T(8,128)}, f32[64,512]{1,0:T(8,128)S(1)}, u32[]{:S(2)}) copy-start(f32[64,512]{1,0:T(8,128)S(1)} %reshape.335) | copy-start | bytes 393220
  (19 other events, 44.8 us)
Sparse Core Ops, SparseCore 0:
  10.3 83.0 all-gather.5
  95.6 53.1 all-gather.3
  151.8 93.4 all-gather.7
  247.5 69.4 reduce-scatter.4
  319.2 62.3 reduce-scatter.2

commit v3 on v2

v3 whole, which is shorter than its diff:
```python
import functools

import jax
import jax.numpy as jnp
from jax import lax
from jax.experimental import pallas as pl
from jax.experimental.pallas import tpu as pltpu
from jax.sharding import PartitionSpec as P

HEAD_SIZE = 64
HALF = 32
N_CTX = 8
N_EXP = 16
eps_norm = 1e-06
rope_base = 10000.0
neg_big = -1e30
f32, bf16 = jnp.float32, jnp.bfloat16

MESH = pl.DeviceIdType.MESH
ANY = pl.BlockSpec(memory_space=pl.ANY)
VMEM = pl.BlockSpec(memory_space=pltpu.VMEM)
DMA = pltpu.SemaphoreType.DMA
NEAR_LAST = (6, 5, 7, 2, 4, 1, 3)
NEAR_FIRST = (1, 3, 2, 4, 5, 7, 6)
CTX_ORDER = (2, 6, 4, 1, 3, 5, 7)


def remote(src, dst, send, recv, where):
    return pltpu.make_async_remote_copy(
        src_ref=src, dst_ref=dst, send_sem=send, recv_sem=recv, device_id=where, device_id_type=MESH
    )


def greet(places, amount=None):
    barrier = pltpu.get_barrier_semaphore()
    for where in places:
        pl.semaphore_signal(barrier, inc=1, device_id=where, device_id_type=MESH)
    pl.semaphore_wait(barrier, len(places) if amount is None else amount)


class Here:
    def __init__(self):
        self.c = lax.axis_index("ctx")
        self.e = lax.axis_index("exp")
        self.core = lax.rem(self.e, 2)
        self.chip = self.e // 2
        self.partner = {"exp": self.e + 1 - 2 * self.core}

    def ctx(self, k):
        return lax.rem(self.c + k, N_CTX)

    def chip_at(self, k):
        return 4 * lax.rem(self.chip // 4 + k // 4, 2) + lax.rem(lax.rem(self.chip, 4) + lax.rem(k, 4), 4)

    def chip_from(self, k):
        return 4 * lax.rem(self.chip // 4 + k // 4, 2) + lax.rem(lax.rem(self.chip, 4) + 4 - lax.rem(k, 4), 4)

    def ctx_peers(self):
        return [{"ctx": self.ctx(k)} for k in range(1, N_CTX)]

    def same_core(self, k):
        return {"exp": 2 * self.chip_at(k) + self.core}

    def exp_peers(self):
        return [self.partner] + [self.same_core(k) for k in range(1, 8)]

    def other_core_peers(self):
        return [{"exp": 2 * self.chip_at(k) + 1 - self.core} for k in range(1, 8)]


class Gather:
    sems = (8, 8)

    def __init__(self, here, x, out, send, recv):
        self.copies = [pltpu.make_async_copy(x, out.at[here.c], send.at[0])]
        for k in CTX_ORDER:
            self.copies.append(remote(x, out.at[here.c], send.at[k], recv.at[k], {"ctx": here.ctx(k)}))

    def start(self):
        for c in self.copies:
            c.start()

    def wait(self):
        for c in self.copies:
            c.wait()


class AxisGather:
    sems = (8, 8)

    def __init__(self, here, x, out, send, recv):
        c = here.c
        self.own = pltpu.make_async_copy(x, out.at[c], send.at[0])
        across = lax.rem(c + 4, 8)
        self.across = remote(x, out.at[c], send.at[4], recv.at[4], {"ctx": across})
        self.near, self.rest = [], []
        for k in (2, 1, 3):
            peer = {"ctx": c // 4 * 4 + lax.rem(lax.rem(c, 4) + k, 4)}
            self.near.append(remote(x, out.at[c], send.at[k], recv.at[k], peer))
            self.rest.append(remote(out.at[across], out.at[across], send.at[4 + k], recv.at[4 + k], peer))

    def start(self):
        self.across.start()
        for copy in self.near:
            copy.start()
        self.own.start()

    def cross(self):
        self.across.wait_recv()
        for copy in self.rest:
            copy.start()

    def wait(self):
        self.own.wait()
        self.across.wait_send()
        for copy in self.near + self.rest:
            copy.wait()


class Turn:
    sems = (8, 8)

    def __init__(self, here, x, out, send, recv):
        rows, cols = out.shape[0], x.shape[1]
        into = out.at[:, pl.ds(pl.multiple_of(here.c * cols, cols), cols)]

        def part(j):
            return x.at[pl.ds(pl.multiple_of(j * rows, rows), rows)]

        self.copies = [pltpu.make_async_copy(part(here.c), into, send.at[0])]
        for k in CTX_ORDER:
            j = here.ctx(k)
            self.copies.append(remote(part(j), into, send.at[k], recv.at[k], {"ctx": j}))

    start = Gather.start
    wait = Gather.wait


class Columns:
    sems = (8, 8)

    def __init__(self, here, x, out, send, recv):
        rows, cols = x.shape[0], out.shape[1]
        into = out.at[pl.ds(pl.multiple_of(here.c * rows, rows), rows)]

        def part(j):
            return x.at[:, pl.ds(pl.multiple_of(j * cols, cols), cols)]

        self.copies = [pltpu.make_async_copy(part(here.c), into, send.at[0])]
        for k in CTX_ORDER:
            j = here.ctx(k)
            self.copies.append(remote(part(j), into, send.at[k], recv.at[k], {"ctx": j}))

    start = Gather.start
    wait = Gather.wait


class PairGather:
    sems = (8, 8, 8, 8)

    def __init__(self, here, x, out, send, recv, fsend, frecv):
        e = here.e
        self.own = pltpu.make_async_copy(x, out.at[e], fsend.at[0])
        self.first = remote(x, out.at[e], send.at[0], recv.at[0], here.partner)
        self.far, self.forward = {}, {}
        across = out.at[2 * here.chip_at(4) + here.core]
        for k in range(1, 8):
            if k <= 4:
                self.far[k] = remote(x, out.at[e], send.at[k], recv.at[k], here.same_core(k))
            else:
                self.far[k] = remote(across, across, send.at[k], recv.at[k], here.same_core(k - 4))
            slot = 2 * here.chip_from(k) + here.core
            self.forward[k] = remote(out.at[slot], out.at[slot], fsend.at[k], frecv.at[k], here.partner)

    def start(self):
        for k in (4, 2, 1, 3):
            self.far[k].start()
        self.first.start()
        self.own.start()

    def cross(self):
        self.far[4].wait_recv()
        for k in (6, 5, 7):
            self.far[k].start()
        self.forward[4].start()

    def pass_on(self):
        for k in (1, 3, 2, 5, 7, 6):
            self.far[k].wait_recv()
            self.forward[k].start()

    def wait(self):
        self.own.wait()
        self.first.wait()
        for k in range(1, 8):
            self.far[k].wait_send()
            self.forward[k].wait()


class PairScatter:
    sems = (8, 8, 8, 8, 8)

    @staticmethod
    def scratch(x):
        return [pltpu.VMEM((8,) + x.shape[1:], x.dtype)] * 4

    def __init__(self, here, x, total, mine, near, summed, far, load, nsend, nrecv, fsend, frecv):
        self.total, self.mine, self.near, self.summed, self.far = total, mine, near, summed, far
        self.loads, self.nears, self.fars = {}, {}, {}
        self.order = (6, 2, 5, 1, 7, 3, 4, 0)
        for k in self.order:
            there = here.chip_at(k)
            self.nears[k] = remote(x.at[2 * there + 1 - here.core], near.at[k], nsend.at[k], nrecv.at[k], here.partner)
            self.loads[k] = pltpu.make_async_copy(x.at[2 * there + here.core], mine.at[k], load.at[k])
            if k:
                where = here.same_core(k if k <= 4 else k - 4)
                self.fars[k] = remote(summed.at[k], far.at[k], fsend.at[k], frecv.at[k], where)

    def start(self):
        for k in self.order:
            self.nears[k].start()
            self.loads[k].start()

    def pass_on(self):
        for k in self.order:
            self.loads[k].wait()
            self.nears[k].wait_recv()
            both = self.mine[k].astype(f32) + self.near[k].astype(f32)
            if k == 0:
                self.total[...] = both
            else:
                self.summed[k] = both.astype(self.summed.dtype)
                if k != 4:
                    self.fars[k].start()

    def cross(self):
        for k in (5, 7, 6):
            self.fars[k].wait_recv()
        both = self.summed[4].astype(f32) + self.far[5].astype(f32)
        both += self.far[6].astype(f32) + self.far[7].astype(f32)
        self.summed[4] = both.astype(self.summed.dtype)
        self.fars[4].start()

    def wait(self):
        for k in (1, 3, 2, 4):
            self.fars[k].wait_recv()
            self.total[...] += self.far[k].astype(f32)
        for k in self.order:
            self.nears[k].wait_send()
            if k:
                self.fars[k].wait_send()


class Spread:
    sems = (16, 16)

    def __init__(self, here, x, out, send, recv):
        self.copies = [pltpu.make_async_copy(x.at[here.e], out.at[here.e], send.at[0])]
        for k in range(1, N_EXP):
            j = lax.rem(here.e + k, N_EXP)
            self.copies.append(remote(x.at[j], out.at[here.e], send.at[k], recv.at[k], {"exp": j}))

    start = Gather.start
    wait = Gather.wait


def sem_shapes(*kinds):
    return [DMA((n,)) for kind in kinds for n in kind.sems]


def params(cid):
    return pltpu.CompilerParams(collective_id=cid, has_side_effects=True, vmem_limit_bytes=40 * 2**20)


def call(kernel, outs, scratch, cid, *args, out_specs=None):
    return pl.pallas_call(
        kernel,
        out_shape=outs,
        in_specs=[ANY] * len(args),
        out_specs=out_specs or [ANY] * len(outs),
        scratch_shapes=scratch,
        compiler_params=params(cid),
    )(*args)


def shape(s, t):
    return jax.ShapeDtypeStruct(s, t)


def start_exchange(over_ctx, *shards):
    n = len(shards)

    def kernel(*refs):
        here = Here()
        greet(here.exp_peers() + here.ctx_peers())
        ins, outs, sems = refs[: n + 1], refs[n + 1 : 2 * n + 2], refs[2 * n + 2 :]
        items = [PairGather(here, ins[i + 1], outs[i + 1], *sems[4 * i + 2 : 4 * i + 6]) for i in range(n)]
        rows = AxisGather(here, ins[0], outs[0], *sems[0:2])
        for i in items:
            i.start()
        rows.start()
        for i in items:
            i.cross()
        rows.cross()
        for i in items:
            i.pass_on()
        for i in items:
            i.wait()
        rows.wait()

    return call(
        kernel,
        [shape((8,) + over_ctx.shape, over_ctx.dtype)] + [shape((16,) + a.shape, a.dtype) for a in shards],
        sem_shapes(AxisGather, *[PairGather] * n),
        1,
        over_ctx,
        *shards,
    )


def dot(a, b, dims=((1,), (0,))):
    return lax.dot_general(a, b, (dims, ((), ())), preferred_element_type=f32)


NT = ((1,), (1,))
TN = ((0,), (0,))


def factor_of(values):
    return lax.rsqrt(jnp.mean(values * values, axis=-1, keepdims=True) + eps_norm)


def normalize_back(values, factor, gain, upstream):
    scaled = upstream * gain
    inner = jnp.mean(scaled * values, axis=-1, keepdims=True)
    return factor * scaled - values * factor * factor * factor * inner


def experts(routed, gates, up_all, wgu_all, wd_all):
    rows, width = routed.shape
    both = 2 * rows
    f = wd_all.shape[2] // 2 * 8 * wd_all.shape[1] // width
    hid = 2 * f
    wrows = rows + rows // 2
    chunk = 256

    def kernel(
        x, g, u, wg, wdown, out_part, total, gback, dwall,
        xs, gs, up, wgu, wd, usem, wsem, parts, near, summed, far, hg, dgu, gparts,
        xsend, xrecv, xfsend, xfrecv, gsend, grecv, gfsend, gfrecv,
        nsend, nrecv, rsend, rrecv, psend, precv,
    ):
        here = Here()
        core, e = here.core, here.e
        greet(here.exp_peers() + here.other_core_peers())
        own = [
            pltpu.make_async_copy(g, gs.at[e], gfsend.at[0]),
            pltpu.make_async_copy(x, xs.at[e], xfsend.at[0]),
            pltpu.make_async_copy(u, up, usem),
        ]
        own.append(pltpu.make_async_copy(wg, wgu, wsem.at[16]))
        for j in range(8):
            for i in range(2):
                own.append(
                    pltpu.make_async_copy(
                        wdown.at[j, :, pl.ds(width * i, width)],
                        wd.at[pl.ds(f * i + rows // 2 * j, rows // 2)],
                        wsem.at[2 * j + i],
                    )
                )
        first = [
            remote(g, gs.at[e], gsend.at[0], grecv.at[0], here.partner),
            remote(x, xs.at[e], xsend.at[0], xrecv.at[0], here.partner),
        ]
        for copy in own + first:
            copy.start()

        def away(k):
            return [
                remote(g, gs.at[e], gsend.at[k], grecv.at[k], here.same_core(k)),
                remote(x, xs.at[e], xsend.at[k], xrecv.at[k], here.same_core(k)),
            ]

        def pass_on(k):
            slot = 2 * here.chip_from(k) + core
            return [
                remote(gs.at[slot], gs.at[slot], gfsend.at[k], gfrecv.at[k], here.partner),
                remote(xs.at[slot], xs.at[slot], xfsend.at[k], xfrecv.at[k], here.partner),
            ]

        def to_partner(k):
            return remote(parts.at[k, 1 - core], near.at[k], nsend.at[k], nrecv.at[k], here.partner)

        def to_chip(k):
            where = {"exp": 2 * here.chip_from(k) + core}
            return remote(summed.at[k], far.at[k], rsend.at[k], rrecv.at[k], where)

        def gate_part(j):
            return remote(gparts.at[j], gback.at[e], psend.at[j], precv.at[e], {"exp": j})

        for k in range(1, 8):
            for copy in away(k):
                copy.start()

        picks = lax.broadcasted_iota(jnp.int32, (32, 2 * 128), 0) == 2 * e + (
            lax.broadcasted_iota(jnp.int32, (32, 2 * 128), 1) // 128
        )
        picks = picks.astype(f32)

        def finish(k):
            to_partner(k).wait_recv()
            both_cores = parts[k, core].astype(f32) + near[k].astype(f32)

            @pl.when(k == 0)
            def _():
                total[...] = both_cores

            @pl.when(k > 0)
            def _():
                summed[k] = both_cores.astype(bf16)
                to_chip(k).start()

        def step(k, carry):
            @pl.when(k < 7)
            def _():
                for copy in away(k + 1):
                    copy.wait_recv()
                for copy in pass_on(k + 1):
                    copy.start()

            @pl.when(k == 0)
            def _():
                for copy in own:
                    copy.wait()
                for copy in first:
                    copy.wait_recv()

            @pl.when(k > 0)
            def _():
                for copy in pass_on(k):
                    copy.wait_recv()

            chip = here.chip_from(k)
            at = pl.ds(pl.multiple_of(chip * both, both), both)
            xb = xs[pl.ds(2 * chip, 2)].reshape(both, width)
            ub = up[pl.ds(2 * chip, 2)].reshape(both, width)
            gate_cols = jnp.concatenate(
                [
                    lax.dot_general(
                        gs[2 * chip + i], picks, (TN, ((), ())), precision=lax.Precision.HIGHEST,
                        preferred_element_type=f32,
                    )
                    for i in range(2)
                ],
                axis=0,
            )
            gate_sums = jnp.zeros((8, both), f32)
            for i in range(2):
                gate = jnp.concatenate([gate_cols[:, 128 * i : 128 * (i + 1)]] * (chunk // 128), axis=1)
                to_row = (lax.broadcasted_iota(jnp.int32, (8, chunk), 0) == i).astype(bf16)
                for j in range(i * f, (i + 1) * f, chunk):
                    cols, up_cols = pl.ds(j, chunk), pl.ds(hid + j, chunk)
                    gate_h = dot(xb, wgu[:, cols])
                    up_h = dot(xb, wgu[:, up_cols])
                    back = dot(ub, wd[cols], NT)
                    sig = 1.0 / (1.0 + jnp.exp(-gate_h))
                    silu = gate_h * sig
                    hidden = silu * up_h
                    hg[at, cols] = (hidden * gate).astype(bf16)
                    gate_sums += dot(to_row, (hidden * back).astype(bf16), NT)
                    grad_hidden = back * gate
                    dgu[at, cols] = (grad_hidden * up_h * (sig * (1.0 + gate_h * (1.0 - sig)))).astype(bf16)
                    dgu[at, up_cols] = (grad_hidden * silu).astype(bf16)
            for i in range(2):
                gparts[2 * chip + i] = gate_sums[:, rows * i : rows * (i + 1)]
            parts[k] = dot(dgu[at], wgu[...], NT).astype(bf16).reshape(2, rows, width)
            to_partner(k).start()
            gate_part(2 * chip + 1 - core).start()

            @pl.when(k > 0)
            def _():
                gate_part(2 * chip + core).start()

            out_part[pl.ds(2 * chip, 2)] = dot(hg[at], wd[...]).astype(bf16).reshape(2, rows, width)

            @pl.when(k > 0)
            def _():
                finish(k - 1)

            return carry

        lax.fori_loop(0, 8, step, 0)
        mine = pltpu.make_async_copy(gparts.at[e], gback.at[e], psend.at[e])
        mine.start()
        finish(jnp.int32(7))

        def weight_rows(i, carry):
            at = pl.ds(pl.multiple_of(i * 256, 256), 256)
            columns = xs[:, :, at].reshape(16 * rows, 256)
            grads = dot(columns, dgu[...], TN).astype(bf16)
            dwall[pl.ds(2 * i, 2), pl.ds(0, rows)] = grads.reshape(2, rows, 2 * hid)
            return carry

        lax.fori_loop(0, width // 256, weight_rows, 0)

        def down_rows(i, carry):
            at = pl.ds(pl.multiple_of(i * 256, 256), 256)
            grads = dot(hg[:, at], up[...].reshape(16 * rows, width), TN).astype(bf16)
            cols = pl.ds(pl.multiple_of((i // 2) * width, width), width)
            dwall[pl.ds(4 * lax.rem(i, 2), 4), pl.ds(rows, rows // 2), cols] = grads.reshape(4, rows // 2, width)
            return carry

        lax.fori_loop(0, hid // 256, down_rows, 0)

        def collect(k, carry):
            to_chip(k).wait_recv()
            total[...] += far[k].astype(f32)
            return carry

        lax.fori_loop(1, 8, collect, 0)
        for copy in first:
            copy.wait_send()
        mine.wait()

        def drain(k, carry):
            for copy in away(k) + pass_on(k) + [to_partner(k), to_chip(k)]:
                copy.wait_send()
            return carry

        lax.fori_loop(1, 8, drain, 0)
        to_partner(0).wait_send()

        def drain_gates(k, carry):
            j = lax.rem(e + k, N_EXP)
            gate_part(j).wait_send()
            remote(gparts.at[j], gback.at[j], psend.at[j], precv.at[j], {"exp": j}).wait_recv()
            return carry

        lax.fori_loop(1, N_EXP, drain_gates, 0)

    block = (8, rows, width)
    return pl.pallas_call(
        kernel,
        out_shape=[
            shape((16, rows, width), bf16),
            shape((rows, width), f32),
            shape((16, 8, rows), f32),
            shape((8, wrows, 2 * hid), bf16),
        ],
        in_specs=[ANY] * 5,
        out_specs=[VMEM, VMEM, ANY, VMEM],
        scratch_shapes=[
            pltpu.VMEM((16, rows, width), bf16),
            pltpu.VMEM((16, 32, rows), f32),
            pltpu.VMEM((16, rows, width), bf16),
            pltpu.VMEM((width, 2 * hid), bf16),
            pltpu.VMEM((hid, width), bf16),
            DMA,
            DMA((17,)),
            pltpu.VMEM((8, 2, rows, width), bf16),
            pltpu.VMEM(block, bf16),
            pltpu.VMEM(block, bf16),
            pltpu.VMEM(block, bf16),
            pltpu.VMEM((16 * rows, hid), bf16),
            pltpu.VMEM((16 * rows, 2 * hid), bf16),
            pltpu.VMEM((16, 8, rows), f32),
        ]
        + [DMA((8,))] * 12
        + [DMA((16,))] * 2,
        compiler_params=pltpu.CompilerParams(collective_id=3, has_side_effects=True, vmem_limit_bytes=60 * 2**20),
    )(routed, gates, up_all, wgu_all, wd_all)


SCALE = HEAD_SIZE ** (-0.5)
QROWS = 256
SPAN = 64
SMEM = pl.BlockSpec(memory_space=pltpu.SMEM)


def left_lanes(shape_):
    return lax.broadcasted_iota(jnp.int32, shape_, 1) % 128 < HEAD_SIZE


def split_heads(kv):
    wide = kv.astype(f32)
    turned = pltpu.roll(wide, HEAD_SIZE, 1)
    left = left_lanes(kv.shape)
    return [
        jnp.where(left, wide, 0.0).astype(bf16),
        jnp.where(left, 0.0, turned).astype(bf16),
        jnp.where(left, turned, 0.0).astype(bf16),
        jnp.where(left, 0.0, wide).astype(bf16),
    ]


def place_column(spans, first, count):
    row = lax.broadcasted_iota(jnp.int32, (count, 1), 0)
    base = jnp.zeros((count, 1), jnp.int32)
    for i in range(count // SPAN):
        base = jnp.where(row // SPAN == i, spans[first + i], base)
    return base * SPAN + row % SPAN


def place_row(spans):
    lane = lax.broadcasted_iota(jnp.int32, (1, 16 * SPAN), 1)
    base = jnp.zeros((1, 16 * SPAN), jnp.int32)
    for i in range(16):
        base = jnp.where(lane // SPAN == i, spans[i], base)
    return base * SPAN + lane % SPAN


def tables(places, freqs):
    turned = places.astype(f32) * freqs
    return jnp.cos(turned), jnp.sin(turned)


def probs_of(q, k, visible):
    scores = jnp.where(visible, dot(q, k, NT) * SCALE, neg_big)
    shifted = jnp.exp(scores - jnp.max(scores, axis=-1, keepdims=True))
    return shifted * (1.0 / jnp.sum(shifted, axis=-1, keepdims=True))


def swap_of(v):
    leading = lax.broadcasted_iota(jnp.int32, v.shape, 1) % HEAD_SIZE < HALF
    return jnp.where(leading, -pltpu.roll(v, v.shape[1] - HALF, 1), pltpu.roll(v, HALF, 1))


def attend(h_one, wqkv, freqs, spans, cot, wd_own):
    rows = h_one.shape[0]
    count = N_CTX * rows

    def kernel(
        h, w, fr, so, u, wd, out, kept, us, wds, stage, seq, heads, attn, send, recv, osend, orecv, ksem, *sems
    ):
        here = Here()
        c = here.c
        greet(here.ctx_peers() + here.exp_peers())
        cots = PairGather(here, u, us, *sems[0:4])
        downs = AxisGather(here, wd, wds, *sems[4:6])
        cots.start()
        cos, sin = tables(place_column(so, 2 * c, rows), fr[...])

        def block_rows(ref, j):
            return ref.at[pl.ds(pl.multiple_of(j * rows, rows), rows)]

        def column(j):
            return out.at[:, pl.ds(pl.multiple_of(j * 128, 128), 128)]

        def arrive(j):
            return remote(stage.at[j], block_rows(seq, c), send.at[j], recv.at[c], {"ctx": j})

        def arrive_own():
            return pltpu.make_async_copy(stage.at[c], block_rows(seq, c), send.at[c])

        def project(b, carry):
            j = lax.rem(c + 1 + b, N_CTX)
            p = dot(h[...], w[:, pl.ds(pl.multiple_of(j * 256, 256), 256)])
            stage[j] = (p * cos + swap_of(p) * sin).astype(bf16)

            @pl.when(b < N_CTX - 1)
            def _():
                arrive(j).start()

            return carry

        lax.fori_loop(0, N_CTX, project, 0)
        arrive_own().start()
        downs.start()
        pr = place_row(so)
        arrive_own().wait()
        for k in range(1, N_CTX):
            j = here.ctx(k)
            arrive(j).wait_send()
            remote(stage.at[j], block_rows(seq, j), send.at[j], recv.at[j], {"ctx": j}).wait_recv()
        keep = pltpu.make_async_copy(seq, kept, ksem)
        keep.start()
        cots.cross()
        downs.cross()
        for i, part in enumerate(split_heads(seq[:, 128:])):
            heads[i] = part

        def leave(j):
            return remote(block_rows(attn, j), column(c), osend.at[j], orecv.at[c], {"ctx": j})

        def local():
            return pltpu.make_async_copy(block_rows(attn, c), column(c), osend.at[c])

        def step(b, carry):
            block = lax.rem(b + c // 2, count // QROWS)
            at = pl.ds(pl.multiple_of(block * QROWS, QROWS), QROWS)
            visible = pr <= place_column(so, block * (QROWS // SPAN), QROWS)
            q = seq[at, :128]
            total = jnp.zeros((QROWS, 128), f32)
            for i in range(2):
                total += dot(probs_of(q, heads[i], visible).astype(bf16), heads[2 + i])
            attn[at] = total.astype(bf16)
            for i in range(QROWS // rows):
                j = block * (QROWS // rows) + i

                @pl.when(j != c)
                def _():
                    leave(j).start()

                @pl.when(j == c)
                def _():
                    local().start()

            return carry

        lax.fori_loop(0, count // QROWS, step, 0)
        cots.pass_on()
        for k in range(1, N_CTX):
            j = here.ctx(k)
            leave(j).wait_send()
            remote(block_rows(attn, c), column(j), osend.at[j], orecv.at[j], {"ctx": j}).wait_recv()
        local().wait()
        keep.wait()
        cots.wait()
        downs.wait()

    return pl.pallas_call(
        kernel,
        out_shape=[
            shape((rows, N_CTX * 128), bf16),
            shape((count, 256), bf16),
            shape((16,) + cot.shape, bf16),
            shape((8,) + wd_own.shape, bf16),
        ],
        in_specs=[VMEM] * 3 + [SMEM] + [ANY] * 2,
        out_specs=[ANY] * 4,
        scratch_shapes=[
            pltpu.VMEM((N_CTX, rows, 256), bf16),
            pltpu.VMEM((count, 256), bf16),
            pltpu.VMEM((4, count, 128), bf16),
            pltpu.VMEM((count, 128), bf16),
        ]
        + [DMA((8,))] * 4
        + [DMA]
        + sem_shapes(PairGather, AxisGather),
        compiler_params=params(2),
    )(h_one, wqkv, freqs, spans, cot, wd_own)


def attend_back(
    grad_routed, gate_back, gates, routed, pack, x_mid, gain, cot, attn_low, wo_full, seq_qkv, freqs, spans, h_all, out_part
):
    rows, width = grad_routed.shape
    count = N_CTX * rows
    own = width // N_EXP
    scatters = [
        out_part,
        jax.ShapeDtypeStruct((16, own, width), bf16),
        jax.ShapeDtypeStruct((16, own, 384), bf16),
    ]

    def kernel(
        gr, gb, gt, ri, pk, xm, gn, u, al, wof, seq, fr, so, h, op, mid, back, moe, wos, alls,
        low_w, low, wo_total, total, payload, wp, ga, grads, heads, acc, dqkv, cos, sin, *rest,
    ):
        here = Here()
        greet(here.ctx_peers() + here.exp_peers())
        bufs, sems = rest[:12], rest[12:]
        arrive = Columns(here, ga, grads, *sems[0:2])
        outs = PairScatter(here, op, moe, *bufs[0:4], *sems[2:7])
        wo = PairScatter(here, wp, wo_total, *bufs[4:8], *sems[7:12])
        proj = PairScatter(here, payload, total, *bufs[8:12], *sems[12:17])
        turn = Turn(here, dqkv, back, *sems[17:19])
        wo_rows = Gather(here, low_w, wos, *sems[19:21])
        all_rows = Gather(here, low, alls, *sems[21:23])
        outs.start()
        spot = lax.broadcasted_iota(jnp.int32, (16 * 8, 128), 0)
        lane = lax.broadcasted_iota(jnp.int32, (16 * 8, 128), 1)
        picks = jnp.where(jnp.logical_and(spot % 8 < 2, spot // 8 * 2 + spot % 8 == lane), 1.0, 0.0)
        exact = functools.partial(
            lax.dot_general, dimension_numbers=(TN, ((), ())), precision=lax.Precision.HIGHEST, preferred_element_type=f32
        )
        grad_gates = exact(gb[...].reshape(16 * 8, rows), picks)
        weighted = gt[...] * grad_gates
        grad_logits = (weighted - gt[...] * jnp.sum(weighted, axis=-1, keepdims=True)).astype(bf16)
        routed_grad = gr[...] + dot(grad_logits, pk[...], NT)
        values = xm[...]
        factor = factor_of(values)
        grad_mid = u[...].astype(f32) + normalize_back(values, factor, gn[...], routed_grad)
        mid[...] = grad_mid
        branch = grad_mid.astype(bf16)
        ga[...] = dot(branch, wof[...], NT).astype(bf16)
        arrive.start()
        wp[...] = dot(al[...], branch, TN).astype(bf16).reshape(16, own, width)
        wo.start()
        column = (lax.broadcasted_iota(jnp.int32, (rows, 128), 1) == 32).astype(f32)
        small = dot(ri[...], grad_logits, TN) + exact(routed_grad * values * factor, column)
        payload[:, :, 256:] = small.astype(bf16).reshape(16, own, 128)
        pr = place_row(so)
        cos[...], sin[...] = tables(place_column(so, 0, count), fr[...])
        for i, part in enumerate(split_heads(seq[:, 128:])):
            heads[i] = part
        acc[...] = jnp.zeros_like(acc)
        arrive.wait()
        wo.pass_on()
        outs.pass_on()

        def step(b, carry):
            at = pl.ds(pl.multiple_of(b * QROWS, QROWS), QROWS)
            visible = pr <= place_column(so, b * (QROWS // SPAN), QROWS)
            q, g = seq[at, :128], grads[at]
            dq = jnp.zeros((QROWS, 128), f32)
            for i in range(2):
                probs = probs_of(q, heads[i], visible)
                grad_probs = dot(g, heads[2 + i], NT)
                inner = jnp.sum(probs * grad_probs, axis=-1, keepdims=True)
                grad_scores = (probs * (grad_probs - inner)).astype(bf16)
                dq += dot(grad_scores, heads[i])
                acc[i] += dot(grad_scores, q, TN)
                acc[2 + i] += dot(probs.astype(bf16), g, TN)
            dq = dq * SCALE
            dqkv[at, :128] = (dq * cos[at] - swap_of(dq * sin[at])).astype(bf16)
            return carry

        lax.fori_loop(0, count // QROWS, step, 0)
        left = left_lanes((count, 128))
        dk = (acc[0] + pltpu.roll(acc[1], HEAD_SIZE, 1)) * SCALE
        dv = pltpu.roll(acc[2], HEAD_SIZE, 1) + acc[3]
        dk = dk * cos[...] - swap_of(dk * sin[...])
        dqkv[:, 128:] = jnp.where(left, dk, dv).astype(bf16)
        turn.start()
        wo.cross()
        outs.cross()
        payload[:, :, :256] = dot(h[...], dqkv[...], TN).astype(bf16).reshape(16, own, 256)
        proj.start()
        wo.wait()
        low_w[...] = wo_total[...].astype(bf16)
        wo_rows.start()
        proj.pass_on()
        proj.cross()
        proj.wait()
        low[...] = total[...].astype(bf16)
        all_rows.start()
        outs.wait()
        turn.wait()
        wo_rows.wait()
        all_rows.wait()

    return pl.pallas_call(
        kernel,
        out_shape=[
            shape((rows, width), f32),
            shape((rows, N_CTX * 256), bf16),
            shape((rows, width), f32),
            shape((8, own, width), bf16),
            shape((8, own, 384), bf16),
        ],
        in_specs=[VMEM] * 12 + [SMEM, VMEM, ANY],
        out_specs=[VMEM, ANY, VMEM, ANY, ANY],
        scratch_shapes=[
            pltpu.VMEM((own, width), bf16),
            pltpu.VMEM((own, 384), bf16),
            pltpu.VMEM((own, width), f32),
            pltpu.VMEM((own, 384), f32),
            pltpu.VMEM((16, own, 384), bf16),
            pltpu.VMEM((16, own, width), bf16),
            pltpu.VMEM((rows, width), bf16),
            pltpu.VMEM((count, 128), bf16),
            pltpu.VMEM((4, count, 128), bf16),
            pltpu.VMEM((4, count, 128), f32),
            pltpu.VMEM((count, 256), bf16),
            pltpu.VMEM((count, 128), f32),
            pltpu.VMEM((count, 128), f32),
        ]
        + [b for x in scatters for b in PairScatter.scratch(x)]
        + sem_shapes(Columns, PairScatter, PairScatter, PairScatter, Turn, Gather, Gather),
        compiler_params=pltpu.CompilerParams(collective_id=4, has_side_effects=True, vmem_limit_bytes=54 * 2**20),
    )(
        grad_routed, gate_back, gates, routed, pack, x_mid, gain, cot, attn_low, wo_full, seq_qkv, freqs, spans, h_all,
        out_part,
    )


def finish_tokens(
    back, wqkv, tokens, gain, grad_mid, x_mid, moe_out, owned, wo_sums, w_query, key_matrix, value_matrix, norm_attn
):
    rows, width = tokens.shape
    own = w_query.shape[0]

    def kernel(
        back, wqkv, x, gain, mid, xm, moe, owned, wos, wq, wk, wv, norm,
        result, grad, gq, gk, gv, go, tail, ga,
    ):
        result[...] = (xm[...] + moe[...]).astype(bf16)
        values = x[...].astype(f32)
        factor = factor_of(values)
        grad[...] = mid[...] + normalize_back(values, factor, gain[...], dot(back[...], wqkv[...], NT))
        left = left_lanes((own, 128))
        rest = jnp.zeros((own, 128), f32)
        sums = jnp.zeros((own, 128), f32)
        for i in range(N_CTX):
            block = owned[i, :, :128].astype(f32)
            at = slice(128 * i, 128 * (i + 1))
            gq[:, at] = block
            sums += block * wq[:, at].astype(f32)
            rest += owned[i, :, 256:].astype(f32)
        for i in range(N_CTX // 2):
            one, two = owned[2 * i, :, 128:256].astype(f32), owned[2 * i + 1, :, 128:256].astype(f32)
            at = slice(128 * i, 128 * (i + 1))
            keys = jnp.where(left, one, pltpu.roll(two, HEAD_SIZE, 1))
            vals = jnp.where(left, pltpu.roll(one, HEAD_SIZE, 1), two)
            gk[:, at] = keys
            gv[:, at] = vals
            sums += keys * wk[:, at].astype(f32) + vals * wv[:, at].astype(f32)
        tail[...] = rest
        ga[...] = jnp.broadcast_to(jnp.sum(sums, axis=1, keepdims=True) / norm[...].astype(f32), (own, 128))
        total = wos[0].astype(f32)
        for i in range(1, N_CTX):
            total += wos[i].astype(f32)
        go[...] = total

    args = (
        back, wqkv, tokens, gain, grad_mid, x_mid, moe_out, owned, wo_sums, w_query, key_matrix, value_matrix,
        norm_attn[:, None],
    )
    return pl.pallas_call(
        kernel,
        out_shape=[
            shape((rows, width), bf16),
            shape((rows, width), f32),
            shape((own, width), f32),
            shape((own, width // 2), f32),
            shape((own, width // 2), f32),
            shape((own, width), f32),
            shape((own, 128), f32),
            shape((own, 128), f32),
        ],
        in_specs=[VMEM] * len(args),
        out_specs=[VMEM] * 8,
        compiler_params=pltpu.CompilerParams(vmem_limit_bytes=40 * 2**20),
    )(*args)


def finish_experts(shares):
    rows = shares.shape[0] * 2 // 3
    f = shares.shape[1] // 4

    def kernel(x, gg, gu, gd):
        for i in range(2):
            gg[i] = x[:rows, f * i : f * (i + 1)].astype(f32)
            gu[i] = x[:rows, f * (2 + i) : f * (3 + i)].astype(f32)
            gd[i] = x[rows:, 2 * f * i : 2 * f * (i + 1)].astype(f32)

    return pl.pallas_call(
        kernel,
        out_shape=[shape((2, rows, f), f32), shape((2, rows, f), f32), shape((2, rows // 2, 2 * f), f32)],
        in_specs=[VMEM],
        out_specs=[VMEM] * 3,
        compiler_params=pltpu.CompilerParams(vmem_limit_bytes=20 * 2**20),
    )(shares)


def body(
    tokens, cotangent, span_order, expert_choice, norm_attn, w_query, key_matrix, value_matrix,
    w_out, norm_moe, w_router, w_gate, w_up, w_down,
):
    c = lax.axis_index("ctx")
    tokens, cotangent, choice = tokens[0], cotangent[0], expert_choice[0]
    rows, width = tokens.shape
    own_rows = w_query.shape[0]
    wgu_own = jnp.concatenate([w_gate[0], w_gate[1], w_up[0], w_up[1]], axis=1)
    wd_own = jnp.concatenate([w_down[0], w_down[1]], axis=1)
    wqkv_own = jnp.concatenate(
        [
            w_query.reshape(own_rows, N_CTX, 128),
            key_matrix.reshape(own_rows, N_CTX, 64),
            value_matrix.reshape(own_rows, N_CTX, 64),
        ],
        axis=2,
    ).reshape(own_rows, N_CTX * 256)
    pack = jnp.pad(w_router, ((0, 0), (0, 128 - 32)))
    gains = jnp.stack([norm_attn, norm_moe])
    odd = lax.axis_index("exp") % 2
    gains = jnp.concatenate([jnp.where(odd == 0, gains, 0.0), jnp.where(odd == 1, gains, 0.0)], axis=1)
    gains = jnp.pad(gains, ((0, 14), (0, 0)))
    wgu_all, wqkv, pack_all, gains, wo = start_exchange(wgu_own, wqkv_own, pack, gains, w_out)
    wgu_all = wgu_all.reshape(width, 4 * w_gate.shape[2])
    wqkv = wqkv.reshape(width, N_CTX * 256)
    pack_all = pack_all.reshape(width, 128)
    wo = wo.reshape(width, width)
    gains = jnp.sum(gains[:, :2].astype(f32).reshape(8, 2, 2, 128), axis=1).transpose(1, 0, 2).reshape(2, width)
    gain_a, gain_m = gains[0:1], gains[1:2]
    lanes = jnp.arange(256, dtype=jnp.int32)
    freqs = rope_base ** (-((lanes % HALF).astype(f32) * 2.0 / HEAD_SIZE))
    freqs = jnp.where(lanes < 192, freqs, 0.0)[None, :]
    inputs = tokens.astype(f32)
    h_one = (inputs * factor_of(inputs) * gain_a).astype(bf16)
    attn_low, seq_qkv, up_all, wd_all = attend(h_one, wqkv, freqs, span_order, cotangent, wd_own)
    x_mid = inputs + dot(attn_low, wo)
    routed_in = (x_mid * factor_of(x_mid) * gain_m).astype(bf16)
    logits = dot(routed_in, pack_all)
    expert_ids = jnp.arange(128, dtype=jnp.int32)
    chosen = jnp.any(choice[:, :, None] == expert_ids[None, None, :], axis=1)
    masked = jnp.where(chosen, logits, neg_big)
    lifted = jnp.where(chosen, jnp.exp(masked - jnp.max(masked, axis=-1, keepdims=True)), 0.0)
    gates = lifted / jnp.sum(lifted, axis=-1, keepdims=True)
    out_part, grad_routed, gate_back, grad_weights = experts(routed_in, gates[:, :32].T, up_all, wgu_all, wd_all)
    h_late, _ = lax.optimization_barrier((h_one, attn_low))
    h_all = lax.all_gather(h_late, "ctx", axis=0, tiled=True)
    shares = lax.psum_scatter(grad_weights, "ctx", scatter_dimension=0, tiled=True)[0]
    grad_mid, back, moe_out, wo_sums, owned = attend_back(
        grad_routed, gate_back, gates, routed_in, pack_all, x_mid, gain_m, cotangent, attn_low, wo, seq_qkv,
        freqs[:, :128], span_order, h_all, out_part,
    )
    result, grad_tokens, out_wq, out_wk, out_wv, out_wo, tail, out_gain_a = finish_tokens(
        back, wqkv, tokens, gain_a, grad_mid, x_mid, moe_out, owned, wo_sums, w_query, key_matrix, value_matrix, norm_attn
    )
    out_wg, out_wu, out_wd = finish_experts(shares)
    return (
        result[None],
        grad_tokens[None],
        out_gain_a[:, 0],
        out_wq,
        out_wk,
        out_wv,
        out_wo,
        tail[:, 32],
        tail[:, :32],
        out_wg,
        out_wu,
        out_wd,
    )


def solution(mesh):
    return jax.shard_map(
        body,
        mesh=mesh,
        in_specs=(
            P("exp", "ctx", None),
            P("exp", "ctx", None),
            P(),
            P("exp", "ctx", None),
            P("exp"),
            P("exp", None),
            P("exp", None),
            P("exp", None),
            P("exp", None),
            P("exp"),
            P("exp", None),
            P("exp", "ctx", None),
            P("exp", "ctx", None),
            P("exp", "ctx", None),
        ),
        out_specs=(
            P("exp", "ctx", None),
            P("exp", "ctx", None),
            P("exp"),
            P("exp", None),
            P("exp", None),
            P("exp", None),
            P("exp", None),
            P("exp"),
            P("exp", None),
            P("exp", "ctx", None),
            P("exp", "ctx", None),
            P("exp", "ctx", None),
        ),
        check_vma=False,
    )
```

time: 434 us -> 349 us (0.80)
  matrix products: 38.2 us -> 0.83 us
  other arithmetic: 29.4 us -> 1.25 us
  local copies, waits for them, and re-layouts: 39.5 us -> 27.6 us
  Pallas kernels: 310 us -> 304 us
    pallas_call x0 -> x4, Pallas kernels: none -> 172 us  [the longest x1 128 us: attend_back(): pl.pallas_call(kernel, out_shape=[shape((rows, width), f32), shape((rows,...]
    pallas_call x4 -> x1, Pallas kernels: 219 us -> 55.2 us  [call(): pl.pallas_call(kernel, out_shape=outs, in_specs=[ANY] * len(args), out_sp...]
    dot_general x5 -> x0, matrix products: 19.7 us -> none  [the longest x1 5.26 us: body(): jnp.einsum('qhd,kd->hqk', heads_grad, v, preferred_element_type=f32)]
    pallas_call x1, Pallas kernels: 90.4 us -> 76.9 us  [experts(): pl.pallas_call(kernel, out_shape=[shape((16, rows, width), bf16), shape((...]
    dot_general x9 -> x2, matrix products: 13.1 us -> 0.83 us  [dot(): return lax.dot_general(a, b, (dims, ((), ())), preferred_element_type=f32)]
    concatenate x4 -> x0, local copies, waits for them, and re-layouts: 7.76 us -> none  [the longest x1 3.35 us: swap_halves(): return jnp.concatenate(parts, axis=1)]
    convert_element_type x10 -> x2, other arithmetic: 7.88 us -> 0.24 us  [the longest x1 0.13 us: body(): h_one = (inputs * factor_of(inputs) * gain_a).astype(bf16)]
    sub x1 -> x0, matrix products: 5.44 us -> none  [body(): shifted = jnp.exp(scores - largest)]
  transfers between devices with their start and end apart: 5 -> 2, of which waited for: 1 -> 0; matrix products, arithmetic and copies ran while one was open for 21% -> 1% of each run, Pallas kernels for 71% -> 60%
where the time goes in v3:
time: 349 us; the launch traced here: 348 us
  Pallas kernels  304 us (87%)
  local copies, waits for them, and re-layouts  27.6 us (8%)
  between operations  14.5 us (4%)
    pallas_call x1, Pallas kernels, attend_back(): pl.pallas_call(kernel, out_shape=[shape((rows, width), f32), shape((rows,...  128 us
    pallas_call x1, Pallas kernels, experts(): pl.pallas_call(kernel, out_shape=[shape((16, rows, width), bf16), shape((...  76.9 us
    pallas_call x1, Pallas kernels, call(): pl.pallas_call(kernel, out_shape=outs, in_specs=[ANY] * len(args), out_sp...  55.2 us
    pallas_call x1, Pallas kernels, attend(): pl.pallas_call(kernel, out_shape=[shape((rows, N_CTX * 128), bf16), shape...  39.5 us
    unnamed x68, local copies, waits for them, and re-layouts  20.1 us
  transfers between devices with their start and end apart: 2, of which 0 were waited for; matrix products, arithmetic and copies ran while one was open for 1% of the time, Pallas kernels for 60%

profile of v3, /device:TPU:2, one launch (start us, length us, event | category | flops | bytes accessed | tf_op | source)
XLA Modules:
  0.0 348.4 jit_solution(1037379717999781848)
XLA Ops:
  7.3 1.0 reshape.123
  8.3 1.0 reshape.122
  9.3 0.9 copy.51
  10.4 0.8 copy.44
  11.2 1.1 slice_bitcast_fusion.3
  12.5 55.2 %shard_map.229 = (bf16[8,128,2048]{2,1,0:T(8,128)(2,1)S(1)}, bf16[16,64,2048]{2,1,0:T(8,128)(2,1)S(1)}, bf16[16,64,128]{2,1,0:T(8,128)(2,1)S(1)}, bf16[16,16,128...) custom-call(bf16[128,2048]{1,0:T(8,128)(2,1)S(1)} %pad_maximum_fusion.refs_0_, bf16[64,2048]{1,0:T(8,128)(2,1)S(1)} %bitcast.59, ...), custom_call_target="tpu_custom_call" | custom-call | tf_op jit(solution)/shard_map/pallas_call | solution.py:276
  67.7 2.1 copy-done
  69.8 2.0 copy-done.6
  71.7 0.7 copy-done.13
  72.4 0.7 slice_bitcast_fusion.8
  73.2 1.0 slice_bitcast_fusion.1
  74.4 2.2 copy-done.1
  76.7 39.5 %shard_map.230 = (bf16[128,1024]{1,0:T(8,128)(2,1)S(1)}, bf16[1024,256]{1,0:T(8,128)(2,1)S(1)}, bf16[16,128,1024]{2,1,0:T(8,128)(2,1)S(1)}, bf16[8,64,2048]{2,1,0:T(8,128)(2,1)S(1)}) custom-call(bf16[128,1024]{1,0:T(8,128)(2,1)S(1)} %fusion.2.h, bf16[1024,2048]{1,0:T(8,128)(2,1)S(1)} %bitcast.49, f32[1,256]{1,0:T(1,128)S(1)} %compare_select_fusion.fr, ...), custom_call_target="tpu_custom_call" | custom-call | tf_op jit(solution)/shard_map/pallas_call | solution.py:721
  116.2 2.0 copy-done.7
  118.2 1.3 copy-done.10
  119.5 0.8 copy-done.21
  121.0 0.5 multiply_reduce_fusion
  122.3 0.7 copy.47.g
  123.0 76.9 %shard_map.231 = (bf16[16,128,1024]{2,1,0:T(8,128)(2,1)}, f32[128,1024]{1,0:T(8,128)}, f32[16,8,128]{2,1,0:T(8,128)}, bf16[8,192,2048]{2,1,0:T(8,128)(2,1)}) custom-call(bf16[128,1024]{1,0:T(8,128)(2,1)} %copy-done.27, f32[32,128]{1,0:T(8,128)} %copy.47.g, bf16[16,128,1024]{2,1,0:T(8,128)(2,1)} %copy-done.7, bf16[1024,2048]{1,0:T(8,128)(2,1)} %bitcast.53, ...), custom_call_target="tpu_custom_call" | custom-call | tf_op jit(solution)/shard_map/pallas_call | solution.py:542
  200.0 0.5 slice.67.fr
  200.7 128.3 %shard_map.232 = (f32[128,1024]{1,0:T(8,128)}, bf16[128,2048]{1,0:T(8,128)(2,1)}, f32[128,1024]{1,0:T(8,128)}, bf16[8,64,1024]{2,1,0:T(8,128)(2,1)}, bf16[8,64,384]{2,1,0:T(8,128)(2,1)}) custom-call(f32[128,1024]{1,0:T(8,128)} %get-tuple-element.50.gr, f32[16,8,128]{2,1,0:T(8,128)} %get-tuple-element.51.gb, f32[128,128]{1,0:T(8,128)} %copy-done.28, ...), custom_call_target="tpu_custom_call" | custom-call | tf_op jit(solution)/shard_map/pallas_call | solution.py:843
  329.1 1.2 copy-done.11
  330.3 1.0 copy-done.18
  331.3 1.0 copy-done.19
  332.4 1.0 copy-done.20
  333.4 1.0 copy-done.22
  334.4 2.8 shard_map.233
  337.2 0.7 copy.49
  337.9 0.7 slice_reduce_fusion
  338.6 0.6 slice_reduce_fusion.1
  339.2 1.1 copy-done.16
  340.3 1.2 shard_map.234
  (78 shorter events, 2.3 us)
Async XLA Ops:
  7.2 5.2 %copy-start.31 = (bf16[64]{0:T(256)(128)(2,1)S(1)}, bf16[64]{0:T(256)(128)(2,1)}, u32[]{:S(2)}) copy-start(bf16[64]{0:T(256)(128)(2,1)} %param.23) | copy-start | bytes 388
  7.2 5.2 %copy-start.30 = (bf16[64]{0:T(256)(128)(2,1)S(1)}, bf16[64]{0:T(256)(128)(2,1)}, u32[]{:S(2)}) copy-start(bf16[64]{0:T(256)(128)(2,1)} %param.18) | copy-start | bytes 388
  7.2 5.3 %copy-start.25 = (bf16[64,1024]{1,0:T(8,128)(2,1)S(1)}, bf16[64,1024]{1,0:T(8,128)(2,1)}, u32[]{:S(2)}) copy-start(bf16[64,1024]{1,0:T(8,128)(2,1)} %refs_4_.1) | copy-start | bytes 393220
  7.2 193.4 %all-gather.2.cloned.1.call-start = ((), (), s32[]{:S(2)}) async-start(), calls=%async_computation.1 | async-start | bytes 2359296 | tf_op jit(solution)/shard_map/all_gather | solution.py:1003
  10.2 62.9 %copy-start.8 = (bf16[1,128,1024]{2,1,0:T(8,128)(2,1)S(1)}, bf16[1,128,1024]{2,1,0:T(8,128)(2,1)}, u32[]{:S(2)}) copy-start(bf16[1,128,1024]{2,1,0:T(8,128)(2,1)} %param.14) | copy-start | bytes 786436
  12.3 62.1 %copy-start.12 = (bf16[1,128,1024]{2,1,0:T(8,128)(2,1)S(1)}, bf16[1,128,1024]{2,1,0:T(8,128)(2,1)}, u32[]{:S(2)}) copy-start(bf16[1,128,1024]{2,1,0:T(8,128)(2,1)} %param.15) | copy-start | bytes 786436
  12.3 62.1 %copy-start.26 = (s32[16]{0:T(128)S(1)}, s32[16]{0:T(128)}, u32[]{:S(2)}) copy-start(s32[16]{0:T(128)} %so.3) | copy-start | bytes 196
  67.7 2.1 copy-start
  69.8 2.0 copy-start.6
  72.4 48.5 %copy-start.3 = (bf16[16,64,1024]{2,1,0:T(8,128)(2,1)}, bf16[16,64,1024]{2,1,0:T(8,128)(2,1)S(1)}, u32[]{:S(2)}) copy-start(bf16[16,64,1024]{2,1,0:T(8,128)(2,1)S(1)} %get-tuple-element.45) | copy-start | bytes 6291460
  74.4 41.8 %copy-start.9 = (bf16[128,1024]{1,0:T(8,128)(2,1)}, bf16[128,1024]{1,0:T(8,128)(2,1)S(1)}, u32[]{:S(2)}) copy-start(bf16[128,1024]{1,0:T(8,128)(2,1)S(1)} %fusion.2.h) | copy-start | bytes 786436
  74.4 2.2 copy-start.1
  76.7 43.9 %copy-start.29 = (s32[1,128,8]{1,2,0:T(8,128)S(1)}, s32[1,128,8]{1,2,0:T(8,128)}, u32[]{:S(2)}) copy-start(s32[1,128,8]{1,2,0:T(8,128)} %param.17) | copy-start | bytes 12292
  116.2 2.0 copy-start.7
  118.2 1.3 copy-start.10
  120.3 1.3 copy-start.15
  120.3 1.3 copy-start.14
  120.4 218.8 %reduce-scatter.2.cloned.1.call-start = ((), (), s32[]{:S(2)}) async-start(), calls=%async_computation.2 | async-start | bytes 7077888 | tf_op jit(solution)/shard_map/reduce_scatter | solution.py:1004
  121.5 78.4 %copy-start.4 = (f32[128,1024]{1,0:T(8,128)}, f32[128,1024]{1,0:T(8,128)S(1)}, u32[]{:S(2)}) copy-start(f32[128,1024]{1,0:T(8,128)S(1)} %get-tuple-element.133.xm) | copy-start | bytes 1572868
  121.7 1.3 copy-start.27
  122.3 77.7 %copy-start.28 = (f32[128,128]{1,0:T(8,128)}, f32[128,128]{1,0:T(8,128)S(1)}, u32[]{:S(2)}) copy-start(f32[128,128]{1,0:T(8,128)S(1)} %fusion.4.gt) | copy-start | bytes 196612
  200.6 128.4 %copy-start.2 = (bf16[16,64,2048]{2,1,0:T(8,128)(2,1)S(1)}, bf16[16,64,2048]{2,1,0:T(8,128)(2,1)}, u32[]{:S(2)}) copy-start(bf16[16,64,2048]{2,1,0:T(8,128)(2,1)} %copy-done) | copy-start | bytes 12582916
  200.7 128.4 %copy-start.5 = (f32[128,1024]{1,0:T(8,128)S(1)}, f32[128,1024]{1,0:T(8,128)}, u32[]{:S(2)}) copy-start(f32[128,1024]{1,0:T(8,128)} %copy-done.4) | copy-start | bytes 1572868
  200.7 128.4 %copy-start.17 = (bf16[64,1024]{1,0:T(8,128)(2,1)S(1)}, bf16[64,1024]{1,0:T(8,128)(2,1)}, u32[]{:S(2)}) copy-start(bf16[64,1024]{1,0:T(8,128)(2,1)} %wq.1) | copy-start | bytes 393220
  200.7 128.4 %copy-start.23 = (bf16[64,512]{1,0:T(8,128)(2,1)S(1)}, bf16[64,512]{1,0:T(8,128)(2,1)}, u32[]{:S(2)}) copy-start(bf16[64,512]{1,0:T(8,128)(2,1)} %wv.1) | copy-start | bytes 196612
  200.7 128.4 %copy-start.24 = (bf16[64,512]{1,0:T(8,128)(2,1)S(1)}, bf16[64,512]{1,0:T(8,128)(2,1)}, u32[]{:S(2)}) copy-start(bf16[64,512]{1,0:T(8,128)(2,1)} %wk.1) | copy-start | bytes 196612
  329.1 1.2 copy-start.11
  330.3 1.0 copy-start.18
  331.3 1.0 copy-start.19
  332.4 1.0 copy-start.20
  333.4 1.0 copy-start.22
  339.2 1.1 copy-start.16
  (2 other events, 1.5 us)
Sparse Core Ops, SparseCore 0:
  120.5 45.5 all-gather.1
  200.1 108.5 reduce-scatter.1

commit v4 on v3

--- a/solution.py
+++ b/solution.py
@@ -18,6 +18,7 @@
 
 MESH = pl.DeviceIdType.MESH
 ANY = pl.BlockSpec(memory_space=pl.ANY)
+HBM = pl.BlockSpec(memory_space=pltpu.HBM)
 VMEM = pl.BlockSpec(memory_space=pltpu.VMEM)
 DMA = pltpu.SemaphoreType.DMA
 NEAR_LAST = (6, 5, 7, 2, 4, 1, 3)
@@ -54,6 +55,19 @@
 
     def chip_from(self, k):
         return 4 * lax.rem(self.chip // 4 + k // 4, 2) + lax.rem(lax.rem(self.chip, 4) + 4 - lax.rem(k, 4), 4)
+
+    def turn(self, k):
+        k = k + k // 3 - 2 * (k // 4) + k // 5 - k // 6
+        m = lax.rem(k, 4)
+        return k // 4, m + m // 2 - 2 * (m // 3)
+
+    def turn_at(self, k):
+        z, y = self.turn(k)
+        return 4 * lax.rem(self.chip // 4 + z, 2) + lax.rem(lax.rem(self.chip, 4) + y, 4)
+
+    def turn_from(self, k):
+        z, y = self.turn(k)
+        return 4 * lax.rem(self.chip // 4 + z, 2) + lax.rem(lax.rem(self.chip, 4) + 4 - y, 4)
 
     def ctx_peers(self):
         return [{"ctx": self.ctx(k)} for k in range(1, N_CTX)]
@@ -115,6 +129,55 @@
         self.across.wait_send()
         for copy in self.near + self.rest:
             copy.wait()
+
+
+class AxisScatter:
+    sems = (2, 8, 8)
+
+    @staticmethod
+    def scratch(x):
+        one = x.shape[1:]
+        return [pltpu.VMEM((2,) + one, x.dtype), pltpu.VMEM((8,) + one, x.dtype), pltpu.VMEM(one, x.dtype)]
+
+    def __init__(self, here, x, total, mine, far, summed, load, send, recv):
+        c = here.c
+        across = lax.rem(c + 4, 8)
+        self.mine, self.far, self.summed, self.total = mine, far, summed, total
+        self.loads = [pltpu.make_async_copy(x.at[j], mine.at[i], load.at[i]) for i, j in enumerate((c, across))]
+        self.copies = []
+        for z in (1, 0):
+            for k in (2, 1, 3):
+                peer = c // 4 * 4 + lax.rem(lax.rem(c, 4) + k, 4)
+                i = 4 * z + k
+                block = lax.rem(peer + 4 * z, 8)
+                self.copies.append(remote(x.at[block], far.at[i], send.at[i], recv.at[i], {"ctx": peer}))
+        self.over = remote(summed, far.at[4], send.at[4], recv.at[4], {"ctx": across})
+
+    def start(self):
+        for copy in self.loads + self.copies:
+            copy.start()
+
+    def cross(self):
+        for copy in self.loads:
+            copy.wait()
+        for copy in self.copies:
+            copy.wait_recv()
+        both = self.mine[1].astype(f32)
+        for k in (5, 6, 7):
+            both += self.far[k].astype(f32)
+        self.summed[...] = both.astype(bf16)
+        self.over.start()
+        both = self.mine[0].astype(f32)
+        for k in (1, 2, 3):
+            both += self.far[k].astype(f32)
+        self.total[...] = both
+
+    def wait(self):
+        self.over.wait_recv()
+        self.total[...] += self.far[4].astype(f32)
+        self.over.wait_send()
+        for copy in self.copies:
+            copy.wait_send()
 
 
 class Turn:
@@ -269,7 +332,7 @@
 
 
 def params(cid):
-    return pltpu.CompilerParams(collective_id=cid, has_side_effects=True, vmem_limit_bytes=40 * 2**20)
+    return pltpu.CompilerParams(collective_id=cid, has_side_effects=True, vmem_limit_bytes=60 * 2**20)
 
 
 def call(kernel, outs, scratch, cid, *args, out_specs=None):
@@ -277,7 +340,7 @@
         kernel,
         out_shape=outs,
         in_specs=[ANY] * len(args),
-        out_specs=out_specs or [ANY] * len(outs),
+        out_specs=out_specs or [HBM] * len(outs),
         scratch_shapes=scratch,
         compiler_params=params(cid),
     )(*args)
@@ -336,23 +399,24 @@
     return factor * scaled - values * factor * factor * factor * inner
 
 
-def experts(routed, gates, up_all, wgu_all, wd_all):
+def experts(routed, gates, up_all, wgu_all, wd_all, h_one):
     rows, width = routed.shape
     both = 2 * rows
     f = wd_all.shape[2] // 2 * 8 * wd_all.shape[1] // width
     hid = 2 * f
-    wrows = rows + rows // 2
     chunk = 256
 
     def kernel(
-        x, g, u, wg, wdown, out_part, total, gback, dwall,
-        xs, gs, up, wgu, wd, usem, wsem, parts, near, summed, far, hg, dgu, gparts,
+        x, g, u, wg, wdown, ho, out_part, total, gback, dwgu, dwd, hs,
+        dparts, dmine, dfar, dsum, xs, gs, up, wgu, wd, usem, wsem, parts, near, summed, far, hg, dgu, gparts,
         xsend, xrecv, xfsend, xfrecv, gsend, grecv, gfsend, gfrecv,
-        nsend, nrecv, rsend, rrecv, psend, precv,
+        nsend, nrecv, rsend, rrecv, hsend, hrecv, dload, dsend, drecv, psend, precv,
     ):
         here = Here()
         core, e = here.core, here.e
-        greet(here.exp_peers() + here.other_core_peers())
+        greet(here.exp_peers() + here.other_core_peers() + here.ctx_peers())
+        rows_h = AxisGather(here, ho, hs, hsend, hrecv)
+        down = AxisScatter(here, dparts, dwd, dmine, dfar, dsum, dload, dsend, drecv)
         own = [
             pltpu.make_async_copy(g, gs.at[e], gfsend.at[0]),
             pltpu.make_async_copy(x, xs.at[e], xfsend.at[0]),
@@ -377,12 +441,12 @@
 
         def away(k):
             return [
-                remote(g, gs.at[e], gsend.at[k], grecv.at[k], here.same_core(k)),
-                remote(x, xs.at[e], xsend.at[k], xrecv.at[k], here.same_core(k)),
+                remote(g, gs.at[e], gsend.at[k], grecv.at[k], {"exp": 2 * here.turn_at(k) + core}),
+                remote(x, xs.at[e], xsend.at[k], xrecv.at[k], {"exp": 2 * here.turn_at(k) + core}),
             ]
 
         def pass_on(k):
-            slot = 2 * here.chip_from(k) + core
+            slot = 2 * here.turn_from(k) + core
             return [
                 remote(gs.at[slot], gs.at[slot], gfsend.at[k], gfrecv.at[k], here.partner),
                 remote(xs.at[slot], xs.at[slot], xfsend.at[k], xfrecv.at[k], here.partner),
@@ -392,15 +456,16 @@
             return remote(parts.at[k, 1 - core], near.at[k], nsend.at[k], nrecv.at[k], here.partner)
 
         def to_chip(k):
-            where = {"exp": 2 * here.chip_from(k) + core}
+            where = {"exp": 2 * here.turn_from(k) + core}
             return remote(summed.at[k], far.at[k], rsend.at[k], rrecv.at[k], where)
 
         def gate_part(j):
             return remote(gparts.at[j], gback.at[e], psend.at[j], precv.at[e], {"exp": j})
 
-        for k in range(1, 8):
-            for copy in away(k):
+        for k in range(1, 4):
+            for copy in away(jnp.int32(k)):
                 copy.start()
+        rows_h.start()
 
         picks = lax.broadcasted_iota(jnp.int32, (32, 2 * 128), 0) == 2 * e + (
             lax.broadcasted_iota(jnp.int32, (32, 2 * 128), 1) // 128
@@ -421,11 +486,9 @@
                 to_chip(k).start()
 
         def step(k, carry):
-            @pl.when(k < 7)
+            @pl.when(k < 4)
             def _():
-                for copy in away(k + 1):
-                    copy.wait_recv()
-                for copy in pass_on(k + 1):
+                for copy in away(k + 4):
                     copy.start()
 
             @pl.when(k == 0)
@@ -440,7 +503,7 @@
                 for copy in pass_on(k):
                     copy.wait_recv()
 
-            chip = here.chip_from(k)
+            chip = here.turn_from(k)
             at = pl.ds(pl.multiple_of(chip * both, both), both)
             xb = xs[pl.ds(2 * chip, 2)].reshape(both, width)
             ub = up[pl.ds(2 * chip, 2)].reshape(both, width)
@@ -477,11 +540,16 @@
             to_partner(k).start()
             gate_part(2 * chip + 1 - core).start()
 
+            @pl.when(k < 7)
+            def _():
+                for copy in away(k + 1):
+                    copy.wait_recv()
+                for copy in pass_on(k + 1):
+                    copy.start()
+
             @pl.when(k > 0)
             def _():
                 gate_part(2 * chip + core).start()
-
-            out_part[pl.ds(2 * chip, 2)] = dot(hg[at], wd[...]).astype(bf16).reshape(2, rows, width)
 
             @pl.when(k > 0)
             def _():
@@ -493,24 +561,33 @@
         mine = pltpu.make_async_copy(gparts.at[e], gback.at[e], psend.at[e])
         mine.start()
         finish(jnp.int32(7))
+        rows_h.cross()
+
+        def down_rows(i, carry):
+            at = pl.ds(pl.multiple_of(i * 256, 256), 256)
+            grads = dot(hg[:, at], up[...].reshape(16 * rows, width), TN).astype(bf16)
+            cols = pl.ds(pl.multiple_of((i // 2) * width, width), width)
+            dparts[pl.ds(4 * lax.rem(i, 2), 4), :, cols] = grads.reshape(4, rows // 2, width)
+            return carry
+
+        lax.fori_loop(0, hid // 256, down_rows, 0)
+        down.start()
 
         def weight_rows(i, carry):
             at = pl.ds(pl.multiple_of(i * 256, 256), 256)
             columns = xs[:, :, at].reshape(16 * rows, 256)
             grads = dot(columns, dgu[...], TN).astype(bf16)
-            dwall[pl.ds(2 * i, 2), pl.ds(0, rows)] = grads.reshape(2, rows, 2 * hid)
+            dwgu[pl.ds(2 * i, 2)] = grads.reshape(2, rows, 2 * hid)
             return carry
 
         lax.fori_loop(0, width // 256, weight_rows, 0)
 
-        def down_rows(i, carry):
-            at = pl.ds(pl.multiple_of(i * 256, 256), 256)
-            grads = dot(hg[:, at], up[...].reshape(16 * rows, width), TN).astype(bf16)
-            cols = pl.ds(pl.multiple_of((i // 2) * width, width), width)
-            dwall[pl.ds(4 * lax.rem(i, 2), 4), pl.ds(rows, rows // 2), cols] = grads.reshape(4, rows // 2, width)
+        def outputs(i, carry):
+            at = pl.ds(pl.multiple_of(i * 512, 512), 512)
+            out_part[pl.ds(512 // rows * i, 512 // rows)] = dot(hg[at], wd[...]).astype(bf16).reshape(512 // rows, rows, width)
             return carry
 
-        lax.fori_loop(0, hid // 256, down_rows, 0)
+        lax.fori_loop(0, 16 * rows // 512, outputs, 0)
 
         def collect(k, carry):
             to_chip(k).wait_recv()
@@ -518,9 +595,11 @@
             return carry
 
         lax.fori_loop(1, 8, collect, 0)
+        down.cross()
         for copy in first:
             copy.wait_send()
         mine.wait()
+        rows_h.wait()
 
         def drain(k, carry):
             for copy in away(k) + pass_on(k) + [to_partner(k), to_chip(k)]:
@@ -537,6 +616,7 @@
             return carry
 
         lax.fori_loop(1, N_EXP, drain_gates, 0)
+        down.wait()
 
     block = (8, rows, width)
     return pl.pallas_call(
@@ -545,11 +625,15 @@
             shape((16, rows, width), bf16),
             shape((rows, width), f32),
             shape((16, 8, rows), f32),
-            shape((8, wrows, 2 * hid), bf16),
+            shape((8, rows, 2 * hid), bf16),
+            shape((rows // 2, 2 * width), f32),
+            shape((8,) + h_one.shape, bf16),
         ],
-        in_specs=[ANY] * 5,
-        out_specs=[VMEM, VMEM, ANY, VMEM],
+        in_specs=[ANY] * 6,
+        out_specs=[VMEM, VMEM, ANY, VMEM, VMEM, HBM],
         scratch_shapes=[
+            pltpu.VMEM((8, rows // 2, 2 * width), bf16),
+            *AxisScatter.scratch(shape((8, rows // 2, 2 * width), bf16)),
             pltpu.VMEM((16, rows, width), bf16),
             pltpu.VMEM((16, 32, rows), f32),
             pltpu.VMEM((16, rows, width), bf16),
@@ -565,10 +649,11 @@
             pltpu.VMEM((16 * rows, 2 * hid), bf16),
             pltpu.VMEM((16, 8, rows), f32),
         ]
-        + [DMA((8,))] * 12
+        + [DMA((8,))] * 14
+        + sem_shapes(AxisScatter)
         + [DMA((16,))] * 2,
         compiler_params=pltpu.CompilerParams(collective_id=3, has_side_effects=True, vmem_limit_bytes=60 * 2**20),
-    )(routed, gates, up_all, wgu_all, wd_all)
+    )(routed, gates, up_all, wgu_all, wd_all, h_one)
 
 
 SCALE = HEAD_SIZE ** (-0.5)
@@ -630,10 +715,12 @@
     count = N_CTX * rows
 
     def kernel(
-        h, w, fr, so, u, wd, out, kept, us, wds, stage, seq, heads, attn, send, recv, osend, orecv, ksem, *sems
+        h, wh, fr, so, u, wd, out, kept, us, wds, w, wsem, stage, seq, heads, attn, send, recv, osend, orecv, ksem, *sems
     ):
         here = Here()
         c = here.c
+        load = pltpu.make_async_copy(wh, w, wsem)
+        load.start()
         greet(here.ctx_peers() + here.exp_peers())
         cots = PairGather(here, u, us, *sems[0:4])
         downs = AxisGather(here, wd, wds, *sems[4:6])
@@ -663,6 +750,7 @@
 
             return carry
 
+        load.wait()
         lax.fori_loop(0, N_CTX, project, 0)
         arrive_own().start()
         downs.start()
@@ -726,9 +814,11 @@
             shape((16,) + cot.shape, bf16),
             shape((8,) + wd_own.shape, bf16),
         ],
-        in_specs=[VMEM] * 3 + [SMEM] + [ANY] * 2,
-        out_specs=[ANY] * 4,
+        in_specs=[VMEM, ANY, VMEM, SMEM] + [ANY] * 2,
+        out_specs=[HBM] * 4,
         scratch_shapes=[
+            pltpu.VMEM(wqkv.shape, bf16),
+            DMA,
             pltpu.VMEM((N_CTX, rows, 256), bf16),
             pltpu.VMEM((count, 256), bf16),
             pltpu.VMEM((4, count, 128), bf16),
@@ -742,7 +832,8 @@
 
 
 def attend_back(
-    grad_routed, gate_back, gates, routed, pack, x_mid, gain, cot, attn_low, wo_full, seq_qkv, freqs, spans, h_all, out_part
+    grad_routed, gate_back, gates, routed, pack, x_mid, gain, cot, attn_low, wo_full, seq_qkv, freqs, spans, h_all, out_part,
+    first_part,
 ):
     rows, width = grad_routed.shape
     count = N_CTX * rows
@@ -754,12 +845,15 @@
     ]
 
     def kernel(
-        gr, gb, gt, ri, pk, xm, gn, u, al, wof, seq, fr, so, h, op, mid, back, moe, wos, alls,
+        gr, gb, gt, ri, pk, xm, gn, u, al, wof, seq, fr, so, hh, op, dp, mid, back, moe, wos, alls, dwgu, h, hsem,
         low_w, low, wo_total, total, payload, wp, ga, grads, heads, acc, dqkv, cos, sin, *rest,
     ):
         here = Here()
+        load = pltpu.make_async_copy(hh, h, hsem)
+        load.start()
         greet(here.ctx_peers() + here.exp_peers())
-        bufs, sems = rest[:12], rest[12:]
+        bufs, sems = rest[:15], rest[15:]
+        first = AxisScatter(here, dp, dwgu, *bufs[12:15], *sems[23:26])
         arrive = Columns(here, ga, grads, *sems[0:2])
         outs = PairScatter(here, op, moe, *bufs[0:4], *sems[2:7])
         wo = PairScatter(here, wp, wo_total, *bufs[4:8], *sems[7:12])
@@ -785,6 +879,7 @@
         branch = grad_mid.astype(bf16)
         ga[...] = dot(branch, wof[...], NT).astype(bf16)
         arrive.start()
+        first.start()
         wp[...] = dot(al[...], branch, TN).astype(bf16).reshape(16, own, width)
         wo.start()
         column = (lax.broadcasted_iota(jnp.int32, (rows, 128), 1) == 32).astype(f32)
@@ -823,22 +918,25 @@
         dk = dk * cos[...] - swap_of(dk * sin[...])
         dqkv[:, 128:] = jnp.where(left, dk, dv).astype(bf16)
         turn.start()
-        wo.cross()
-        outs.cross()
+        load.wait()
         payload[:, :, :256] = dot(h[...], dqkv[...], TN).astype(bf16).reshape(16, own, 256)
         proj.start()
+        wo.cross()
+        proj.pass_on()
         wo.wait()
         low_w[...] = wo_total[...].astype(bf16)
         wo_rows.start()
-        proj.pass_on()
         proj.cross()
+        outs.cross()
         proj.wait()
         low[...] = total[...].astype(bf16)
         all_rows.start()
         outs.wait()
+        first.cross()
         turn.wait()
         wo_rows.wait()
         all_rows.wait()
+        first.wait()
 
     return pl.pallas_call(
         kernel,
@@ -848,10 +946,13 @@
             shape((rows, width), f32),
             shape((8, own, width), bf16),
             shape((8, own, 384), bf16),
+            shape(first_part.shape[1:], f32),
         ],
-        in_specs=[VMEM] * 12 + [SMEM, VMEM, ANY],
-        out_specs=[VMEM, ANY, VMEM, ANY, ANY],
+        in_specs=[VMEM] * 12 + [SMEM, ANY, ANY, ANY],
+        out_specs=[VMEM, HBM, VMEM, HBM, HBM, VMEM],
         scratch_shapes=[
+            pltpu.VMEM(h_all.shape, bf16),
+            DMA,
             pltpu.VMEM((own, width), bf16),
             pltpu.VMEM((own, 384), bf16),
             pltpu.VMEM((own, width), f32),
@@ -867,24 +968,41 @@
             pltpu.VMEM((count, 128), f32),
         ]
         + [b for x in scatters for b in PairScatter.scratch(x)]
-        + sem_shapes(Columns, PairScatter, PairScatter, PairScatter, Turn, Gather, Gather),
-        compiler_params=pltpu.CompilerParams(collective_id=4, has_side_effects=True, vmem_limit_bytes=54 * 2**20),
+        + AxisScatter.scratch(first_part)
+        + sem_shapes(Columns, PairScatter, PairScatter, PairScatter, Turn, Gather, Gather, AxisScatter),
+        compiler_params=pltpu.CompilerParams(collective_id=4, has_side_effects=True, vmem_limit_bytes=60 * 2**20),
     )(
         grad_routed, gate_back, gates, routed, pack, x_mid, gain, cot, attn_low, wo_full, seq_qkv, freqs, spans, h_all,
-        out_part,
+        out_part, first_part,
     )
 
 
 def finish_tokens(
-    back, wqkv, tokens, gain, grad_mid, x_mid, moe_out, owned, wo_sums, w_query, key_matrix, value_matrix, norm_attn
+    back, wqkv, tokens, gain, grad_mid, x_mid, moe_out, owned, wo_sums, w_query, key_matrix, value_matrix, norm_attn,
+    grad_first, grad_down,
 ):
     rows, width = tokens.shape
     own = w_query.shape[0]
-
-    def kernel(
-        back, wqkv, x, gain, mid, xm, moe, owned, wos, wq, wk, wv, norm,
-        result, grad, gq, gk, gv, go, tail, ga,
-    ):
+    f = grad_first.shape[1] // 4
+    args = (
+        back, wqkv, tokens, gain, grad_mid, x_mid, moe_out, owned, wo_sums, w_query, key_matrix, value_matrix,
+        norm_attn[None, :], grad_first, grad_down,
+    )
+
+    def kernel(*refs):
+        n = len(args)
+        ins, (result, grad, gq, gk, gv, go, tail, gm, ga, gg, gu, gd) = refs[:n], refs[n : n + 12]
+        held, sems = refs[n + 12 : -1], refs[-1]
+        loads = [pltpu.make_async_copy(a, b, sems.at[i]) for i, (a, b) in enumerate(zip(ins, held))]
+        for load in loads:
+            load.start()
+        for load in loads:
+            load.wait()
+        back, wqkv, x, gain, mid, xm, moe, owned, wos, wq, wk, wv, norm, first, down = held
+        for i in range(2):
+            gg[i] = first[:, f * i : f * (i + 1)]
+            gu[i] = first[:, f * (2 + i) : f * (3 + i)]
+            gd[i] = down[:, 2 * f * i : 2 * f * (i + 1)]
         result[...] = (xm[...] + moe[...]).astype(bf16)
         values = x[...].astype(f32)
         factor = factor_of(values)
@@ -906,17 +1024,15 @@
             gk[:, at] = keys
             gv[:, at] = vals
             sums += keys * wk[:, at].astype(f32) + vals * wv[:, at].astype(f32)
-        tail[...] = rest
-        ga[...] = jnp.broadcast_to(jnp.sum(sums, axis=1, keepdims=True) / norm[...].astype(f32), (own, 128))
+        turned = jnp.transpose(rest)
+        tail[...] = turned[:32]
+        gm[...] = turned[32:33]
+        ga[...] = jnp.sum(jnp.transpose(sums), axis=0, keepdims=True) / norm[...].astype(f32)
         total = wos[0].astype(f32)
         for i in range(1, N_CTX):
             total += wos[i].astype(f32)
         go[...] = total
 
-    args = (
-        back, wqkv, tokens, gain, grad_mid, x_mid, moe_out, owned, wo_sums, w_query, key_matrix, value_matrix,
-        norm_attn[:, None],
-    )
     return pl.pallas_call(
         kernel,
         out_shape=[
@@ -926,32 +1042,18 @@
             shape((own, width // 2), f32),
             shape((own, width // 2), f32),
             shape((own, width), f32),
-            shape((own, 128), f32),
-            shape((own, 128), f32),
+            shape((32, own), f32),
+            shape((1, own), f32),
+            shape((1, own), f32),
+            shape((2, rows, f), f32),
+            shape((2, rows, f), f32),
+            shape((2, rows // 2, 2 * f), f32),
         ],
-        in_specs=[VMEM] * len(args),
-        out_specs=[VMEM] * 8,
-        compiler_params=pltpu.CompilerParams(vmem_limit_bytes=40 * 2**20),
+        in_specs=[ANY] * len(args),
+        out_specs=[VMEM] * 12,
+        scratch_shapes=[pltpu.VMEM(a.shape, a.dtype) for a in args] + [DMA((len(args),))],
+        compiler_params=pltpu.CompilerParams(vmem_limit_bytes=60 * 2**20),
     )(*args)
-
-
-def finish_experts(shares):
-    rows = shares.shape[0] * 2 // 3
-    f = shares.shape[1] // 4
-
-    def kernel(x, gg, gu, gd):
-        for i in range(2):
-            gg[i] = x[:rows, f * i : f * (i + 1)].astype(f32)
-            gu[i] = x[:rows, f * (2 + i) : f * (3 + i)].astype(f32)
-            gd[i] = x[rows:, 2 * f * i : 2 * f * (i + 1)].astype(f32)
-
-    return pl.pallas_call(
-        kernel,
-        out_shape=[shape((2, rows, f), f32), shape((2, rows, f), f32), shape((2, rows // 2, 2 * f), f32)],
-        in_specs=[VMEM],
-        out_specs=[VMEM] * 3,
-        compiler_params=pltpu.CompilerParams(vmem_limit_bytes=20 * 2**20),
-    )(shares)
 
 
 def body(
@@ -998,28 +1100,28 @@
     masked = jnp.where(chosen, logits, neg_big)
     lifted = jnp.where(chosen, jnp.exp(masked - jnp.max(masked, axis=-1, keepdims=True)), 0.0)
     gates = lifted / jnp.sum(lifted, axis=-1, keepdims=True)
-    out_part, grad_routed, gate_back, grad_weights = experts(routed_in, gates[:, :32].T, up_all, wgu_all, wd_all)
-    h_late, _ = lax.optimization_barrier((h_one, attn_low))
-    h_all = lax.all_gather(h_late, "ctx", axis=0, tiled=True)
-    shares = lax.psum_scatter(grad_weights, "ctx", scatter_dimension=0, tiled=True)[0]
-    grad_mid, back, moe_out, wo_sums, owned = attend_back(
+    out_part, grad_routed, gate_back, grad_wgu, grad_wd, h_all = experts(
+        routed_in, gates[:, :32].T, up_all, wgu_all, wd_all, h_one
+    )
+    h_all = h_all.reshape(N_CTX * rows, width)
+    grad_mid, back, moe_out, wo_sums, owned, grad_first = attend_back(
         grad_routed, gate_back, gates, routed_in, pack_all, x_mid, gain_m, cotangent, attn_low, wo, seq_qkv,
-        freqs[:, :128], span_order, h_all, out_part,
+        freqs[:, :128], span_order, h_all, out_part, grad_wgu,
     )
-    result, grad_tokens, out_wq, out_wk, out_wv, out_wo, tail, out_gain_a = finish_tokens(
-        back, wqkv, tokens, gain_a, grad_mid, x_mid, moe_out, owned, wo_sums, w_query, key_matrix, value_matrix, norm_attn
+    result, grad_tokens, out_wq, out_wk, out_wv, out_wo, tail, out_gain_m, out_gain_a, out_wg, out_wu, out_wd = finish_tokens(
+        back, wqkv, tokens, gain_a, grad_mid, x_mid, moe_out, owned, wo_sums, w_query, key_matrix, value_matrix, norm_attn,
+        grad_first, grad_wd,
     )
-    out_wg, out_wu, out_wd = finish_experts(shares)
     return (
         result[None],
         grad_tokens[None],
-        out_gain_a[:, 0],
+        out_gain_a[0],
         out_wq,
         out_wk,
         out_wv,
         out_wo,
-        tail[:, 32],
-        tail[:, :32],
+        out_gain_m[0],
+        tail.T,
         out_wg,
         out_wu,
         out_wd,

time: 349 us -> 311 us (0.89)
  local copies, waits for them, and re-layouts: 27.6 us -> 7.74 us
  between operations: 14.5 us -> 1.07 us
  Pallas kernels: 304 us -> 292 us
  other arithmetic: 1.25 us -> 6.49 us
    pallas_call x1, Pallas kernels: 128 us -> 88.6 us  [attend_back(): pl.pallas_call(kernel, out_shape=[shape((rows, width), f32), shape((rows,...]
    pallas_call x1, Pallas kernels: 76.9 us -> 101 us  [experts(): pl.pallas_call(kernel, out_shape=[shape((16, rows, width), bf16), shape((...]
    unnamed x68 -> x23, local copies, waits for them, and re-layouts: 20.1 us -> 2.52 us
    pallas_call x1, Pallas kernels: 2.77 us -> 7.21 us  [finish_tokens(): pl.pallas_call(kernel, out_shape=[shape((rows, width), bf16), shape((rows...]
  transfers between devices with their start and end apart: 2 -> 0, of which waited for: 0 -> 0; matrix products, arithmetic and copies ran while one was open for 1% -> 0% of each run, Pallas kernels for 60% -> 0%
where the time goes in v4:
time: 311 us; the launch traced here: 309 us
  Pallas kernels  292 us (94%)
  local copies, waits for them, and re-layouts  7.74 us (2%)
  other arithmetic  6.49 us (2%)
    pallas_call x1, Pallas kernels, experts(): pl.pallas_call(kernel, out_shape=[shape((16, rows, width), bf16), shape((...  101 us
    pallas_call x1, Pallas kernels, attend_back(): pl.pallas_call(kernel, out_shape=[shape((rows, width), f32), shape((rows,...  88.6 us
    pallas_call x1, Pallas kernels, call(): pl.pallas_call(kernel, out_shape=outs, in_specs=[ANY] * len(args), out_sp...  55.1 us
    pallas_call x1, Pallas kernels, attend(): pl.pallas_call(kernel, out_shape=[shape((rows, N_CTX * 128), bf16), shape...  40.3 us
    pallas_call x1, Pallas kernels, finish_tokens(): pl.pallas_call(kernel, out_shape=[shape((rows, width), bf16), shape((rows...  7.21 us

profile of v4, /device:TPU:2, one launch (start us, length us, event | category | flops | bytes accessed | tf_op | source)
XLA Modules:
  0.0 309.1 jit_solution(18207397043057416733)
XLA Ops:
  0.7 0.8 broadcast_select_fusion.1
  1.4 1.1 fusion
  2.5 0.0 copy-start.9
  2.6 0.5 slice.55.fr
  3.1 0.7 fusion.8.refs_3_
  3.7 0.8 copy.34
  4.5 0.6 pad.8.refs_2_
  5.1 0.8 copy.35
  5.9 0.3 fusion.3
  6.2 0.9 copy.39
  7.1 1.0 reshape.125
  8.1 1.0 reshape.126
  9.1 0.1 pad_maximum_fusion.1
  9.2 0.8 copy.40
  10.0 0.7 pad_maximum_fusion.2.wd
  10.8 0.8 pad_maximum_fusion.refs_0_
  11.6 55.1 %shard_map.229 = (bf16[8,128,2048]{2,1,0:T(8,128)(2,1)}, bf16[16,64,2048]{2,1,0:T(8,128)(2,1)}, bf16[16,64,128]{2,1,0:T(8,128)(2,1)}, bf16[16,16,128]{2,1,0:T(8,128)(2,1)}, bf16[16,64,1024]{2,1,0:T(8,128)(2,1)}) custom-call(bf16[128,2048]{1,0:T(8,128)(2,1)} %pad_maximum_fusion.refs_0_, bf16[64,2048]{1,0:T(8,128)(2,1)} %bitcast.61, ...), custom_call_target="tpu_custom_call" | custom-call | tf_op jit(solution)/shard_map/pallas_call | solution.py:339
  66.7 0.8 convert_reduce_fusion
  67.5 0.6 slice_bitcast_fusion.8
  68.1 0.8 fusion.2.h.ho
  68.9 40.3 %shard_map.230 = (bf16[128,1024]{1,0:T(8,128)(2,1)}, bf16[1024,256]{1,0:T(8,128)(2,1)}, bf16[16,128,1024]{2,1,0:T(8,128)(2,1)}, bf16[8,64,2048]{2,1,0:T(8,128)(2,1)}) custom-call(bf16[128,1024]{1,0:T(8,128)(2,1)} %fusion.2.h.ho, bf16[1024,2048]{1,0:T(8,128)(2,1)} %bitcast.50, f32[1,256]{1,0:T(1,128)} %copy-done.9, s32[16]{0:T(128)} %so.3, ...), custom_call_target="tpu_custom_call" | custom-call | tf_op jit(solution)/shard_map/pallas_call | solution.py:809
  109.3 1.5 multiply_reduce_fusion
  110.8 0.1 multiply_convert_fusion.x.ri
  110.9 0.0 copy-start.2
  110.9 0.3 fusion.13
  111.2 0.2 fusion.5
  111.4 0.1 fusion.4.gt
  111.6 0.0 copy-start.5
  111.6 0.7 copy.37.g
  112.3 100.8 %shard_map.231 = (bf16[16,128,1024]{2,1,0:T(8,128)(2,1)}, f32[128,1024]{1,0:T(8,128)}, f32[16,8,128]{2,1,0:T(8,128)}, bf16[8,128,2048]{2,1,0:T(8,128)(2,1)}, f32...) custom-call(bf16[128,1024]{1,0:T(8,128)(2,1)} %copy-done.2, f32[32,128]{1,0:T(8,128)} %copy.37.g, ...), custom_call_target="tpu_custom_call" | custom-call | tf_op jit(solution)/shard_map/pallas_call | solution.py:622
  213.1 88.6 %shard_map.232 = (f32[128,1024]{1,0:T(8,128)}, bf16[128,2048]{1,0:T(8,128)(2,1)}, f32[128,1024]{1,0:T(8,128)}, bf16[8,64,1024]{2,1,0:T(8,128)(2,1)}, bf16[8,64,384]{2,1,0:T(8,128)(2,1)}, /*index=5*/f32[128,2048]{1,0:T(8,128)}) custom-call(f32[128,1024]{1,0:T(8,128)} %get-tuple-element.53.gr, f32[16,8,128]{2,1,0:T(8,128)} %get-tuple-element.54.gb, ...), custom_call_target="tpu_custom_call" | custom-call | tf_op jit(solution)/shard_map/pallas_call | solution.py:941
  301.7 7.2 %shard_map.233 = (bf16[128,1024]{1,0:T(8,128)(2,1)}, f32[128,1024]{1,0:T(8,128)}, f32[64,1024]{1,0:T(8,128)}, f32[64,512]{1,0:T(8,128)}, f32[64,512]{1,0:T(8,128...) custom-call(bf16[128,2048]{1,0:T(8,128)(2,1)} %get-tuple-element.59., ...), custom_call_target="tpu_custom_call" | custom-call | tf_op jit(solution)/shard_map/pallas_call | solution.py:1036
  (23 shorter events, 0.1 us)
Async XLA Ops:
  0.6 9.3 %copy-start.6 = (bf16[2,64,1024]{2,1,0:T(8,128)(2,1)S(1)}, bf16[2,64,1024]{2,1,0:T(8,128)(2,1)}, u32[]{:S(2)}) copy-start(bf16[2,64,1024]{2,1,0:T(8,128)(2,1)} %param.27) | copy-start | bytes 786436
  0.7 10.1 %copy-start.7 = (bf16[2,128,512]{2,1,0:T(8,128)(2,1)S(1)}, bf16[2,128,512]{2,1,0:T(8,128)(2,1)}, u32[]{:S(2)}) copy-start(bf16[2,128,512]{2,1,0:T(8,128)(2,1)} %param.26) | copy-start | bytes 786436
  0.7 10.1 %copy-start.8 = (bf16[2,128,512]{2,1,0:T(8,128)(2,1)S(1)}, bf16[2,128,512]{2,1,0:T(8,128)(2,1)}, u32[]{:S(2)}) copy-start(bf16[2,128,512]{2,1,0:T(8,128)(2,1)} %param.25) | copy-start | bytes 786436
  2.5 9.1 %copy-start.9 = (f32[1,256]{1,0:T(1,128)}, f32[1,256]{1,0:T(1,128)S(1)}, u32[]{:S(2)}) copy-start(f32[1,256]{1,0:T(1,128)S(1)} %compare_select_fusion.fr) | copy-start | bytes 3076
  10.0 58.1 %copy-start.3 = (bf16[1,128,1024]{2,1,0:T(8,128)(2,1)S(1)}, bf16[1,128,1024]{2,1,0:T(8,128)(2,1)}, u32[]{:S(2)}) copy-start(bf16[1,128,1024]{2,1,0:T(8,128)(2,1)} %param.14) | copy-start | bytes 786436
  68.9 40.3 %copy-start.1 = (bf16[16,64,1024]{2,1,0:T(8,128)(2,1)S(1)}, bf16[16,64,1024]{2,1,0:T(8,128)(2,1)}, u32[]{:S(2)}) copy-start(bf16[16,64,1024]{2,1,0:T(8,128)(2,1)} %get-tuple-element.48) | copy-start | bytes 6291460
  109.2 1.7 copy-start.4
  110.8 102.3 %copy-start = (f32[128,1024]{1,0:T(8,128)}, f32[128,1024]{1,0:T(8,128)S(1)}, u32[]{:S(2)}) copy-start(f32[128,1024]{1,0:T(8,128)S(1)} %get-tuple-element.91.xm.refs_5_) | copy-start | bytes 1572868
  110.9 1.3 copy-start.2
  111.6 101.6 %copy-start.5 = (f32[128,128]{1,0:T(8,128)}, f32[128,128]{1,0:T(8,128)S(1)}, u32[]{:S(2)}) copy-start(f32[128,128]{1,0:T(8,128)S(1)} %fusion.4.gt) | copy-start | bytes 196612

commit v5 on v4

--- a/solution.py
+++ b/solution.py
@@ -348,37 +348,6 @@
 
 def shape(s, t):
     return jax.ShapeDtypeStruct(s, t)
-
-
-def start_exchange(over_ctx, *shards):
-    n = len(shards)
-
-    def kernel(*refs):
-        here = Here()
-        greet(here.exp_peers() + here.ctx_peers())
-        ins, outs, sems = refs[: n + 1], refs[n + 1 : 2 * n + 2], refs[2 * n + 2 :]
-        items = [PairGather(here, ins[i + 1], outs[i + 1], *sems[4 * i + 2 : 4 * i + 6]) for i in range(n)]
-        rows = AxisGather(here, ins[0], outs[0], *sems[0:2])
-        for i in items:
-            i.start()
-        rows.start()
-        for i in items:
-            i.cross()
-        rows.cross()
-        for i in items:
-            i.pass_on()
-        for i in items:
-            i.wait()
-        rows.wait()
-
-    return call(
-        kernel,
-        [shape((8,) + over_ctx.shape, over_ctx.dtype)] + [shape((16,) + a.shape, a.dtype) for a in shards],
-        sem_shapes(AxisGather, *[PairGather] * n),
-        1,
-        over_ctx,
-        *shards,
-    )
 
 
 def dot(a, b, dims=((1,), (0,))):
@@ -536,8 +505,6 @@
                     dgu[at, up_cols] = (grad_hidden * silu).astype(bf16)
             for i in range(2):
                 gparts[2 * chip + i] = gate_sums[:, rows * i : rows * (i + 1)]
-            parts[k] = dot(dgu[at], wgu[...], NT).astype(bf16).reshape(2, rows, width)
-            to_partner(k).start()
             gate_part(2 * chip + 1 - core).start()
 
             @pl.when(k < 7)
@@ -551,16 +518,11 @@
             def _():
                 gate_part(2 * chip + core).start()
 
-            @pl.when(k > 0)
-            def _():
-                finish(k - 1)
-
             return carry
 
         lax.fori_loop(0, 8, step, 0)
         mine = pltpu.make_async_copy(gparts.at[e], gback.at[e], psend.at[e])
         mine.start()
-        finish(jnp.int32(7))
         rows_h.cross()
 
         def down_rows(i, carry):
@@ -572,6 +534,20 @@
 
         lax.fori_loop(0, hid // 256, down_rows, 0)
         down.start()
+
+        def input_rows(k, carry):
+            at = pl.ds(pl.multiple_of(here.turn_from(k) * both, both), both)
+            parts[k] = dot(dgu[at], wgu[...], NT).astype(bf16).reshape(2, rows, width)
+            to_partner(k).start()
+
+            @pl.when(k > 0)
+            def _():
+                finish(k - 1)
+
+            return carry
+
+        lax.fori_loop(0, 8, input_rows, 0)
+        finish(jnp.int32(7))
 
         def weight_rows(i, carry):
             at = pl.ds(pl.multiple_of(i * 256, 256), 256)
@@ -710,22 +686,73 @@
     return jnp.where(leading, -pltpu.roll(v, v.shape[1] - HALF, 1), pltpu.roll(v, HALF, 1))
 
 
-def attend(h_one, wqkv, freqs, spans, cot, wd_own):
-    rows = h_one.shape[0]
+def front(tokens, w_query, key_matrix, value_matrix, gains, router, w_out, cot, w_gate, w_up, w_down, freqs, spans):
+    rows, width = tokens.shape
+    own = w_query.shape[0]
+    f = w_gate.shape[2]
     count = N_CTX * rows
 
     def kernel(
-        h, wh, fr, so, u, wd, out, kept, us, wds, w, wsem, stage, seq, heads, attn, send, recv, osend, orecv, ksem, *sems
+        x, wq, wk, wv, gn, ro, wo, u, wg, wup, wdn, fr, so,
+        out, kept, h_out, gain_out, w_out_, ros, wos, us, wgus, wds,
+        own_w, own_wgu, own_wd, own_gain, w, gs, h, stage, seq, heads, attn, lsem,
+        send, recv, osend, orecv, ksem, *sems,
     ):
         here = Here()
         c = here.c
-        load = pltpu.make_async_copy(wh, w, wsem)
-        load.start()
+        loads = []
+        for i in range(2):
+            loads.append(pltpu.make_async_copy(wg.at[i], own_wgu.at[:, pl.ds(f * i, f)], lsem.at[3 * i]))
+            loads.append(pltpu.make_async_copy(wup.at[i], own_wgu.at[:, pl.ds(f * (2 + i), f)], lsem.at[3 * i + 1]))
+            loads.append(pltpu.make_async_copy(wdn.at[i], own_wd.at[:, pl.ds(width * i, width)], lsem.at[3 * i + 2]))
+        for load in loads:
+            load.start()
+        left = left_lanes((own, 128))
+        for i in range(N_CTX // 2):
+            at = slice(128 * i, 128 * (i + 1))
+            keys, vals = wk[:, at].astype(f32), wv[:, at].astype(f32)
+            one = jnp.where(left, keys, pltpu.roll(vals, HEAD_SIZE, 1))
+            two = jnp.where(left, pltpu.roll(keys, HEAD_SIZE, 1), vals)
+            for j, kv in ((2 * i, one), (2 * i + 1, two)):
+                own_w[:, 256 * j : 256 * j + 128] = wq[:, 128 * j : 128 * (j + 1)]
+                own_w[:, 256 * j + 128 : 256 * (j + 1)] = kv.astype(bf16)
+        half = gn[...].astype(f32)
+        odd = here.core == 1
+        lane = lax.broadcasted_iota(jnp.int32, half.shape, 1)
+        own_gain[...] = jnp.where(odd, jnp.where(lane < 64, 0.0, pltpu.roll(half, 64, 1)), jnp.where(lane < 64, half, 0.0))
         greet(here.ctx_peers() + here.exp_peers())
-        cots = PairGather(here, u, us, *sems[0:4])
-        downs = AxisGather(here, wd, wds, *sems[4:6])
-        cots.start()
+        gain_all = PairGather(here, own_gain, gs, *sems[0:4])
+        w_all = PairGather(here, own_w, w, *sems[4:8])
+        ro_all = PairGather(here, ro, ros, *sems[8:12])
+        wo_all = PairGather(here, wo, wos, *sems[12:16])
+        cots = PairGather(here, u, us, *sems[16:20])
+        firsts = AxisGather(here, own_wgu, wgus, *sems[20:22])
+        downs = AxisGather(here, own_wd, wds, *sems[22:24])
+        gain_all.start()
+        w_all.start()
+        for load in loads:
+            load.wait()
+        firsts.start()
         cos, sin = tables(place_column(so, 2 * c, rows), fr[...])
+        pr = place_row(so)
+        gain_all.cross()
+        w_all.cross()
+        for item in (wo_all, ro_all, cots):
+            item.start()
+        firsts.cross()
+        gain_all.pass_on()
+        gain_all.wait()
+        for i in range(8):
+            pair = gs[2 * i] + gs[2 * i + 1]
+            gain_out[:, 128 * i : 128 * (i + 1)] = pair
+        values = x[...].astype(f32)
+        h[...] = (values * factor_of(values) * gain_out[0:1, :]).astype(bf16)
+        keep_h = pltpu.make_async_copy(h, h_out, ksem.at[1])
+        keep_h.start()
+        w_all.pass_on()
+        w_all.wait()
+        keep_w = pltpu.make_async_copy(w, w_out_, ksem.at[2])
+        keep_w.start()
 
         def block_rows(ref, j):
             return ref.at[pl.ds(pl.multiple_of(j * rows, rows), rows)]
@@ -741,7 +768,8 @@
 
         def project(b, carry):
             j = lax.rem(c + 1 + b, N_CTX)
-            p = dot(h[...], w[:, pl.ds(pl.multiple_of(j * 256, 256), 256)])
+            at = pl.ds(pl.multiple_of(j * 256, 256), 256)
+            p = dot(h[...], w[:, :, at].reshape(width, 256))
             stage[j] = (p * cos + swap_of(p) * sin).astype(bf16)
 
             @pl.when(b < N_CTX - 1)
@@ -750,20 +778,18 @@
 
             return carry
 
-        load.wait()
         lax.fori_loop(0, N_CTX, project, 0)
         arrive_own().start()
-        downs.start()
-        pr = place_row(so)
+        for item in (wo_all, ro_all, cots):
+            item.cross()
         arrive_own().wait()
         for k in range(1, N_CTX):
             j = here.ctx(k)
             arrive(j).wait_send()
             remote(stage.at[j], block_rows(seq, j), send.at[j], recv.at[j], {"ctx": j}).wait_recv()
-        keep = pltpu.make_async_copy(seq, kept, ksem)
+        downs.start()
+        keep = pltpu.make_async_copy(seq, kept, ksem.at[0])
         keep.start()
-        cots.cross()
-        downs.cross()
         for i, part in enumerate(split_heads(seq[:, 128:])):
             heads[i] = part
 
@@ -796,39 +822,52 @@
             return carry
 
         lax.fori_loop(0, count // QROWS, step, 0)
-        cots.pass_on()
+        downs.cross()
+        for item in (wo_all, ro_all, cots):
+            item.pass_on()
         for k in range(1, N_CTX):
             j = here.ctx(k)
             leave(j).wait_send()
             remote(block_rows(attn, c), column(j), osend.at[j], orecv.at[j], {"ctx": j}).wait_recv()
         local().wait()
-        keep.wait()
-        cots.wait()
-        downs.wait()
+        for item in (keep, keep_h, keep_w, wo_all, ro_all, cots, firsts, downs):
+            item.wait()
 
     return pl.pallas_call(
         kernel,
         out_shape=[
             shape((rows, N_CTX * 128), bf16),
             shape((count, 256), bf16),
+            shape((rows, width), bf16),
+            shape((8, width), f32),
+            shape((16, own, N_CTX * 256), bf16),
+            shape((16,) + router.shape, bf16),
+            shape((16,) + w_out.shape, bf16),
             shape((16,) + cot.shape, bf16),
-            shape((8,) + wd_own.shape, bf16),
+            shape((8, rows, 4 * f), bf16),
+            shape((8, w_down.shape[1], 2 * width), bf16),
         ],
-        in_specs=[VMEM, ANY, VMEM, SMEM] + [ANY] * 2,
-        out_specs=[HBM] * 4,
+        in_specs=[VMEM] * 5 + [ANY] * 6 + [VMEM, SMEM],
+        out_specs=[HBM] * 3 + [VMEM] + [HBM] * 6,
         scratch_shapes=[
-            pltpu.VMEM(wqkv.shape, bf16),
-            DMA,
+            pltpu.VMEM((own, N_CTX * 256), bf16),
+            pltpu.VMEM((rows, 4 * f), bf16),
+            pltpu.VMEM((w_down.shape[1], 2 * width), bf16),
+            pltpu.VMEM((8, 128), f32),
+            pltpu.VMEM((16, own, N_CTX * 256), bf16),
+            pltpu.VMEM((16, 8, 128), f32),
+            pltpu.VMEM((rows, width), bf16),
             pltpu.VMEM((N_CTX, rows, 256), bf16),
             pltpu.VMEM((count, 256), bf16),
             pltpu.VMEM((4, count, 128), bf16),
             pltpu.VMEM((count, 128), bf16),
+            DMA((6,)),
         ]
         + [DMA((8,))] * 4
-        + [DMA]
-        + sem_shapes(PairGather, AxisGather),
+        + [DMA((3,))]
+        + sem_shapes(*[PairGather] * 5, AxisGather, AxisGather),
         compiler_params=params(2),
-    )(h_one, wqkv, freqs, spans, cot, wd_own)
+    )(tokens, w_query, key_matrix, value_matrix, gains, router, w_out, cot, w_gate, w_up, w_down, freqs, spans)
 
 
 def attend_back(
@@ -931,8 +970,8 @@
         proj.wait()
         low[...] = total[...].astype(bf16)
         all_rows.start()
+        first.cross()
         outs.wait()
-        first.cross()
         turn.wait()
         wo_rows.wait()
         all_rows.wait()
@@ -1060,38 +1099,22 @@
     tokens, cotangent, span_order, expert_choice, norm_attn, w_query, key_matrix, value_matrix,
     w_out, norm_moe, w_router, w_gate, w_up, w_down,
 ):
-    c = lax.axis_index("ctx")
     tokens, cotangent, choice = tokens[0], cotangent[0], expert_choice[0]
     rows, width = tokens.shape
-    own_rows = w_query.shape[0]
-    wgu_own = jnp.concatenate([w_gate[0], w_gate[1], w_up[0], w_up[1]], axis=1)
-    wd_own = jnp.concatenate([w_down[0], w_down[1]], axis=1)
-    wqkv_own = jnp.concatenate(
-        [
-            w_query.reshape(own_rows, N_CTX, 128),
-            key_matrix.reshape(own_rows, N_CTX, 64),
-            value_matrix.reshape(own_rows, N_CTX, 64),
-        ],
-        axis=2,
-    ).reshape(own_rows, N_CTX * 256)
     pack = jnp.pad(w_router, ((0, 0), (0, 128 - 32)))
-    gains = jnp.stack([norm_attn, norm_moe])
-    odd = lax.axis_index("exp") % 2
-    gains = jnp.concatenate([jnp.where(odd == 0, gains, 0.0), jnp.where(odd == 1, gains, 0.0)], axis=1)
-    gains = jnp.pad(gains, ((0, 14), (0, 0)))
-    wgu_all, wqkv, pack_all, gains, wo = start_exchange(wgu_own, wqkv_own, pack, gains, w_out)
+    gains = jnp.pad(jnp.stack([norm_attn, norm_moe]), ((0, 6), (0, 64)))
+    lanes = jnp.arange(256, dtype=jnp.int32)
+    freqs = rope_base ** (-((lanes % HALF).astype(f32) * 2.0 / HEAD_SIZE))
+    freqs = jnp.where(lanes < 192, freqs, 0.0)[None, :]
+    attn_low, seq_qkv, h_one, gains, wqkv, pack_all, wo, up_all, wgu_all, wd_all = front(
+        tokens, w_query, key_matrix, value_matrix, gains, pack, w_out, cotangent, w_gate, w_up, w_down, freqs, span_order
+    )
+    gain_a, gain_m = gains[0:1], gains[1:2]
     wgu_all = wgu_all.reshape(width, 4 * w_gate.shape[2])
     wqkv = wqkv.reshape(width, N_CTX * 256)
     pack_all = pack_all.reshape(width, 128)
     wo = wo.reshape(width, width)
-    gains = jnp.sum(gains[:, :2].astype(f32).reshape(8, 2, 2, 128), axis=1).transpose(1, 0, 2).reshape(2, width)
-    gain_a, gain_m = gains[0:1], gains[1:2]
-    lanes = jnp.arange(256, dtype=jnp.int32)
-    freqs = rope_base ** (-((lanes % HALF).astype(f32) * 2.0 / HEAD_SIZE))
-    freqs = jnp.where(lanes < 192, freqs, 0.0)[None, :]
     inputs = tokens.astype(f32)
-    h_one = (inputs * factor_of(inputs) * gain_a).astype(bf16)
-    attn_low, seq_qkv, up_all, wd_all = attend(h_one, wqkv, freqs, span_order, cotangent, wd_own)
     x_mid = inputs + dot(attn_low, wo)
     routed_in = (x_mid * factor_of(x_mid) * gain_m).astype(bf16)
     logits = dot(routed_in, pack_all)

time: 311 us -> 304 us (0.977)
  other arithmetic: 6.49 us -> 1.94 us
    pallas_call x1, Pallas kernels: 88.6 us -> 97.5 us  [attend_back(): pl.pallas_call(kernel, out_shape=[shape((rows, width), f32), shape((rows,...]
    pallas_call x2 -> x1, Pallas kernels: 95.4 us -> 90.6 us  [front(): pl.pallas_call(kernel, out_shape=[shape((rows, N_CTX * 128), bf16), shape...]
where the time goes in v5:
time: 304 us; the launch traced here: 303 us
  Pallas kernels  293 us (96%)
  local copies, waits for them, and re-layouts  4.85 us (2%)
    pallas_call x1, Pallas kernels, experts(): pl.pallas_call(kernel, out_shape=[shape((16, rows, width), bf16), shape((...  97.8 us
    pallas_call x1, Pallas kernels, attend_back(): pl.pallas_call(kernel, out_shape=[shape((rows, width), f32), shape((rows,...  97.5 us
    pallas_call x1, Pallas kernels, front(): pl.pallas_call(kernel, out_shape=[shape((rows, N_CTX * 128), bf16), shape...  90.6 us
    pallas_call x1, Pallas kernels, finish_tokens(): pl.pallas_call(kernel, out_shape=[shape((rows, width), bf16), shape((rows...  7.22 us

profile of v5, /device:TPU:2, one launch (start us, length us, event | category | flops | bytes accessed | tf_op | source)
XLA Modules:
  0.0 303.5 jit_solution(15163141677695582771)
XLA Ops:
  0.6 0.0 copy-start.2
  0.7 0.0 copy-start.6
  0.7 0.5 slice.17.fr
  1.2 1.3 fusion.8.gn
  2.5 0.8 copy.30
  3.2 0.6 pad.9.ro
  3.9 0.8 copy.31
  4.6 0.3 fusion
  4.9 0.0 copy-done.6
  4.9 90.6 %shard_map.229 = (bf16[128,1024]{1,0:T(8,128)(2,1)}, bf16[1024,256]{1,0:T(8,128)(2,1)}, bf16[128,1024]{1,0:T(8,128)(2,1)}, f32[8,1024]{1,0:T(8,128)}, bf16[16,64...) custom-call(bf16[128,1024]{1,0:T(8,128)(2,1)} %bitcast.27, ...), custom_call_target="tpu_custom_call" | custom-call | tf_op jit(solution)/shard_map/pallas_call | solution.py:836
  95.6 0.0 copy-start.3
  95.6 1.4 fusion.13
  97.0 0.0 copy-start.5
  97.0 0.0 copy-done.2
  97.0 2.2 multiply_reduce_fusion
  99.2 0.0 copy-start
  99.3 0.1 multiply_convert_fusion.x.ri
  99.4 0.0 copy-done.3
  99.4 0.0 copy-start.1
  99.4 0.3 fusion.14
  99.7 0.0 copy-done.5
  99.7 0.2 fusion.2
  99.9 0.1 fusion.1.gt
  100.0 0.0 copy-start.4
  100.0 0.7 copy.33.g
  100.7 0.0 copy-done.1
  100.7 97.8 %shard_map.230 = (bf16[16,128,1024]{2,1,0:T(8,128)(2,1)}, f32[128,1024]{1,0:T(8,128)}, f32[16,8,128]{2,1,0:T(8,128)}, bf16[8,128,2048]{2,1,0:T(8,128)(2,1)}, f32...) custom-call(bf16[128,1024]{1,0:T(8,128)(2,1)} %copy-done.1, f32[32,128]{1,0:T(8,128)} %copy.33.g, ...), custom_call_target="tpu_custom_call" | custom-call | tf_op jit(solution)/shard_map/pallas_call | solution.py:598
  198.6 0.0 copy-done
  198.6 0.0 copy-done.4
  198.6 97.5 %shard_map.231 = (f32[128,1024]{1,0:T(8,128)}, bf16[128,2048]{1,0:T(8,128)(2,1)}, f32[128,1024]{1,0:T(8,128)}, bf16[8,64,1024]{2,1,0:T(8,128)(2,1)}, bf16[8,64,384]{2,1,0:T(8,128)(2,1)}, /*index=5*/f32[128,2048]{1,0:T(8,128)}) custom-call(f32[128,1024]{1,0:T(8,128)} %get-tuple-element.54.gr, f32[16,8,128]{2,1,0:T(8,128)} %get-tuple-element.55.gb, ...), custom_call_target="tpu_custom_call" | custom-call | tf_op jit(solution)/shard_map/pallas_call | solution.py:980
  296.1 7.2 %shard_map.232 = (bf16[128,1024]{1,0:T(8,128)(2,1)}, f32[128,1024]{1,0:T(8,128)}, f32[64,1024]{1,0:T(8,128)}, f32[64,512]{1,0:T(8,128)}, f32[64,512]{1,0:T(8,128...) custom-call(bf16[128,2048]{1,0:T(8,128)(2,1)} %get-tuple-element.60., ...), custom_call_target="tpu_custom_call" | custom-call | tf_op jit(solution)/shard_map/pallas_call | solution.py:1075
  (3 shorter events, 0.0 us)
Async XLA Ops:
  0.6 96.4 %copy-start.2 = (bf16[1,128,1024]{2,1,0:T(8,128)(2,1)S(1)}, bf16[1,128,1024]{2,1,0:T(8,128)(2,1)}, u32[]{:S(2)}) copy-start(bf16[1,128,1024]{2,1,0:T(8,128)(2,1)} %param.14) | copy-start | bytes 786436
  0.7 4.2 %copy-start.6 = (f32[1,256]{1,0:T(1,128)}, f32[1,256]{1,0:T(1,128)S(1)}, u32[]{:S(2)}) copy-start(f32[1,256]{1,0:T(1,128)S(1)} %compare_select_fusion.fr) | copy-start | bytes 3076
  95.6 3.8 %copy-start.3 = (bf16[16,64,128]{2,1,0:T(8,128)(2,1)S(1)}, bf16[16,64,128]{2,1,0:T(8,128)(2,1)}, u32[]{:S(2)}) copy-start(bf16[16,64,128]{2,1,0:T(8,128)(2,1)} %get-tuple-element.49) | copy-start | bytes 786436
  97.0 2.7 copy-start.5
  99.2 99.3 %copy-start = (f32[128,1024]{1,0:T(8,128)}, f32[128,1024]{1,0:T(8,128)S(1)}, u32[]{:S(2)}) copy-start(f32[128,1024]{1,0:T(8,128)S(1)} %get-tuple-element.83.xm.refs_5_) | copy-start | bytes 1572868
  99.4 1.3 copy-start.1
  100.0 98.6 %copy-start.4 = (f32[128,128]{1,0:T(8,128)}, f32[128,128]{1,0:T(8,128)S(1)}, u32[]{:S(2)}) copy-start(f32[128,128]{1,0:T(8,128)S(1)} %fusion.1.gt) | copy-start | bytes 196612

commit v6 on v5

--- a/solution.py
+++ b/solution.py
@@ -518,6 +518,7 @@
             def _():
                 gate_part(2 * chip + core).start()
 
+            out_part[pl.ds(2 * chip, 2)] = dot(hg[at], wd[...]).astype(bf16).reshape(2, rows, width)
             return carry
 
         lax.fori_loop(0, 8, step, 0)
@@ -557,13 +558,6 @@
             return carry
 
         lax.fori_loop(0, width // 256, weight_rows, 0)
-
-        def outputs(i, carry):
-            at = pl.ds(pl.multiple_of(i * 512, 512), 512)
-            out_part[pl.ds(512 // rows * i, 512 // rows)] = dot(hg[at], wd[...]).astype(bf16).reshape(512 // rows, rows, width)
-            return carry
-
-        lax.fori_loop(0, 16 * rows // 512, outputs, 0)
 
         def collect(k, carry):
             to_chip(k).wait_recv()
@@ -740,6 +734,7 @@
         for item in (wo_all, ro_all, cots):
             item.start()
         firsts.cross()
+        downs.start()
         gain_all.pass_on()
         gain_all.wait()
         for i in range(8):
@@ -787,7 +782,7 @@
             j = here.ctx(k)
             arrive(j).wait_send()
             remote(stage.at[j], block_rows(seq, j), send.at[j], recv.at[j], {"ctx": j}).wait_recv()
-        downs.start()
+        downs.cross()
         keep = pltpu.make_async_copy(seq, kept, ksem.at[0])
         keep.start()
         for i, part in enumerate(split_heads(seq[:, 128:])):
@@ -822,7 +817,6 @@
             return carry
 
         lax.fori_loop(0, count // QROWS, step, 0)
-        downs.cross()
         for item in (wo_all, ro_all, cots):
             item.pass_on()
         for k in range(1, N_CTX):

time: 304 us -> 302 us (level)
    pallas_call x1, Pallas kernels: 97.5 us -> 88.9 us  [attend_back(): pl.pallas_call(kernel, out_shape=[shape((rows, width), f32), shape((rows,...]
    pallas_call x1, Pallas kernels: 97.8 us -> 103 us  [experts(): pl.pallas_call(kernel, out_shape=[shape((16, rows, width), bf16), shape((...]
where the time goes in v6:
time: 302 us; the launch traced here: 300 us
  Pallas kernels  290 us (96%)
  local copies, waits for them, and re-layouts  4.85 us (2%)
    pallas_call x1, Pallas kernels, experts(): pl.pallas_call(kernel, out_shape=[shape((16, rows, width), bf16), shape((...  103 us
    pallas_call x1, Pallas kernels, front(): pl.pallas_call(kernel, out_shape=[shape((rows, N_CTX * 128), bf16), shape...  90.9 us
    pallas_call x1, Pallas kernels, attend_back(): pl.pallas_call(kernel, out_shape=[shape((rows, width), f32), shape((rows,...  88.9 us
    pallas_call x1, Pallas kernels, finish_tokens(): pl.pallas_call(kernel, out_shape=[shape((rows, width), bf16), shape((rows...  7.22 us

profile of v6, /device:TPU:2, one launch (start us, length us, event | category | flops | bytes accessed | tf_op | source)
XLA Modules:
  0.0 300.1 jit_solution(6502171059353917883)
XLA Ops:
  0.6 0.0 copy-start.2
  0.7 0.0 copy-start.6
  0.7 0.5 slice.17.fr
  1.2 1.3 fusion.8.gn
  2.5 0.8 copy.30
  3.2 0.6 pad.9.ro
  3.9 0.8 copy.31
  4.6 0.3 fusion
  4.9 0.0 copy-done.6
  4.9 90.9 %shard_map.229 = (bf16[128,1024]{1,0:T(8,128)(2,1)}, bf16[1024,256]{1,0:T(8,128)(2,1)}, bf16[128,1024]{1,0:T(8,128)(2,1)}, f32[8,1024]{1,0:T(8,128)}, bf16[16,64...) custom-call(bf16[128,1024]{1,0:T(8,128)(2,1)} %bitcast.27, ...), custom_call_target="tpu_custom_call" | custom-call | tf_op jit(solution)/shard_map/pallas_call | solution.py:830
  95.8 0.0 copy-start.3
  95.8 1.4 fusion.13
  97.3 0.0 copy-start.5
  97.3 0.0 copy-done.2
  97.3 2.2 multiply_reduce_fusion
  99.5 0.0 copy-start
  99.5 0.1 multiply_convert_fusion.x.ri
  99.6 0.0 copy-done.3
  99.7 0.0 copy-start.1
  99.7 0.3 fusion.14
  100.0 0.0 copy-done.5
  100.0 0.2 fusion.2
  100.2 0.1 fusion.1.gt
  100.3 0.0 copy-start.4
  100.3 0.7 copy.33.g
  101.0 0.0 copy-done.1
  101.0 102.8 %shard_map.230 = (bf16[16,128,1024]{2,1,0:T(8,128)(2,1)}, f32[128,1024]{1,0:T(8,128)}, f32[16,8,128]{2,1,0:T(8,128)}, bf16[8,128,2048]{2,1,0:T(8,128)(2,1)}, f32...) custom-call(bf16[128,1024]{1,0:T(8,128)(2,1)} %copy-done.1, f32[32,128]{1,0:T(8,128)} %copy.33.g, ...), custom_call_target="tpu_custom_call" | custom-call | tf_op jit(solution)/shard_map/pallas_call | solution.py:592
  203.8 0.0 copy-done
  203.8 0.0 copy-done.4
  203.8 88.9 %shard_map.231 = (f32[128,1024]{1,0:T(8,128)}, bf16[128,2048]{1,0:T(8,128)(2,1)}, f32[128,1024]{1,0:T(8,128)}, bf16[8,64,1024]{2,1,0:T(8,128)(2,1)}, bf16[8,64,384]{2,1,0:T(8,128)(2,1)}, /*index=5*/f32[128,2048]{1,0:T(8,128)}) custom-call(f32[128,1024]{1,0:T(8,128)} %get-tuple-element.54.gr, f32[16,8,128]{2,1,0:T(8,128)} %get-tuple-element.55.gb, ...), custom_call_target="tpu_custom_call" | custom-call | tf_op jit(solution)/shard_map/pallas_call | solution.py:974
  292.7 7.2 %shard_map.232 = (bf16[128,1024]{1,0:T(8,128)(2,1)}, f32[128,1024]{1,0:T(8,128)}, f32[64,1024]{1,0:T(8,128)}, f32[64,512]{1,0:T(8,128)}, f32[64,512]{1,0:T(8,128...) custom-call(bf16[128,2048]{1,0:T(8,128)(2,1)} %get-tuple-element.60., ...), custom_call_target="tpu_custom_call" | custom-call | tf_op jit(solution)/shard_map/pallas_call | solution.py:1069
  (3 shorter events, 0.0 us)
Async XLA Ops:
  0.6 96.6 %copy-start.2 = (bf16[1,128,1024]{2,1,0:T(8,128)(2,1)S(1)}, bf16[1,128,1024]{2,1,0:T(8,128)(2,1)}, u32[]{:S(2)}) copy-start(bf16[1,128,1024]{2,1,0:T(8,128)(2,1)} %param.14) | copy-start | bytes 786436
  0.7 4.2 %copy-start.6 = (f32[1,256]{1,0:T(1,128)}, f32[1,256]{1,0:T(1,128)S(1)}, u32[]{:S(2)}) copy-start(f32[1,256]{1,0:T(1,128)S(1)} %compare_select_fusion.fr) | copy-start | bytes 3076
  95.8 3.8 %copy-start.3 = (bf16[16,64,128]{2,1,0:T(8,128)(2,1)S(1)}, bf16[16,64,128]{2,1,0:T(8,128)(2,1)}, u32[]{:S(2)}) copy-start(bf16[16,64,128]{2,1,0:T(8,128)(2,1)} %get-tuple-element.49) | copy-start | bytes 786436
  97.3 2.7 copy-start.5
  99.5 104.3 %copy-start = (f32[128,1024]{1,0:T(8,128)}, f32[128,1024]{1,0:T(8,128)S(1)}, u32[]{:S(2)}) copy-start(f32[128,1024]{1,0:T(8,128)S(1)} %get-tuple-element.83.xm.refs_5_) | copy-start | bytes 1572868
  99.7 1.3 copy-start.1
  100.3 103.5 %copy-start.4 = (f32[128,128]{1,0:T(8,128)}, f32[128,128]{1,0:T(8,128)S(1)}, u32[]{:S(2)}) copy-start(f32[128,128]{1,0:T(8,128)S(1)} %fusion.1.gt) | copy-start | bytes 196612
